TPU v7x, 32 devices: a whole 2x2x4 slice. The times are simulated.
32 devices in a mesh: dp: 2 (over y), space: 16 (over z, x, core).
Axes of the slice: x: 2, y: 2, z: 4, core: 2. Of those that a mesh axis runs over, the one named last changes fastest.
Arguments:
- fields: bfloat16 [2, 128, 128, 512], P('dp', 'space'), may hold values from -6 to 6
- bn_scale: float32 [512], replicated, may hold values from 0.5 to 1.5
- bn_shift: float32 [512], replicated, may hold values from -3 to 3
- w_expand: bfloat16 [512, 2048], P(None, 'dp'), may hold values from -0.25 to 0.25
- expand_bias: float32 [2048], replicated, may hold values from -3 to 3
- dw_kernel: float32 [3, 3, 2048], replicated, may hold values from -2 to 2
- dw_bias: float32 [2048], replicated, may hold values from -3 to 3
- w_project: bfloat16 [2048, 512], P(None, 'dp'), may hold values from -0.125 to 0.125
- ln_gain: float32 [512], replicated, may hold values from 0.5 to 1.5
- ln_bias: float32 [512], replicated, may hold values from -3 to 3
- w_qkv: bfloat16 [512, 1536], P(None, 'dp'), may hold values from -0.25 to 0.25
- w_out: bfloat16 [512, 512], P(None, 'dp'), may hold values from -0.25 to 0.25
Outputs:
- output: bfloat16 [2, 128, 128, 512], P('dp', 'space')
All inputs are finite; a program needn't handle non-finite values.
Results may differ from a plain program's by a relative error of at most 0.0056.
Values may be sent and summed in bfloat16 or wider, within the bound.
No kernel may reach another device: no remote copies, remote signals or barrier semaphores. Data moves between devices by JAX's collectives and lax.ppermute only.
A program may use at most 64 MiB of HBM per device.

v0:
```python
import jax
import jax.numpy as jnp
from jax import lax
from jax.sharding import PartitionSpec as P

HD = 32
GRID = 8
HEIGHT = 128


def padded_2(cells, sides, width):
    for axis, dim in sides:
        count = lax.axis_size(axis)
        ends = count - 1
        head = lax.slice_in_dim(cells, 0, width, axis=dim)
        tail = lax.slice_in_dim(cells, cells.shape[dim] - width, cells.shape[dim], axis=dim)
        cells = jnp.concatenate(
            [
                lax.ppermute(tail, axis, [(i, (i + 1) % count) for i in range(ends)]),
                cells,
                lax.ppermute(head, axis, [((i + 1) % count, i) for i in range(ends)]),
            ],
            axis=dim,
        )
    return cells


def layer_normed(tokens, ln_gain, ln_bias):
    values = tokens.astype(jnp.float32)
    center = jnp.mean(values, axis=-1, keepdims=True)
    spread = jnp.mean(jnp.square(values - center), axis=-1, keepdims=True)
    return ((values - center) * lax.rsqrt(spread + 1e-05) * ln_gain + ln_bias).astype(jnp.bfloat16)


def expand_tokens(tokens, w_expand, expand_bias):
    flat = tokens.reshape(-1, tokens.shape[-1])
    summed = jnp.dot(
        flat, lax.all_gather(w_expand, "dp", axis=1, tiled=True), preferred_element_type=jnp.float32
    )
    expanded = jax.nn.gelu(summed + expand_bias).astype(jnp.bfloat16)
    return expanded.reshape(tokens.shape[:-1] + (summed.shape[1],))


def depthwise(padded, dw_kernel, dw_bias):
    band_rows = padded.shape[1] - 2
    image_cols = padded.shape[2]
    wide = jnp.pad(padded, ((0, 0), (0, 0), (1, 1), (0, 0)))
    accum = jnp.zeros((padded.shape[0], band_rows, image_cols, padded.shape[3]), jnp.float32)
    for row_off in range(3):
        for col_off in range(3):
            accum = (
                accum
                + wide[:, row_off : row_off + band_rows, col_off : col_off + image_cols].astype(
                    jnp.float32
                )
                * dw_kernel[row_off, col_off]
            )
    return jax.nn.gelu(accum + dw_bias).astype(jnp.bfloat16)


def project_back(spatial, w_project):
    flat = spatial.reshape(-1, spatial.shape[-1])
    return jnp.dot(
        flat,
        lax.all_gather(w_project, "dp", axis=1, tiled=True),
        preferred_element_type=jnp.float32,
    )


def qkv_of(tokens, w_qkv):
    flat = tokens.reshape(-1, tokens.shape[-1])
    summed = jnp.dot(
        flat, lax.all_gather(w_qkv, "dp", axis=1, tiled=True), preferred_element_type=jnp.float32
    )
    return summed.astype(jnp.bfloat16).reshape(tokens.shape[:-1] + (summed.shape[1],))


def out_of(attended, w_out):
    flat = attended.reshape(-1, attended.shape[-1])
    summed = jnp.dot(
        flat, lax.all_gather(w_out, "dp", axis=1, tiled=True), preferred_element_type=jnp.float32
    )
    return summed.reshape(attended.shape[:-1] + (summed.shape[1],))


def to_windows(gridded):
    items, height, grid_count, blocks_here, width = gridded.shape
    stride_rows = height // grid_count
    split = gridded.reshape(items, grid_count, stride_rows, grid_count, blocks_here, width)
    split = split.transpose(0, 2, 4, 1, 3, 5)
    return split.reshape(items * stride_rows * blocks_here, grid_count * grid_count, width)


def from_windows(windows, items, blocks_here):
    width = windows.shape[-1]
    stride_rows = HEIGHT // GRID
    split = windows.reshape(items, stride_rows, blocks_here, GRID, GRID, width)
    split = split.transpose(0, 3, 1, 4, 2, 5)
    return split.reshape(items, HEIGHT, GRID, blocks_here, width)


def attend_windows(queries, keyset, valueset):
    window_count, length, width = queries.shape
    heads = width // HD
    query_heads = queries.reshape(window_count, length, heads, HD)
    key_heads = keyset.reshape(window_count, length, heads, HD)
    value_heads = valueset.reshape(window_count, length, heads, HD)
    scores = jnp.einsum(
        "wqhd,wkhd->whqk", query_heads, key_heads, preferred_element_type=jnp.float32
    ) / jnp.sqrt(jnp.float32(HD))
    exponent = jnp.exp(scores)
    soft_weights = (exponent / jnp.sum(exponent, axis=-1, keepdims=True)).astype(jnp.bfloat16)
    mixed = jnp.einsum(
        "whqk,wkhd->wqhd", soft_weights, value_heads, preferred_element_type=jnp.float32
    )
    return mixed.astype(jnp.bfloat16).reshape(window_count, length, width)


def local(
    fields,
    bn_scale,
    bn_shift,
    w_expand,
    expand_bias,
    dw_kernel,
    dw_bias,
    w_project,
    ln_gain,
    ln_bias,
    w_qkv,
    w_out,
):
    batch_local, band_rows, image_cols, chans = fields.shape
    col_blocks = image_cols // GRID
    normed = (fields.astype(jnp.float32) * bn_scale + bn_shift).astype(jnp.bfloat16)
    expanded = expand_tokens(normed, w_expand, expand_bias)
    expanded = padded_2(expanded, (("space", 1),), 1)
    spatial = depthwise(expanded, dw_kernel, dw_bias)
    projected = project_back(spatial, w_project).reshape(fields.shape)
    conv_out = (fields.astype(jnp.float32) + projected).astype(jnp.bfloat16)
    banded_in = conv_out.reshape(batch_local, band_rows, GRID, col_blocks, chans)
    gridded = lax.all_to_all(banded_in, "space", split_axis=3, concat_axis=1, tiled=True)
    triple = qkv_of(layer_normed(gridded, ln_gain, ln_bias), w_qkv)
    blocks_here = gridded.shape[3]
    attended = attend_windows(
        to_windows(triple[..., :chans]),
        to_windows(triple[..., chans : 2 * chans]),
        to_windows(triple[..., 2 * chans :]),
    )
    attended = from_windows(attended, batch_local, blocks_here)
    finished = (gridded.astype(jnp.float32) + out_of(attended, w_out)).astype(jnp.bfloat16)
    banded = lax.all_to_all(finished, "space", split_axis=1, concat_axis=3, tiled=True)
    return banded.reshape(fields.shape)


def solution(mesh):
    in_specs = (
        P("dp", "space", None, None),
        P(),
        P(),
        P(None, "dp"),
        P(),
        P(),
        P(),
        P(None, "dp"),
        P(),
        P(),
        P(None, "dp"),
        P(None, "dp"),
    )
    out_specs = P("dp", "space", None, None)
    return jax.shard_map(local, mesh=mesh, in_specs=in_specs, out_specs=out_specs, check_vma=False)
```

profile of v0, /device:TPU:0, one launch (start us, length us, event | category | flops | bytes accessed | tf_op | source)
XLA Modules:
  0.0 220.6 jit_solution(14280994443042432014)
XLA Ops:
  6.5 0.7 all-gather.4.cloned.1.call-update
  7.3 0.7 all-gather.6.cloned.1.call-update
  8.0 1.5 fusion.34
  9.5 35.3 %all-gather.4.cloned.1.call-done = bf16[512,2048]{1,0:T(8,128)(2,1)} async-done(((bf16[512,1024]{1,0:T(8,128)(2,1)}), bf16[512,2048]{1,0:T(8,128)(2,1)}) %all-gather.4.cloned.1.call-update) | async-done | bytes 2097168 | tf_op jit(solution)/shard_map/all_gather | solution.py:38
  44.8 6.0 %fusion.8 = bf16[1024,2048]{1,0:T(8,128)(2,1)S(1)} fusion(f32[2048]{0:T(1024)} %param.16, bf16[1024,512]{1,0:T(8,128)(2,1)S(1)} %bitcast.110, bf16[512,2048]{1,0:T(8,128)(2,1)} %all-gather.4.cloned.1.call-done), kind=kOutput, calls=%fused_computation.12 | convolution fusion | flops 2168455168 | bytes 7348224 | tf_op jit(solution)/shard_map/dot_general | solution.py:37
  50.9 1.6 collective-permute-start.1
  52.4 3.1 %collective-permute-start = (bf16[1,1,128,2048]{3,2,1,0:T(8,128)(2,1)S(1)}, bf16[1,1,128,2048]{3,2,1,0:T(8,128)(2,1)S(1)}, u32[]{:S(2)}, u32[]{:S(2)}) collective-permute-start(bf16[1,1,128,2048]{3,2,1,0:T(8,128)(2,1)S(1)} %get-tuple-element.5), channel_id=1, source_target_pairs={{0,1},{1,2},{2,3},{3,4},{4,5},{5,6},{6,7},{7,8},{8,9},{9,10},{10,1... | collective-permute-start | bytes 1572872 | tf_op jit(solution)/shard_map/ppermute | solution.py:19
  55.6 1.4 collective-permute-done
  57.0 5.9 %fusion.22 = bf16[1,10,130,2048]{3,2,1,0:T(8,128)(2,1)} fusion(bf16[1,1,128,2048]{3,2,1,0:T(8,128)(2,1)S(1)} %collective-permute-done.1, bf16[1,8,128,2048]{3,2,1,0:T(8,128)(2,1)S(1)} %bitcast.101, bf16[1,1,128,2048]{3,2,1,0:T(8,128)(2,1)S(1)} %collective-permute-done), kind=kLoop, calls=%fused_computation.28 | loop fusion | flops 31948800 | bytes 10567680 | tf_op jit(solution)/shard_map/concatenate | solution.py:17
  62.9 16.5 %all-gather.6.cloned.1.call-done = bf16[2048,512]{1,0:T(8,128)(2,1)} async-done(((bf16[2048,256]{1,0:T(8,128)(2,1)}), bf16[2048,512]{1,0:T(8,128)(2,1)}) %all-gather.6.cloned.1.call-update) | async-done | bytes 2097168 | tf_op jit(solution)/shard_map/all_gather | solution.py:65
  79.4 21.8 %fusion.35 = bf16[1,8,128,512]{3,2,1,0:T(8,128)(2,1)S(1)} fusion(bf16[1,8,128,512]{3,2,1,0:T(8,128)(2,1)S(1)} %copy-done.2, bf16[2048,512]{1,0:T(8,128)(2,1)} %all-gather.6.cloned.1.call-done, f32[2048]{0:T(1024)S(1)} %copy-done.7, f32[2048]{0:T(1024)S(1)} %bitcast.118, bf16[1,10,130,2048]{3,2,1,0:T(8,128)(2,1)} %fusion.22, f32[2048]{0:T(1024)S(1)} %bitcast.119, ...), kind=kOutput, calls=%fused_computation.45 | convolution fusion | flops 2228748288 | bytes 34684928 | tf_op jit(solution)/shard_map/dot_general | solution.py:63
  101.3 1.6 copy.41
  102.8 5.7 %all-to-all-start = ((bf16[1,8,8,16,512]{4,2,1,0,3:T(8,128)(2,1)}), bf16[1,8,8,16,512]{4,2,1,0,3:T(8,128)(2,1)S(1)}, u32[]{:S(2)}, u32[]{:S(2)}) async-start(bf16[1,8,8,16,512]{4,2,1,0,3:T(8,128)(2,1)} %copy.41), calls=%async_computation | async-start | bytes 2097152 | tf_op jit(solution)/shard_map/all_to_all | solution.py:142
  108.6 0.7 all-gather.8.cloned.1.call-update
  109.3 9.6 %all_gather.15 = bf16[512,512]{1,0:T(8,128)(2,1)} all-gather(bf16[512,256]{1,0:T(8,128)(2,1)S(1)} %copy-done.3), channel_id=1, replica_groups=mesh['dp'=2,'space'=16] {'dp'}, dimensions={1}, use_global_device_ids=true | all-gather | bytes 786432 | tf_op jit(solution)/shard_map/all_gather | solution.py:81
  118.9 12.6 %all-to-all-done = bf16[1,8,8,16,512]{4,2,1,0,3:T(8,128)(2,1)S(1)} async-done(((bf16[1,8,8,16,512]{4,2,1,0,3:T(8,128)(2,1)}), bf16[1,8,8,16,512]{4,2,1,0,3:T(8,128)(2,1)S(1)}, u32[]{:S(2)}, u32[]{:S(2)}) %all-to-all-start) | async-done | bytes 1048608 | tf_op jit(solution)/shard_map/all_to_all | solution.py:142
  133.2 5.4 %all-gather.8.cloned.1.call-done = bf16[512,1536]{1,0:T(8,128)(2,1)} async-done(((bf16[512,768]{1,0:T(8,128)(2,1)}), bf16[512,1536]{1,0:T(8,128)(2,1)}) %all-gather.8.cloned.1.call-update) | async-done | bytes 1572880 | tf_op jit(solution)/shard_map/all_gather | solution.py:73
  138.6 3.2 %fusion.32 = bf16[1,128,8,1,1536]{4,2,1,3,0:T(8,128)(2,1)S(1)} fusion(bf16[1024,512]{1,0:T(8,128)(2,1)S(1)} %fusion.39, bf16[512,1536]{1,0:T(8,128)(2,1)} %all-gather.8.cloned.1.call-done), kind=kOutput, calls=%fused_computation.40 | convolution fusion | flops 1612185600 | bytes 5767168 | tf_op jit(solution)/shard_map/dot_general | solution.py:72
  141.8 1.5 fusion.60
  143.4 3.8 %reshape_reshape.15 = bf16[16,64,16,32]{3,2,1,0:T(8,128)(2,1)} reshape(bf16[1,16,1,8,8,512]{5,4,3,1,2,0:T(8,128)(2,1)S(1)} %copy.46) | data formatting | bytes 2097152 | tf_op jit(solution)/shard_map/reshape;reshape | solution.py:106
  147.2 1.3 copy.45
  148.6 3.8 %reshape_reshape.14 = bf16[16,64,16,32]{3,2,1,0:T(8,128)(2,1)} reshape(bf16[1,16,1,8,8,512]{5,4,3,1,2,0:T(8,128)(2,1)S(1)} %copy.45) | data formatting | bytes 2097152 | tf_op jit(solution)/shard_map/reshape;reshape | solution.py:105
  152.4 1.3 copy.44
  153.7 3.8 %reshape_reshape.13 = bf16[16,64,16,32]{3,2,1,0:T(8,128)(2,1)} reshape(bf16[1,16,1,8,8,512]{5,4,3,1,2,0:T(8,128)(2,1)S(1)} %copy.44) | data formatting | bytes 2097152 | tf_op jit(solution)/shard_map/reshape;reshape | solution.py:107
  157.6 6.5 %fusion.17 = (f32[16,16,64]{2,1,0:T(8,128)S(1)}, f32[16,16,64,64]{2,3,1,0:T(8,128)S(1)}) fusion(bf16[16,64,16,32]{3,2,1,0:T(8,128)(2,1)} %reshape_reshape.15, bf16[16,64,16,32]{3,2,1,0:T(8,128)(2,1)} %reshape_reshape.14), kind=kOutput, calls=%fused_computation.23 | convolution fusion | flops 69189632 | bytes 6356992 | tf_op jit(solution)/shard_map/wqhd,wkhd->whqk/dot_general | solution.py:108
  164.1 3.1 %convert_bitcast_fusion = bf16[16,64,16,32]{1,3,2,0:T(8,128)(2,1)} fusion(f32[16,16,64,64]{2,3,1,0:T(8,128)S(1)} %get-tuple-element.22, f32[16,16,64]{2,1,0:T(8,128)S(1)} %get-tuple-element.21, bf16[16,64,16,32]{3,2,1,0:T(8,128)(2,1)S(1)} %copy-done.1), kind=kOutput, calls=%fused_computation.54 | convolution fusion | flops 70778880 | bytes 6356992 | tf_op jit(solution)/shard_map/whqk,wkhd->wqhd/dot_general | solution.py:113
  167.2 5.7 %copy.51 = bf16[16,64,16,32]{3,2,1,0:T(8,128)(2,1)} copy(bf16[16,64,16,32]{1,3,2,0:T(8,128)(2,1)} %convert_bitcast_fusion) | data formatting | bytes 2097152 | tf_op jit(solution)/shard_map/convert_element_type | solution.py:116
  172.9 5.9 %reshape_reshape.16 = bf16[1,16,1,8,8,512]{5,4,3,1,2,0:T(8,128)(2,1)S(1)} reshape(bf16[16,64,16,32]{3,2,1,0:T(8,128)(2,1)} %copy.51) | data formatting | bytes 2097152 | tf_op jit(solution)/shard_map/reshape;reshape | solution.py:97
  178.9 2.8 %fusion.48 = bf16[1,128,8,1,512]{4,1,2,3,0:T(8,128)(2,1)S(1)} fusion(f32[1,16,8,8,1,512]{5,3,2,1,4,0:T(8,128)S(1)} %get-tuple-element.11, bf16[128,8,512]{2,1,0:T(8,128)(2,1)S(1)} %bitcast.108, bf16[512,512]{1,0:T(8,128)(2,1)} %all_gather.15), kind=kOutput, calls=%fused_computation.56 | convolution fusion | flops 537919488 | bytes 4718592 | tf_op jit(solution)/shard_map/dot_general | solution.py:80
  181.7 0.6 copy.54
  182.3 30.3 %all_to_all.24 = bf16[1,128,8,1,512]{4,2,3,0,1:T(8,128)(2,1)S(1)} all-to-all(bf16[1,128,8,1,512]{4,2,3,0,1:T(8,128)(2,1)S(1)} %copy.54), channel_id=1, replica_groups=mesh['dp'=2,'space'=16] {'space'}, dimensions={1} | all-to-all | bytes 2097152 | tf_op jit(solution)/shard_map/all_to_all | solution.py:152
  212.5 1.5 copy.55
  (32 shorter events, 2.1 us)
Async XLA Ops:
  6.5 38.2 %all-gather.4.cloned.1.call-start = ((), (), s32[]{:S(2)}) async-start(), calls=%async_computation.2 | async-start | bytes 3145728 | tf_op jit(solution)/shard_map/all_gather | solution.py:38
  7.3 72.2 %all-gather.6.cloned.1.call-start = ((), (), s32[]{:S(2)}) async-start(), calls=%async_computation.3 | async-start | bytes 3145728 | tf_op jit(solution)/shard_map/all_gather | solution.py:65
  44.8 10.8 %copy-start.4 = (f32[3,3,2048]{2,1,0:T(4,128)S(1)}, f32[3,3,2048]{2,1,0:T(4,128)}, u32[]{:S(2)}) copy-start(f32[3,3,2048]{2,1,0:T(4,128)} %param.17) | copy-start | bytes 221188
  50.7 6.3 %copy-start = (bf16[1024,2048]{1,0:T(8,128)(2,1)}, bf16[1024,2048]{1,0:T(8,128)(2,1)S(1)}, u32[]{:S(2)}) copy-start(bf16[1024,2048]{1,0:T(8,128)(2,1)S(1)} %fusion.8) | copy-start | bytes 12582916
  50.9 28.6 %copy-start.2 = (bf16[1,8,128,512]{3,2,1,0:T(8,128)(2,1)S(1)}, bf16[1,8,128,512]{3,2,1,0:T(8,128)(2,1)}, u32[]{:S(2)}) copy-start(bf16[1,8,128,512]{3,2,1,0:T(8,128)(2,1)} %param.12) | copy-start | bytes 3145732
  50.9 28.5 %copy-start.7 = (f32[2048]{0:T(1024)S(1)}, f32[2048]{0:T(1024)}, u32[]{:S(2)}) copy-start(f32[2048]{0:T(1024)} %param.18) | copy-start | bytes 24580
  50.9 4.7 %collective-permute-start.1 = (bf16[1,1,128,2048]{3,2,1,0:T(8,128)(2,1)S(1)}, bf16[1,1,128,2048]{3,2,1,0:T(8,128)(2,1)S(1)}, u32[]{:S(2)}, u32[]{:S(2)}) collective-permute-start(bf16[1,1,128,2048]{3,2,1,0:T(8,128)(2,1)S(1)} %get-tuple-element.6), channel_id=1, source_target_pairs={{1,0},{2,1},{3,2},{4,3},{5,4},{6,5},{7,6},{8,7},{9,8},{10,9},{11,1... | collective-permute-start | bytes 1572872 | tf_op jit(solution)/shard_map/ppermute | solution.py:21
  52.4 4.6 %collective-permute-start = (bf16[1,1,128,2048]{3,2,1,0:T(8,128)(2,1)S(1)}, bf16[1,1,128,2048]{3,2,1,0:T(8,128)(2,1)S(1)}, u32[]{:S(2)}, u32[]{:S(2)}) collective-permute-start(bf16[1,1,128,2048]{3,2,1,0:T(8,128)(2,1)S(1)} %get-tuple-element.5), channel_id=1, source_target_pairs={{0,1},{1,2},{2,3},{3,4},{4,5},{5,6},{6,7},{7,8},{8,9},{9,10},{10,1... | collective-permute-start | bytes 1572872 | tf_op jit(solution)/shard_map/ppermute | solution.py:19
  79.4 29.9 %copy-start.3 = (bf16[512,256]{1,0:T(8,128)(2,1)S(1)}, bf16[512,256]{1,0:T(8,128)(2,1)}, u32[]{:S(2)}) copy-start(bf16[512,256]{1,0:T(8,128)(2,1)} %param.23) | copy-start | bytes 786436
  102.8 30.0 %copy-start.5 = (f32[512]{0:T(512)S(1)}, f32[512]{0:T(512)}, u32[]{:S(2)}) copy-start(f32[512]{0:T(512)} %param.21) | copy-start | bytes 6148
  102.8 30.0 %copy-start.6 = (f32[512]{0:T(512)S(1)}, f32[512]{0:T(512)}, u32[]{:S(2)}) copy-start(f32[512]{0:T(512)} %param.20) | copy-start | bytes 6148
  102.8 28.7 %all-to-all-start = ((bf16[1,8,8,16,512]{4,2,1,0,3:T(8,128)(2,1)}), bf16[1,8,8,16,512]{4,2,1,0,3:T(8,128)(2,1)S(1)}, u32[]{:S(2)}, u32[]{:S(2)}) async-start(bf16[1,8,8,16,512]{4,2,1,0,3:T(8,128)(2,1)} %copy.41), calls=%async_computation | async-start | bytes 2097152 | tf_op jit(solution)/shard_map/all_to_all | solution.py:142
  108.6 30.0 %all-gather.8.cloned.1.call-start = ((), (), s32[]{:S(2)}) async-start(), calls=%async_computation.4 | async-start | bytes 2359296 | tf_op jit(solution)/shard_map/all_gather | solution.py:73
  157.6 6.5 %copy-start.1 = (bf16[16,64,16,32]{3,2,1,0:T(8,128)(2,1)S(1)}, bf16[16,64,16,32]{3,2,1,0:T(8,128)(2,1)}, u32[]{:S(2)}) copy-start(bf16[16,64,16,32]{3,2,1,0:T(8,128)(2,1)} %reshape_reshape.13) | copy-start | bytes 3145732
Sparse Core Ops, SparseCore 0:
  8.9 35.8 all-gather.3
  46.3 33.0 all-gather.5
  110.9 27.5 all-gather.7
where the time goes:
time: 222 us; the launch traced here: 221 us
  waiting for transfers between devices  73.2 us (33%)
  matrix products  43.4 us (20%)
  blocking collectives  39.9 us (18%)
  local copies, waits for them, and re-layouts  31.5 us (14%)
  between operations  13.4 us (6%)
  starting transfers between devices  10.4 us (5%)
  other arithmetic  8.81 us (4%)
    all_gather x1, waiting for transfers between devices, expand_tokens(): lax.all_gather(w_expand, 'dp', axis=1, tiled=True)  35.3 us
    all_to_all x1, blocking collectives, local(): lax.all_to_all(finished, 'space', split_axis=1, concat_axis=3, tiled=True)  30.3 us
    dot_general x1, matrix products, project_back(): jnp.dot(flat, lax.all_gather(w_project, 'dp', axis=1, tiled=True), prefer...  21.8 us
    all_gather x1, waiting for transfers between devices, project_back(): lax.all_gather(w_project, 'dp', axis=1, tiled=True)  16.5 us
    all_to_all x1, waiting for transfers between devices, local(): lax.all_to_all(banded_in, 'space', split_axis=3, concat_axis=1, tiled=True)  12.6 us
    all_gather x1, blocking collectives, out_of(): lax.all_gather(w_out, 'dp', axis=1, tiled=True)  9.61 us
    dot_general x1, matrix products, attend_windows(): jnp.einsum('wqhd,wkhd->whqk', query_heads, key_heads, preferred_element_t...  6.45 us
    dot_general x1, matrix products, expand_tokens(): jnp.dot(flat, lax.all_gather(w_expand, 'dp', axis=1, tiled=True), preferr...  5.98 us
  transfers between devices with their start and end apart: 6, of which 5 were waited for; matrix products, arithmetic and copies ran while one was open for 7% of the time, Pallas kernels for 0%

commit v1 on v0

v1 whole, which is shorter than its diff:
```python
import functools
import math

import jax
import jax.numpy as jnp
from jax import lax
from jax.experimental import pallas as pl
from jax.experimental.pallas import tpu as pltpu
from jax.sharding import PartitionSpec as P

HD = 32
GRID = 8
CHUNKS = 2
ROOT = math.sqrt(2.0 / math.pi)
LIN = 2.0 * ROOT
CUBE = 8.0 * ROOT * 0.044715
F32 = jnp.float32
BF16 = jnp.bfloat16
VMEM_LIMIT = 56 * 1024 * 1024


def half_gelu(half):
    return half + half * jnp.tanh(half * (LIN + CUBE * (half * half)))


def one_hot_order(cols, inverse=False):
    stride = cols // GRID
    row = lax.broadcasted_iota(jnp.int32, (cols, cols), 0)
    col = lax.broadcasted_iota(jnp.int32, (cols, cols), 1)
    if inverse:
        row, col = col, row
    return jnp.where(col == (row % GRID) * stride + row // GRID, 1.0, 0.0).astype(BF16)


def dot(a, b):
    return jnp.dot(a, b, preferred_element_type=F32)


def vmem():
    return pl.BlockSpec(memory_space=pltpu.VMEM)


def smem():
    return pl.BlockSpec(memory_space=pltpu.SMEM)


def params():
    return pltpu.CompilerParams(vmem_limit_bytes=VMEM_LIMIT)


def order_kernel(fields, scale, shift, ordered, normed):
    rows, cols, _ = fields.shape
    pick = one_hot_order(cols)
    for row in range(rows):
        placed = dot(pick, fields[row])
        ordered[row] = placed.astype(BF16)
        normed[row] = (placed * (0.5 * scale[...]) + 0.5 * shift[...]).astype(BF16)


def order_rows(fields, scale, shift):
    shape = jax.ShapeDtypeStruct(fields.shape, BF16)
    return pl.pallas_call(
        order_kernel,
        out_shape=(shape, shape),
        in_specs=[vmem()] * 3,
        out_specs=(vmem(), vmem()),
        compiler_params=params(),
        name="order_rows",
    )(fields, scale, shift)


def expand_kernel(pieces, aliased, info, normed, above, below, scale, shift, *refs):
    weights = refs[:pieces]
    bias, taps, tap_bias = refs[pieces : pieces + 3]
    out, edge, wide = refs[pieces + 3 + aliased :]
    rows, cols, _ = normed.shape
    width = bias.shape[-1]

    @pl.when(pl.program_id(0) == 0)
    def _():
        pick = one_hot_order(cols)
        for side, ref in enumerate((above, below)):
            placed = dot(pick, ref[0])
            edge[side] = (placed * (0.5 * scale[...]) + 0.5 * shift[...]).astype(BF16)

    half_bias = 0.5 * bias[...]
    half_taps = 0.5 * taps[...]
    half_tap_bias = 0.5 * tap_bias[...]
    lane = lax.broadcasted_iota(jnp.int32, (GRID, width), 0)
    for row in range(rows + 2):
        total = half_bias
        for piece, weight in enumerate(weights):
            depth = weight.shape[0]
            if pieces == 1:
                span = slice(None)
            else:
                span = pl.ds(pl.multiple_of(info[3 + piece] * depth, depth), depth)
            if row == 0:
                tokens = edge[0, :, span]
            elif row == rows + 1:
                tokens = edge[1, :, span]
            else:
                tokens = normed[row - 1, :, span]
            total = total + dot(tokens, weight[...])
        value = half_gelu(total)
        if row == 0:
            value = value * info[1].astype(F32)
        elif row == rows + 1:
            value = value * info[2].astype(F32)
        wide[row, GRID : GRID + cols, :] = value
        first = value[:GRID]
        last = value[cols - GRID :]
        wide[row, :GRID, :] = jnp.where(lane == 0, 0.0, pltpu.roll(last, 1, 0))
        wide[row, GRID + cols :, :] = jnp.where(
            lane == GRID - 1, 0.0, pltpu.roll(first, GRID - 1, 0)
        )
        if row >= 2:
            total = half_tap_bias
            for row_off in range(3):
                for col_off in range(3):
                    total = (
                        total
                        + wide[row - 2 + row_off, GRID * col_off : GRID * col_off + cols, :]
                        * half_taps[row_off, col_off][None]
                    )
            out[(row - 2) * cols : (row - 1) * cols, :] = half_gelu(total).astype(BF16)


def expand_some(normed, above, below, scale, shift, weights, info, bias, taps, tap_bias, spatial):
    rows, cols, chans = normed.shape
    inner = bias.shape[-1]
    here = weights[0].shape[1]
    width = min(256, here)
    aliased = spatial is not None
    whole = lambda shape: pl.BlockSpec(shape, lambda t, info: (0,) * len(shape))
    in_specs = [
        whole(normed.shape),
        whole(above.shape),
        whole(below.shape),
        whole(scale.shape),
        whole(shift.shape),
    ]
    in_specs += [pl.BlockSpec((w.shape[0], width), lambda t, info: (0, t)) for w in weights]
    in_specs += [
        pl.BlockSpec((1, width), lambda t, info: (0, info[0] + t)),
        pl.BlockSpec((3, 3, width), lambda t, info: (0, 0, info[0] + t)),
        pl.BlockSpec((1, width), lambda t, info: (0, info[0] + t)),
    ]
    operands = [info, normed, above, below, scale, shift, *weights, bias, taps, tap_bias]
    aliases = {}
    if aliased:
        in_specs.append(pl.BlockSpec(memory_space=pl.ANY))
        aliases = {len(operands): 0}
        operands.append(spatial)
    return pl.pallas_call(
        functools.partial(expand_kernel, len(weights), int(aliased)),
        grid_spec=pltpu.PrefetchScalarGridSpec(
            num_scalar_prefetch=1,
            grid=(here // width,),
            in_specs=in_specs,
            out_specs=pl.BlockSpec((rows * cols, width), lambda t, info: (0, info[0] + t)),
            scratch_shapes=[
                pltpu.VMEM((2, cols, chans), BF16),
                pltpu.VMEM((rows + 2, cols + 2 * GRID, width), F32),
            ],
        ),
        out_shape=jax.ShapeDtypeStruct((rows * cols, inner), BF16),
        input_output_aliases=aliases,
        compiler_params=params(),
        name="expand_conv",
    )(*operands)


def assemble(target, pieces, info):
    for n, piece in enumerate(pieces):
        depth, width = piece.shape
        if piece.shape == target.shape:
            target[...] = piece[...]
        else:
            target[
                pl.ds(pl.multiple_of(info[2 * n] * depth, depth), depth),
                pl.ds(pl.multiple_of(info[2 * n + 1] * width, width), width),
            ] = piece[...]


def project_kernel(pieces, info, spatial, ordered, *refs):
    weights = refs[:pieces]
    outs = refs[pieces : pieces + GRID]
    full, conv = refs[pieces + GRID :]

    @pl.when(pl.program_id(0) == 0)
    def _():
        assemble(full, weights, [info[1 + n] for n in range(2 * pieces)])

    conv[...] = (ordered[0].astype(F32) + dot(spatial[...], full[...])).astype(BF16)
    size = outs[0].shape[1]
    for k in range(GRID):
        start = pl.multiple_of((info[0] ^ k) * size, size)
        outs[k][0] = conv[pl.ds(start, size), :]


def project_rows(spatial, ordered, weights, info, first, count):
    rows, cols, chans = ordered.shape
    inner = spatial.shape[1]
    size = cols // GRID
    out = jax.ShapeDtypeStruct((count, size, chans), BF16)
    whole = lambda shape: pl.BlockSpec(shape, lambda t, info: (0,) * len(shape))
    return pl.pallas_call(
        functools.partial(project_kernel, len(weights)),
        grid_spec=pltpu.PrefetchScalarGridSpec(
            num_scalar_prefetch=1,
            grid=(count,),
            in_specs=[
                pl.BlockSpec((cols, inner), lambda t, info: (first + t, 0)),
                pl.BlockSpec((1, cols, chans), lambda t, info: (first + t, 0, 0)),
            ]
            + [whole(w.shape) for w in weights],
            out_specs=[pl.BlockSpec((1, size, chans), lambda t, info: (t, 0, 0))] * GRID,
            scratch_shapes=[pltpu.VMEM((inner, chans), BF16), pltpu.VMEM((cols, chans), BF16)],
        ),
        out_shape=[out] * GRID,
        compiler_params=params(),
        name="project_rows",
    )(info, spatial, ordered, *weights)


def attend_kernel(n_qkv, n_out, info, gain, bias, *refs):
    refs = list(refs)
    take = lambda n: [refs.pop(0) for _ in range(n)]
    qkv_pieces, out_pieces = take(n_qkv), take(n_out)
    tokens, outs = take(GRID), take(GRID)
    qkv_full, out_full, lned, triple, mixed, resid = refs
    count, size, chans = tokens[0].shape
    wins = size // GRID
    length = GRID * GRID
    group = min(256, chans)
    heads = group // HD
    keys = heads * length

    assemble(qkv_full, qkv_pieces, [info[n] for n in range(2 * n_qkv)])
    assemble(out_full, out_pieces, [info[2 * n_qkv + n] for n in range(2 * n_out)])

    for a in range(count):
        rows = [tokens[k][a].astype(F32) for k in range(GRID)]
        for w in range(wins):
            x = jnp.concatenate([r[w * GRID : (w + 1) * GRID] for r in rows], axis=0)
            start = (a * wins + w) * length
            resid[start : start + length, :] = x
            center = jnp.mean(x, axis=-1, keepdims=True)
            off = x - center
            spread = jnp.mean(off * off, axis=-1, keepdims=True)
            lned[start : start + length, :] = (
                off * lax.rsqrt(spread + 1e-05) * gain[...] + bias[...]
            ).astype(BF16)

    triple[...] = dot(lned[...], qkv_full[...]).astype(BF16)

    def same(shape, row_block, col_block):
        row = lax.broadcasted_iota(jnp.int32, shape, 0) // row_block
        col = lax.broadcasted_iota(jnp.int32, shape, 1) // col_block
        return jnp.where(row == col, 1.0, 0.0).astype(BF16)

    spread_mask = same((keys, group), length, HD)
    sum_mask = same((256, 256), length, length)
    factor = math.log2(math.e) / math.sqrt(HD)
    for win in range(count * wins):
        at = slice(win * length, (win + 1) * length)
        for g in range(chans // group):
            cols = slice(g * group, (g + 1) * group)
            query = triple[at, cols]
            key = triple[at, chans + g * group : chans + (g + 1) * group]
            value = triple[at, 2 * chans + g * group : 2 * chans + (g + 1) * group]
            key_wide = jnp.concatenate([key] * heads, axis=0) * spread_mask
            value_wide = jnp.concatenate([value] * heads, axis=0) * spread_mask
            scores = lax.dot_general(
                query, key_wide, (((1,), (1,)), ((), ())), preferred_element_type=F32
            )
            exponent = jnp.minimum(jnp.exp2(scores * factor), 3.3895e38)
            rounded = exponent.astype(BF16)
            sums = jnp.concatenate(
                [dot(rounded[:, n : n + 256], sum_mask) for n in range(0, keys, 256)], axis=1
            )
            soft = (exponent / sums).astype(BF16)
            mixed[at, cols] = dot(soft, value_wide).astype(BF16)

    resid[...] = resid[...] + dot(mixed[...], out_full[...])
    for a in range(count):
        for k in range(GRID):
            parts = []
            for w in range(wins):
                start = (a * wins + w) * length + k * GRID
                parts.append(resid[start : start + GRID, :])
            outs[k][a] = jnp.concatenate(parts, axis=0).astype(BF16)


def attend(tokens, gain, bias, w_qkv, w_out, info):
    count, size, chans = tokens[0].shape
    total = count * size * GRID
    out = jax.ShapeDtypeStruct(tokens[0].shape, BF16)
    return pl.pallas_call(
        functools.partial(attend_kernel, len(w_qkv), len(w_out)),
        out_shape=[out] * GRID,
        in_specs=[smem()] + [vmem()] * (2 + len(w_qkv) + len(w_out) + GRID),
        out_specs=[vmem()] * GRID,
        scratch_shapes=[
            pltpu.VMEM((chans, 3 * chans), BF16),
            pltpu.VMEM((chans, chans), BF16),
            pltpu.VMEM((total, chans), BF16),
            pltpu.VMEM((total, 3 * chans), BF16),
            pltpu.VMEM((total, chans), BF16),
            pltpu.VMEM((total, chans), F32),
        ],
        compiler_params=params(),
        name="attend",
    )(info, gain, bias, *w_qkv, *w_out, *tokens)


def restore_kernel(aliased, info, *refs):
    parts = refs[:GRID]
    out, row_buf = refs[GRID + aliased :]
    _, cols, _ = out.shape
    size = parts[0].shape[1]
    for k in range(GRID):
        row_buf[pl.ds(pl.multiple_of((info[0] ^ k) * size, size), size), :] = parts[k][0]
    out[0] = dot(one_hot_order(cols, inverse=True), row_buf[...]).astype(BF16)


def restore_rows(parts, info, rows, first, out):
    count, size, chans = parts[0].shape
    cols = size * GRID
    aliased = out is not None
    in_specs = [pl.BlockSpec((1, size, chans), lambda t, info: (t, 0, 0))] * GRID
    operands = [info, *parts]
    aliases = {}
    if aliased:
        in_specs.append(pl.BlockSpec(memory_space=pl.ANY))
        aliases = {len(operands): 0}
        operands.append(out)
    return pl.pallas_call(
        functools.partial(restore_kernel, int(aliased)),
        grid_spec=pltpu.PrefetchScalarGridSpec(
            num_scalar_prefetch=1,
            grid=(count,),
            in_specs=in_specs,
            out_specs=pl.BlockSpec((1, cols, chans), lambda t, info: (first + t, 0, 0)),
            scratch_shapes=[pltpu.VMEM((cols, chans), BF16)],
        ),
        out_shape=jax.ShapeDtypeStruct((rows, cols, chans), BF16),
        input_output_aliases=aliases,
        compiler_params=params(),
        name="restore_rows",
    )(*operands)


def scalars(*values):
    return jnp.stack([jnp.asarray(v, jnp.int32) for v in values])


def local(
    fields,
    bn_scale,
    bn_shift,
    w_expand,
    expand_bias,
    dw_kernel,
    dw_bias,
    w_project,
    ln_gain,
    ln_bias,
    w_qkv,
    w_out,
):
    _, rows, cols, chans = fields.shape
    inner = expand_bias.shape[0]
    dp, space = lax.axis_size("dp"), lax.axis_size("space")
    dp_at, space_at = lax.axis_index("dp"), lax.axis_index("space")
    groups = space // GRID
    grid_at = space_at // groups
    pairs = dp == 2 and space % 2 == 0
    core = space_at % 2
    as_row = lambda v: v.reshape(1, -1)
    scale, shift = as_row(bn_scale), as_row(bn_shift)
    image = fields.reshape(rows, cols, chans)

    down = [(i, i + 1) for i in range(space - 1)]
    up = [(i + 1, i) for i in range(space - 1)]
    above = lax.ppermute(image[rows - 1 :], "space", down)
    below = lax.ppermute(image[:1], "space", up)

    def fetch(weight):
        if not pairs:
            return [lax.all_gather(weight, "dp", axis=1, tiled=True)], [0, 0]
        part = weight.shape[0] // 2
        mine = lax.dynamic_slice_in_dim(weight, core * part, part, axis=0)
        got = lax.ppermute(mine, "dp", [(0, 1), (1, 0)])
        other = lax.ppermute(got, "space", [(i, i ^ 1) for i in range(space)])
        return [weight, got, other], [0, dp_at, core, 1 - dp_at, 1 - core, 1 - dp_at]

    expand_all, _ = fetch(w_expand)
    project_all, project_at = fetch(w_project)
    qkv_all, qkv_at = fetch(w_qkv)
    out_all, out_at = fetch(w_out)

    ordered, normed = order_rows(image, scale, shift)
    top = (space_at > 0).astype(jnp.int32)
    bottom = (space_at < space - 1).astype(jnp.int32)
    some = functools.partial(expand_some, normed, above, below, scale, shift)
    small = (as_row(expand_bias), dw_kernel, as_row(dw_bias))
    if pairs:
        tiles = w_expand.shape[1] // min(256, w_expand.shape[1])
        info = scalars(dp_at * tiles, top, bottom, 0, 0)
        spatial = some([w_expand], info, *small, None)
        info = scalars((1 - dp_at) * tiles, top, bottom, core, 1 - core)
        spatial = some(expand_all[1:], info, *small, spatial)
    else:
        spatial = some(expand_all, scalars(0, top, bottom, 0, 0), *small, None)

    count = rows // CHUNKS
    swaps = [
        [(s, (((s // groups) ^ k) * groups) + s % groups) for s in range(space)]
        for k in range(GRID)
    ]
    order = (4, 6, 5, 7, 2, 3, 1)

    def exchange(parts):
        parts = list(parts)
        for k in order:
            parts[k] = lax.ppermute(parts[k], "space", swaps[k])
        return parts

    sent = []
    for chunk in range(CHUNKS):
        info = scalars(grid_at, *project_at)
        sent.append(
            exchange(project_rows(spatial, ordered, project_all, info, chunk * count, count))
        )
    info = scalars(*qkv_at, *out_at)
    gain, bias = as_row(ln_gain), as_row(ln_bias)
    back = [exchange(attend(parts, gain, bias, qkv_all, out_all, info)) for parts in sent]
    result = None
    for chunk in range(CHUNKS):
        result = restore_rows(back[chunk], scalars(grid_at), rows, chunk * count, result)
    return result.reshape(fields.shape)


def solution(mesh):
    in_specs = (
        P("dp", "space", None, None),
        P(),
        P(),
        P(None, "dp"),
        P(),
        P(),
        P(),
        P(None, "dp"),
        P(),
        P(),
        P(None, "dp"),
        P(None, "dp"),
    )
    out_specs = P("dp", "space", None, None)
    return jax.shard_map(local, mesh=mesh, in_specs=in_specs, out_specs=out_specs, check_vma=False)
```

time: 222 us -> 157 us (0.71)
  Pallas kernels: 0 us -> 59.6 us
  starting transfers between devices: 10.4 us -> 55.2 us
  waiting for transfers between devices: 73.2 us -> 29.4 us
  matrix products: 43.4 us -> 0 us
  blocking collectives: 39.9 us -> 0 us
  local copies, waits for them, and re-layouts: 31.5 us -> 10.3 us
  between operations: 13.4 us -> 0.43 us
  other arithmetic: 8.81 us -> 0.61 us
    pallas_call x0 -> x9, Pallas kernels: none -> 59.6 us  [the longest x2 19.1 us: expand_some(): pl.pallas_call(functools.partial(expand_kernel, len(weights), int(aliased...]
    all_gather x3 -> x0, waiting for transfers between devices: 57.2 us -> none  [the longest x1 35.3 us: expand_tokens(): lax.all_gather(w_expand, 'dp', axis=1, tiled=True)]
    ppermute x2 -> x38, starting transfers between devices: 4.62 us -> 55.2 us  [the longest x28 43.6 us: exchange(): parts[k] = lax.ppermute(parts[k], 'space', swaps[k])]
    dot_general x6 -> x0, matrix products: 43.4 us -> none  [the longest x1 21.8 us: project_back(): jnp.dot(flat, lax.all_gather(w_project, 'dp', axis=1, tiled=True), prefer...]
    all_to_all x1 -> x0, blocking collectives: 30.3 us -> none  [local(): lax.all_to_all(finished, 'space', split_axis=1, concat_axis=3, tiled=True)]
    ppermute x2 -> x38, waiting for transfers between devices: 1.41 us -> 29.4 us  [the longest x4 23.9 us: fetch(): got = lax.ppermute(mine, 'dp', [(0, 1), (1, 0)])]
    another operation x4, local copies, waits for them, and re-layouts: 17.4 us -> 1.9 us  [the longest x3 1.9 us: scalars(): return jnp.stack([jnp.asarray(v, jnp.int32) for v in values])]
    all_to_all x1 -> x0, waiting for transfers between devices: 12.6 us -> none  [local(): lax.all_to_all(banded_in, 'space', split_axis=3, concat_axis=1, tiled=True)]
  transfers between devices with their start and end apart: 6 -> 38, of which waited for: 5 -> 6; matrix products, arithmetic and copies ran while one was open for 7% -> 4% of each run, Pallas kernels for 0% -> 36%
where the time goes in v1:
time: 157 us; the launch traced here: 156 us
  Pallas kernels  59.6 us (38%)
  starting transfers between devices  55.2 us (35%)
  waiting for transfers between devices  29.4 us (19%)
  local copies, waits for them, and re-layouts  10.3 us (7%)
    ppermute x28, starting transfers between devices, exchange(): parts[k] = lax.ppermute(parts[k], 'space', swaps[k])  43.6 us
    ppermute x4, waiting for transfers between devices, fetch(): got = lax.ppermute(mine, 'dp', [(0, 1), (1, 0)])  23.9 us
    pallas_call x2, Pallas kernels, expand_some(): pl.pallas_call(functools.partial(expand_kernel, len(weights), int(aliased...  19.1 us
    pallas_call x2, Pallas kernels, attend(): pl.pallas_call(functools.partial(attend_kernel, len(w_qkv), len(w_out)),...  18.9 us
    pallas_call x2, Pallas kernels, project_rows(): pl.pallas_call(functools.partial(project_kernel, len(weights)), grid_spec...  11.9 us
    ppermute x4, starting transfers between devices, fetch(): got = lax.ppermute(mine, 'dp', [(0, 1), (1, 0)])  7.02 us
    pallas_call x2, Pallas kernels, restore_rows(): pl.pallas_call(functools.partial(restore_kernel, int(aliased)), grid_spec...  6.76 us
    ppermute x28, waiting for transfers between devices, exchange(): parts[k] = lax.ppermute(parts[k], 'space', swaps[k])  5.52 us
  transfers between devices with their start and end apart: 38, of which 6 were waited for; matrix products, arithmetic and copies ran while one was open for 4% of the time, Pallas kernels for 36%

profile of v1, /device:TPU:0, one launch (start us, length us, event | category | flops | bytes accessed | tf_op | source)
XLA Modules:
  0.0 155.6 jit_solution(16316620618696577951)
XLA Ops:
  1.1 3.0 %collective-permute-start.6 = (bf16[256,1024]{1,0:T(8,128)(2,1)S(1)}, bf16[256,1024]{1,0:T(8,128)(2,1)S(1)}, u32[]{:S(2)}, u32[]{:S(2)}) collective-permute-start(bf16[256,1024]{1,0:T(8,128)(2,1)S(1)} %constant_dynamic-slice_fusion.1), channel_id=1, source_target_pairs={{0,16},{16,0},{1,17},{17,1},{2,18},{18,2},{3,19},{19,3},{4,20},{20... | collective-permute-start | bytes 1572872 | tf_op jit(solution)/shard_map/ppermute | solution.py:395
  6.3 2.1 %collective-permute-start = (bf16[256,768]{1,0:T(8,128)(2,1)S(1)}, bf16[256,768]{1,0:T(8,128)(2,1)S(1)}, u32[]{:S(2)}, u32[]{:S(2)}) collective-permute-start(bf16[256,768]{1,0:T(8,128)(2,1)S(1)} %constant_dynamic-slice_fusion.3), channel_id=1, source_target_pairs={{0,16},{16,0},{1,17},{17,1},{2,18},{18,2},{3,19},{19,3},{4,20},{20... | collective-permute-start | bytes 1179656 | tf_op jit(solution)/shard_map/ppermute | solution.py:395
  8.4 8.5 %collective-permute-done.6.refs_0_ = bf16[256,1024]{1,0:T(8,128)(2,1)S(1)} collective-permute-done((bf16[256,1024]{1,0:T(8,128)(2,1)S(1)}, bf16[256,1024]{1,0:T(8,128)(2,1)S(1)}, u32[]{:S(2)}, u32[]{:S(2)}) %collective-permute-start.6) | collective-permute-done | bytes 524320 | tf_op jit(solution)/shard_map/ppermute | solution.py:395
  16.9 11.2 %collective-permute-done.8.refs_1_ = bf16[1024,256]{1,0:T(8,128)(2,1)S(1)} collective-permute-done((bf16[1024,256]{1,0:T(8,128)(2,1)S(1)}, bf16[1024,256]{1,0:T(8,128)(2,1)S(1)}, u32[]{:S(2)}, u32[]{:S(2)}) %collective-permute-start.8) | collective-permute-done | bytes 524320 | tf_op jit(solution)/shard_map/ppermute | solution.py:395
  29.3 2.2 %collective-permute-start.4 = (bf16[1,128,512]{2,1,0:T(8,128)(2,1)S(1)}, bf16[1,128,512]{2,1,0:T(8,128)(2,1)S(1)}, u32[]{:S(2)}, u32[]{:S(2)}) collective-permute-start(bf16[1,128,512]{2,1,0:T(8,128)(2,1)S(1)} %get-tuple-element.74), channel_id=1, source_target_pairs={{0,1},{1,2},{2,3},{3,4},{4,5},{5,6},{6,7},{7,8},{8,9},{9,10},{10,1... | collective-permute-start | bytes 393224 | tf_op jit(solution)/shard_map/ppermute | solution.py:387
  31.5 4.2 %collective-permute-done.refs_1_ = bf16[256,768]{1,0:T(8,128)(2,1)S(1)} collective-permute-done((bf16[256,768]{1,0:T(8,128)(2,1)S(1)}, bf16[256,768]{1,0:T(8,128)(2,1)S(1)}, u32[]{:S(2)}, u32[]{:S(2)}) %collective-permute-start) | collective-permute-done | bytes 393248 | tf_op jit(solution)/shard_map/ppermute | solution.py:395
  36.7 1.8 %collective-permute-start.2 = (bf16[256,256]{1,0:T(8,128)(2,1)S(1)}, bf16[256,256]{1,0:T(8,128)(2,1)S(1)}, u32[]{:S(2)}, u32[]{:S(2)}) collective-permute-start(bf16[256,256]{1,0:T(8,128)(2,1)S(1)} %constant_dynamic-slice_fusion.2), channel_id=1, source_target_pairs={{0,16},{16,0},{1,17},{17,1},{2,18},{18,2},{3,19},{19,3},{4,20},{20... | collective-permute-start | bytes 393224 | tf_op jit(solution)/shard_map/ppermute | solution.py:395
  39.9 3.0 %order_rows.1 = (bf16[8,128,512]{2,1,0:T(8,128)(2,1)}, bf16[8,128,512]{2,1,0:T(8,128)(2,1)}) custom-call(bf16[8,128,512]{2,1,0:T(8,128)(2,1)} %bitcast.21, f32[1,512]{1,0:T(1,128)} %bitcast.26, f32[1,512]{1,0:T(1,128)} %bitcast.29), custom_call_target="tpu_custom_call" | custom-call | tf_op jit(solution)/shard_map/order_rows/pallas_call | solution.py:62
  46.6 9.4 %expand_conv.2.refs_5_ = bf16[1024,2048]{1,0:T(8,128)(2,1)} custom-call(s32[5]{0:T(128)} %pad_add_fusion.info, bf16[8,128,512]{2,1,0:T(8,128)(2,1)} %get-tuple-element.39.normed, bf16[1,128,512]{2,1,0:T(8,128)(2,1)} %copy-done.4, bf16[1,128,512]{2,1,0:T(8,128)(2,1)} %copy-done.5, f32[1,512]{1,0:T(1,128)} %bitcast.27, f32[1,512]{1,0:T(1,128)} %bitcast.30, ...), custom_call_target="tpu_custom_call" | custom-call | tf_op jit(solution)/shard_map/expand_conv/pallas_call | solution.py:155
  56.8 9.7 %expand_conv.3.spatial = bf16[1024,2048]{1,0:T(8,128)(2,1)} custom-call(s32[5]{0:T(128)} %stack.81.info, bf16[8,128,512]{2,1,0:T(8,128)(2,1)} %get-tuple-element.39.normed, bf16[1,128,512]{2,1,0:T(8,128)(2,1)} %copy-done.4, bf16[1,128,512]{2,1,0:T(8,128)(2,1)} %copy-done.5, f32[1,512]{1,0:T(1,128)} %bitcast.28, ...), custom_call_target="tpu_custom_call", output_to_operand_aliasing={{}: (11, {})} | custom-call | tf_op jit(solution)/shard_map/expand_conv/pallas_call | solution.py:155
  67.3 5.9 %project_rows.3 = (bf16[4,16,512]{2,1,0:T(8,128)(2,1)}, bf16[4,16,512]{2,1,0:T(8,128)(2,1)}, bf16[4,16,512]{2,1,0:T(8,128)(2,1)}, bf16[4,16,512]{2,1,0:T(8,128)(...) custom-call(s32[7]{0:T(128)} %stack.75.info, ...), custom_call_target="tpu_custom_call" | custom-call | tf_op jit(solution)/shard_map/project_rows/pallas_call | solution.py:208
  73.2 1.6 collective-permute-start.24
  74.8 1.6 %collective-permute-start.25 = (bf16[4,16,512]{2,1,0:T(8,128)(2,1)}, bf16[4,16,512]{2,1,0:T(8,128)(2,1)S(1)}, u32[]{:S(2)}, u32[]{:S(2)}) collective-permute-start(bf16[4,16,512]{2,1,0:T(8,128)(2,1)} %get-tuple-element.59), channel_id=1, source_target_pairs={{0,4},{1,5},{2,6},{3,7},{4,0},{5,1},{6,2},{7,3},{8,12},{9,13},{10,... | collective-permute-start | bytes 196616 | tf_op jit(solution)/shard_map/ppermute | solution.py:428
  76.9 3.0 %collective-permute-start.27 = (bf16[4,16,512]{2,1,0:T(8,128)(2,1)}, bf16[4,16,512]{2,1,0:T(8,128)(2,1)S(1)}, u32[]{:S(2)}, u32[]{:S(2)}) collective-permute-start(bf16[4,16,512]{2,1,0:T(8,128)(2,1)} %get-tuple-element.61), channel_id=1, source_target_pairs={{0,8},{1,9},{2,10},{3,11},{4,12},{5,13},{6,14},{7,15},{8,0},{9,1},... | collective-permute-start | bytes 196616 | tf_op jit(solution)/shard_map/ppermute | solution.py:428
  80.0 5.9 %project_rows.2 = (bf16[4,16,512]{2,1,0:T(8,128)(2,1)}, bf16[4,16,512]{2,1,0:T(8,128)(2,1)}, bf16[4,16,512]{2,1,0:T(8,128)(2,1)}, bf16[4,16,512]{2,1,0:T(8,128)(...) custom-call(s32[7]{0:T(128)} %stack.75.info, ...), custom_call_target="tpu_custom_call" | custom-call | tf_op jit(solution)/shard_map/project_rows/pallas_call | solution.py:208
  86.7 3.7 %collective-permute-start.29 = (bf16[4,16,512]{2,1,0:T(8,128)(2,1)S(1)}, bf16[4,16,512]{2,1,0:T(8,128)(2,1)S(1)}, u32[]{:S(2)}, u32[]{:S(2)}) collective-permute-start(bf16[4,16,512]{2,1,0:T(8,128)(2,1)S(1)} %copy-done.39), channel_id=1, source_target_pairs={{0,12},{1,13},{2,14},{3,15},{4,8},{5,9},{6,10},{7,11},{8,4},{9,5},... | collective-permute-start | bytes 196616 | tf_op jit(solution)/shard_map/ppermute | solution.py:428
  92.2 3.7 %collective-permute-done.28.refs_11_ = bf16[4,16,512]{2,1,0:T(8,128)(2,1)S(1)} collective-permute-done((bf16[4,16,512]{2,1,0:T(8,128)(2,1)S(1)}, bf16[4,16,512]{2,1,0:T(8,128)(2,1)S(1)}, u32[]{:S(2)}, u32[]{:S(2)}) %collective-permute-start.28) | collective-permute-done | bytes 65568 | tf_op jit(solution)/shard_map/ppermute | solution.py:428
  97.7 1.3 collective-permute-start.14
  99.1 2.6 %collective-permute-start.15 = (bf16[4,16,512]{2,1,0:T(8,128)(2,1)}, bf16[4,16,512]{2,1,0:T(8,128)(2,1)S(1)}, u32[]{:S(2)}, u32[]{:S(2)}) collective-permute-start(bf16[4,16,512]{2,1,0:T(8,128)(2,1)} %get-tuple-element.47), channel_id=1, source_target_pairs={{0,12},{1,13},{2,14},{3,15},{4,8},{5,9},{6,10},{7,11},{8,4},{9,5},... | collective-permute-start | bytes 196616 | tf_op jit(solution)/shard_map/ppermute | solution.py:428
  102.3 2.1 %collective-permute-start.16 = (bf16[4,16,512]{2,1,0:T(8,128)(2,1)}, bf16[4,16,512]{2,1,0:T(8,128)(2,1)S(1)}, u32[]{:S(2)}, u32[]{:S(2)}) collective-permute-start(bf16[4,16,512]{2,1,0:T(8,128)(2,1)} %get-tuple-element.48), channel_id=1, source_target_pairs={{0,14},{1,15},{2,12},{3,13},{4,10},{5,11},{6,8},{7,9},{8,6},{9,7},... | collective-permute-start | bytes 196616 | tf_op jit(solution)/shard_map/ppermute | solution.py:428
  104.5 9.4 %attend.3 = (bf16[4,16,512]{2,1,0:T(8,128)(2,1)}, bf16[4,16,512]{2,1,0:T(8,128)(2,1)}, bf16[4,16,512]{2,1,0:T(8,128)(2,1)}, bf16[4,16,512]{2,1,0:T(8,128)(2,1)},...) custom-call(s32[12]{0:T(128)} %stack.74.info, ...), custom_call_target="tpu_custom_call" | custom-call | tf_op jit(solution)/shard_map/attend/pallas_call | solution.py:300
  115.5 2.0 %collective-permute-start.33 = (bf16[4,16,512]{2,1,0:T(8,128)(2,1)}, bf16[4,16,512]{2,1,0:T(8,128)(2,1)S(1)}, u32[]{:S(2)}, u32[]{:S(2)}) collective-permute-start(bf16[4,16,512]{2,1,0:T(8,128)(2,1)} %get-tuple-element.68), channel_id=1, source_target_pairs={{0,6},{1,7},{2,4},{3,5},{4,2},{5,3},{6,0},{7,1},{8,14},{9,15},{10,... | collective-permute-start | bytes 196616 | tf_op jit(solution)/shard_map/ppermute | solution.py:428
  117.5 2.3 %collective-permute-start.34 = (bf16[4,16,512]{2,1,0:T(8,128)(2,1)}, bf16[4,16,512]{2,1,0:T(8,128)(2,1)S(1)}, u32[]{:S(2)}, u32[]{:S(2)}) collective-permute-start(bf16[4,16,512]{2,1,0:T(8,128)(2,1)} %get-tuple-element.69), channel_id=1, source_target_pairs={{0,8},{1,9},{2,10},{3,11},{4,12},{5,13},{6,14},{7,15},{8,0},{9,1},... | collective-permute-start | bytes 196616 | tf_op jit(solution)/shard_map/ppermute | solution.py:428
  120.5 9.4 %attend.2 = (bf16[4,16,512]{2,1,0:T(8,128)(2,1)}, bf16[4,16,512]{2,1,0:T(8,128)(2,1)}, bf16[4,16,512]{2,1,0:T(8,128)(2,1)}, bf16[4,16,512]{2,1,0:T(8,128)(2,1)},...) custom-call(s32[12]{0:T(128)} %stack.74.info, ...), custom_call_target="tpu_custom_call" | custom-call | tf_op jit(solution)/shard_map/attend/pallas_call | solution.py:300
  130.0 3.2 %collective-permute-start.36 = (bf16[4,16,512]{2,1,0:T(8,128)(2,1)}, bf16[4,16,512]{2,1,0:T(8,128)(2,1)S(1)}, u32[]{:S(2)}, u32[]{:S(2)}) collective-permute-start(bf16[4,16,512]{2,1,0:T(8,128)(2,1)} %get-tuple-element.71), channel_id=1, source_target_pairs={{0,12},{1,13},{2,14},{3,15},{4,8},{5,9},{6,10},{7,11},{8,4},{9,5},... | collective-permute-start | bytes 196616 | tf_op jit(solution)/shard_map/ppermute | solution.py:428
  133.2 1.5 collective-permute-start.37
  135.4 2.9 %collective-permute-start.19 = (bf16[4,16,512]{2,1,0:T(8,128)(2,1)}, bf16[4,16,512]{2,1,0:T(8,128)(2,1)S(1)}, u32[]{:S(2)}, u32[]{:S(2)}) collective-permute-start(bf16[4,16,512]{2,1,0:T(8,128)(2,1)} %get-tuple-element.52), channel_id=1, source_target_pairs={{0,6},{1,7},{2,4},{3,5},{4,2},{5,3},{6,0},{7,1},{8,14},{9,15},{10,... | collective-permute-start | bytes 196616 | tf_op jit(solution)/shard_map/ppermute | solution.py:428
  138.3 2.3 %collective-permute-start.20 = (bf16[4,16,512]{2,1,0:T(8,128)(2,1)}, bf16[4,16,512]{2,1,0:T(8,128)(2,1)S(1)}, u32[]{:S(2)}, u32[]{:S(2)}) collective-permute-start(bf16[4,16,512]{2,1,0:T(8,128)(2,1)} %get-tuple-element.53), channel_id=1, source_target_pairs={{0,8},{1,9},{2,10},{3,11},{4,12},{5,13},{6,14},{7,15},{8,0},{9,1},... | collective-permute-start | bytes 196616 | tf_op jit(solution)/shard_map/ppermute | solution.py:428
  140.6 2.8 %collective-permute-start.21 = (bf16[4,16,512]{2,1,0:T(8,128)(2,1)}, bf16[4,16,512]{2,1,0:T(8,128)(2,1)S(1)}, u32[]{:S(2)}, u32[]{:S(2)}) collective-permute-start(bf16[4,16,512]{2,1,0:T(8,128)(2,1)} %get-tuple-element.54), channel_id=1, source_target_pairs={{0,10},{1,11},{2,8},{3,9},{4,14},{5,15},{6,12},{7,13},{8,2},{9,3},... | collective-permute-start | bytes 196616 | tf_op jit(solution)/shard_map/ppermute | solution.py:428
  144.4 2.6 %collective-permute-start.23 = (bf16[4,16,512]{2,1,0:T(8,128)(2,1)}, bf16[4,16,512]{2,1,0:T(8,128)(2,1)S(1)}, u32[]{:S(2)}, u32[]{:S(2)}) collective-permute-start(bf16[4,16,512]{2,1,0:T(8,128)(2,1)} %get-tuple-element.56), channel_id=1, source_target_pairs={{0,14},{1,15},{2,12},{3,13},{4,10},{5,11},{6,8},{7,9},{8,6},{9,7},... | collective-permute-start | bytes 196616 | tf_op jit(solution)/shard_map/ppermute | solution.py:428
  147.0 3.4 %restore_rows.2.refs_8_ = bf16[8,128,512]{2,1,0:T(8,128)(2,1)} custom-call(s32[1]{0:T(128)} %bitcast.info, bf16[4,16,512]{2,1,0:T(8,128)(2,1)} %get-tuple-element.65.refs_0_, bf16[4,16,512]{2,1,0:T(8,128)(2,1)} %copy-done.10, bf16[4,16,512]{2,1,0:T(8,128)(2,1)} %copy-done.13, bf16[4,16,512]{2,1,0:T(8,128)(2,1)} %copy-done.17, ...), custom_call_target="tpu_custom_call" | custom-call | tf_op jit(solution)/shard_map/restore_rows/pallas_call | solution.py:339
  152.2 3.4 %restore_rows.3 = bf16[8,128,512]{2,1,0:T(8,128)(2,1)} custom-call(s32[1]{0:T(128)} %bitcast.info, bf16[4,16,512]{2,1,0:T(8,128)(2,1)} %get-tuple-element.49.refs_0_, bf16[4,16,512]{2,1,0:T(8,128)(2,1)} %copy-done.27, bf16[4,16,512]{2,1,0:T(8,128)(2,1)} %copy-done.30, bf16[4,16,512]{2,1,0:T(8,128)(2,1)} %copy-done.32, ...), custom_call_target="tpu_custom_call", output_to_operand_aliasing={{}: (9, {})} | custom-call | tf_op jit(solution)/shard_map/restore_rows/pallas_call | solution.py:339
  (145 shorter events, 23.3 us)
Async XLA Ops:
  1.1 15.8 %collective-permute-start.6 = (bf16[256,1024]{1,0:T(8,128)(2,1)S(1)}, bf16[256,1024]{1,0:T(8,128)(2,1)S(1)}, u32[]{:S(2)}, u32[]{:S(2)}) collective-permute-start(bf16[256,1024]{1,0:T(8,128)(2,1)S(1)} %constant_dynamic-slice_fusion.1), channel_id=1, source_target_pairs={{0,16},{16,0},{1,17},{17,1},{2,18},{18,2},{3,19},{19,3},{4,20},{20... | collective-permute-start | bytes 1572872 | tf_op jit(solution)/shard_map/ppermute | solution.py:395
  5.2 22.9 %collective-permute-start.8 = (bf16[1024,256]{1,0:T(8,128)(2,1)S(1)}, bf16[1024,256]{1,0:T(8,128)(2,1)S(1)}, u32[]{:S(2)}, u32[]{:S(2)}) collective-permute-start(bf16[1024,256]{1,0:T(8,128)(2,1)S(1)} %constant_dynamic-slice_fusion), channel_id=1, source_target_pairs={{0,16},{16,0},{1,17},{17,1},{2,18},{18,2},{3,19},{19,3},{4,20},{20... | collective-permute-start | bytes 1572872 | tf_op jit(solution)/shard_map/ppermute | solution.py:395
  6.3 29.4 %collective-permute-start = (bf16[256,768]{1,0:T(8,128)(2,1)S(1)}, bf16[256,768]{1,0:T(8,128)(2,1)S(1)}, u32[]{:S(2)}, u32[]{:S(2)}) collective-permute-start(bf16[256,768]{1,0:T(8,128)(2,1)S(1)} %constant_dynamic-slice_fusion.3), channel_id=1, source_target_pairs={{0,16},{16,0},{1,17},{17,1},{2,18},{18,2},{3,19},{19,3},{4,20},{20... | collective-permute-start | bytes 1179656 | tf_op jit(solution)/shard_map/ppermute | solution.py:395
  16.9 39.1 %collective-permute-start.7 = (bf16[256,1024]{1,0:T(8,128)(2,1)S(1)}, bf16[256,1024]{1,0:T(8,128)(2,1)S(1)}, u32[]{:S(2)}, u32[]{:S(2)}) collective-permute-start(bf16[256,1024]{1,0:T(8,128)(2,1)S(1)} %collective-permute-done.6.refs_0_), channel_id=1, source_target_pairs={{0,1},{1,0},{2,3},{3,2},{4,5},{5,4},{6,7},{7,6},{8,9},{9,8},{10,11... | collective-permute-start | bytes 1572872 | tf_op jit(solution)/shard_map/ppermute | solution.py:396
  28.1 38.4 %collective-permute-start.9 = (bf16[1024,256]{1,0:T(8,128)(2,1)S(1)}, bf16[1024,256]{1,0:T(8,128)(2,1)S(1)}, u32[]{:S(2)}, u32[]{:S(2)}) collective-permute-start(bf16[1024,256]{1,0:T(8,128)(2,1)S(1)} %collective-permute-done.8.refs_1_), channel_id=1, source_target_pairs={{0,1},{1,0},{2,3},{3,2},{4,5},{5,4},{6,7},{7,6},{8,9},{9,8},{10,11... | collective-permute-start | bytes 1572872 | tf_op jit(solution)/shard_map/ppermute | solution.py:396
  29.3 9.3 %collective-permute-start.4 = (bf16[1,128,512]{2,1,0:T(8,128)(2,1)S(1)}, bf16[1,128,512]{2,1,0:T(8,128)(2,1)S(1)}, u32[]{:S(2)}, u32[]{:S(2)}) collective-permute-start(bf16[1,128,512]{2,1,0:T(8,128)(2,1)S(1)} %get-tuple-element.74), channel_id=1, source_target_pairs={{0,1},{1,2},{2,3},{3,4},{4,5},{5,6},{6,7},{7,8},{8,9},{9,10},{10,1... | collective-permute-start | bytes 393224 | tf_op jit(solution)/shard_map/ppermute | solution.py:387
  35.7 50.2 %collective-permute-start.1 = (bf16[256,768]{1,0:T(8,128)(2,1)S(1)}, bf16[256,768]{1,0:T(8,128)(2,1)S(1)}, u32[]{:S(2)}, u32[]{:S(2)}) collective-permute-start(bf16[256,768]{1,0:T(8,128)(2,1)S(1)} %collective-permute-done.refs_1_), channel_id=1, source_target_pairs={{0,1},{1,0},{2,3},{3,2},{4,5},{5,4},{6,7},{7,6},{8,9},{9,8},{10,11... | collective-permute-start | bytes 1179656 | tf_op jit(solution)/shard_map/ppermute | solution.py:396
  44.2 32.8 %collective-permute-start.3 = (bf16[256,256]{1,0:T(8,128)(2,1)S(1)}, bf16[256,256]{1,0:T(8,128)(2,1)S(1)}, u32[]{:S(2)}, u32[]{:S(2)}) collective-permute-start(bf16[256,256]{1,0:T(8,128)(2,1)S(1)} %collective-permute-done.2.refs_4_), channel_id=1, source_target_pairs={{0,1},{1,0},{2,3},{3,2},{4,5},{5,4},{6,7},{7,6},{8,9},{9,8},{10,11... | collective-permute-start | bytes 393224 | tf_op jit(solution)/shard_map/ppermute | solution.py:396
  73.2 13.5 %collective-permute-start.24 = (bf16[4,16,512]{2,1,0:T(8,128)(2,1)}, bf16[4,16,512]{2,1,0:T(8,128)(2,1)S(1)}, u32[]{:S(2)}, u32[]{:S(2)}) collective-permute-start(bf16[4,16,512]{2,1,0:T(8,128)(2,1)} %get-tuple-element.58), channel_id=1, source_target_pairs={{0,2},{1,3},{2,0},{3,1},{4,6},{5,7},{6,4},{7,5},{8,10},{9,11},{10,... | collective-permute-start | bytes 196616 | tf_op jit(solution)/shard_map/ppermute | solution.py:428
  74.8 15.6 %collective-permute-start.25 = (bf16[4,16,512]{2,1,0:T(8,128)(2,1)}, bf16[4,16,512]{2,1,0:T(8,128)(2,1)S(1)}, u32[]{:S(2)}, u32[]{:S(2)}) collective-permute-start(bf16[4,16,512]{2,1,0:T(8,128)(2,1)} %get-tuple-element.59), channel_id=1, source_target_pairs={{0,4},{1,5},{2,6},{3,7},{4,0},{5,1},{6,2},{7,3},{8,12},{9,13},{10,... | collective-permute-start | bytes 196616 | tf_op jit(solution)/shard_map/ppermute | solution.py:428
  76.4 14.7 %collective-permute-start.26 = (bf16[4,16,512]{2,1,0:T(8,128)(2,1)}, bf16[4,16,512]{2,1,0:T(8,128)(2,1)S(1)}, u32[]{:S(2)}, u32[]{:S(2)}) collective-permute-start(bf16[4,16,512]{2,1,0:T(8,128)(2,1)} %get-tuple-element.60), channel_id=1, source_target_pairs={{0,6},{1,7},{2,4},{3,5},{4,2},{5,3},{6,0},{7,1},{8,14},{9,15},{10,... | collective-permute-start | bytes 196616 | tf_op jit(solution)/shard_map/ppermute | solution.py:428
  76.9 15.2 %collective-permute-start.27 = (bf16[4,16,512]{2,1,0:T(8,128)(2,1)}, bf16[4,16,512]{2,1,0:T(8,128)(2,1)S(1)}, u32[]{:S(2)}, u32[]{:S(2)}) collective-permute-start(bf16[4,16,512]{2,1,0:T(8,128)(2,1)} %get-tuple-element.61), channel_id=1, source_target_pairs={{0,8},{1,9},{2,10},{3,11},{4,12},{5,13},{6,14},{7,15},{8,0},{9,1},... | collective-permute-start | bytes 196616 | tf_op jit(solution)/shard_map/ppermute | solution.py:428
  86.0 9.9 %collective-permute-start.28 = (bf16[4,16,512]{2,1,0:T(8,128)(2,1)S(1)}, bf16[4,16,512]{2,1,0:T(8,128)(2,1)S(1)}, u32[]{:S(2)}, u32[]{:S(2)}) collective-permute-start(bf16[4,16,512]{2,1,0:T(8,128)(2,1)S(1)} %copy-done.40), channel_id=1, source_target_pairs={{0,10},{1,11},{2,8},{3,9},{4,14},{5,15},{6,12},{7,13},{8,2},{9,3},... | collective-permute-start | bytes 196616 | tf_op jit(solution)/shard_map/ppermute | solution.py:428
  86.7 9.2 %collective-permute-start.29 = (bf16[4,16,512]{2,1,0:T(8,128)(2,1)S(1)}, bf16[4,16,512]{2,1,0:T(8,128)(2,1)S(1)}, u32[]{:S(2)}, u32[]{:S(2)}) collective-permute-start(bf16[4,16,512]{2,1,0:T(8,128)(2,1)S(1)} %copy-done.39), channel_id=1, source_target_pairs={{0,12},{1,13},{2,14},{3,15},{4,8},{5,9},{6,10},{7,11},{8,4},{9,5},... | collective-permute-start | bytes 196616 | tf_op jit(solution)/shard_map/ppermute | solution.py:428
  91.1 8.0 %collective-permute-start.10 = (bf16[4,16,512]{2,1,0:T(8,128)(2,1)}, bf16[4,16,512]{2,1,0:T(8,128)(2,1)S(1)}, u32[]{:S(2)}, u32[]{:S(2)}) collective-permute-start(bf16[4,16,512]{2,1,0:T(8,128)(2,1)} %get-tuple-element.42), channel_id=1, source_target_pairs={{0,2},{1,3},{2,0},{3,1},{4,6},{5,7},{6,4},{7,5},{8,10},{9,11},{10,... | collective-permute-start | bytes 196616 | tf_op jit(solution)/shard_map/ppermute | solution.py:428
  92.1 10.2 %collective-permute-start.11 = (bf16[4,16,512]{2,1,0:T(8,128)(2,1)}, bf16[4,16,512]{2,1,0:T(8,128)(2,1)S(1)}, u32[]{:S(2)}, u32[]{:S(2)}) collective-permute-start(bf16[4,16,512]{2,1,0:T(8,128)(2,1)} %get-tuple-element.43), channel_id=1, source_target_pairs={{0,4},{1,5},{2,6},{3,7},{4,0},{5,1},{6,2},{7,3},{8,12},{9,13},{10,... | collective-permute-start | bytes 196616 | tf_op jit(solution)/shard_map/ppermute | solution.py:428
  95.9 18.1 %collective-permute-start.12 = (bf16[4,16,512]{2,1,0:T(8,128)(2,1)}, bf16[4,16,512]{2,1,0:T(8,128)(2,1)S(1)}, u32[]{:S(2)}, u32[]{:S(2)}) collective-permute-start(bf16[4,16,512]{2,1,0:T(8,128)(2,1)} %get-tuple-element.44), channel_id=1, source_target_pairs={{0,6},{1,7},{2,4},{3,5},{4,2},{5,3},{6,0},{7,1},{8,14},{9,15},{10,... | collective-permute-start | bytes 196616 | tf_op jit(solution)/shard_map/ppermute | solution.py:428
  95.9 18.7 %collective-permute-start.13 = (bf16[4,16,512]{2,1,0:T(8,128)(2,1)}, bf16[4,16,512]{2,1,0:T(8,128)(2,1)S(1)}, u32[]{:S(2)}, u32[]{:S(2)}) collective-permute-start(bf16[4,16,512]{2,1,0:T(8,128)(2,1)} %get-tuple-element.45), channel_id=1, source_target_pairs={{0,8},{1,9},{2,10},{3,11},{4,12},{5,13},{6,14},{7,15},{8,0},{9,1},... | collective-permute-start | bytes 196616 | tf_op jit(solution)/shard_map/ppermute | solution.py:428
  97.7 17.8 %collective-permute-start.14 = (bf16[4,16,512]{2,1,0:T(8,128)(2,1)}, bf16[4,16,512]{2,1,0:T(8,128)(2,1)S(1)}, u32[]{:S(2)}, u32[]{:S(2)}) collective-permute-start(bf16[4,16,512]{2,1,0:T(8,128)(2,1)} %get-tuple-element.46), channel_id=1, source_target_pairs={{0,10},{1,11},{2,8},{3,9},{4,14},{5,15},{6,12},{7,13},{8,2},{9,3},... | collective-permute-start | bytes 196616 | tf_op jit(solution)/shard_map/ppermute | solution.py:428
  99.1 18.5 %collective-permute-start.15 = (bf16[4,16,512]{2,1,0:T(8,128)(2,1)}, bf16[4,16,512]{2,1,0:T(8,128)(2,1)S(1)}, u32[]{:S(2)}, u32[]{:S(2)}) collective-permute-start(bf16[4,16,512]{2,1,0:T(8,128)(2,1)} %get-tuple-element.47), channel_id=1, source_target_pairs={{0,12},{1,13},{2,14},{3,15},{4,8},{5,9},{6,10},{7,11},{8,4},{9,5},... | collective-permute-start | bytes 196616 | tf_op jit(solution)/shard_map/ppermute | solution.py:428
  102.3 17.5 %collective-permute-start.16 = (bf16[4,16,512]{2,1,0:T(8,128)(2,1)}, bf16[4,16,512]{2,1,0:T(8,128)(2,1)S(1)}, u32[]{:S(2)}, u32[]{:S(2)}) collective-permute-start(bf16[4,16,512]{2,1,0:T(8,128)(2,1)} %get-tuple-element.48), channel_id=1, source_target_pairs={{0,14},{1,15},{2,12},{3,13},{4,10},{5,11},{6,8},{7,9},{8,6},{9,7},... | collective-permute-start | bytes 196616 | tf_op jit(solution)/shard_map/ppermute | solution.py:428
  114.0 16.0 %collective-permute-start.31 = (bf16[4,16,512]{2,1,0:T(8,128)(2,1)}, bf16[4,16,512]{2,1,0:T(8,128)(2,1)S(1)}, u32[]{:S(2)}, u32[]{:S(2)}) collective-permute-start(bf16[4,16,512]{2,1,0:T(8,128)(2,1)} %get-tuple-element.66), channel_id=1, source_target_pairs={{0,2},{1,3},{2,0},{3,1},{4,6},{5,7},{6,4},{7,5},{8,10},{9,11},{10,... | collective-permute-start | bytes 196616 | tf_op jit(solution)/shard_map/ppermute | solution.py:428
  114.6 18.6 %collective-permute-start.32 = (bf16[4,16,512]{2,1,0:T(8,128)(2,1)}, bf16[4,16,512]{2,1,0:T(8,128)(2,1)S(1)}, u32[]{:S(2)}, u32[]{:S(2)}) collective-permute-start(bf16[4,16,512]{2,1,0:T(8,128)(2,1)} %get-tuple-element.67), channel_id=1, source_target_pairs={{0,4},{1,5},{2,6},{3,7},{4,0},{5,1},{6,2},{7,3},{8,12},{9,13},{10,... | collective-permute-start | bytes 196616 | tf_op jit(solution)/shard_map/ppermute | solution.py:428
  115.5 19.2 %collective-permute-start.33 = (bf16[4,16,512]{2,1,0:T(8,128)(2,1)}, bf16[4,16,512]{2,1,0:T(8,128)(2,1)S(1)}, u32[]{:S(2)}, u32[]{:S(2)}) collective-permute-start(bf16[4,16,512]{2,1,0:T(8,128)(2,1)} %get-tuple-element.68), channel_id=1, source_target_pairs={{0,6},{1,7},{2,4},{3,5},{4,2},{5,3},{6,0},{7,1},{8,14},{9,15},{10,... | collective-permute-start | bytes 196616 | tf_op jit(solution)/shard_map/ppermute | solution.py:428
  117.5 17.8 %collective-permute-start.34 = (bf16[4,16,512]{2,1,0:T(8,128)(2,1)}, bf16[4,16,512]{2,1,0:T(8,128)(2,1)S(1)}, u32[]{:S(2)}, u32[]{:S(2)}) collective-permute-start(bf16[4,16,512]{2,1,0:T(8,128)(2,1)} %get-tuple-element.69), channel_id=1, source_target_pairs={{0,8},{1,9},{2,10},{3,11},{4,12},{5,13},{6,14},{7,15},{8,0},{9,1},... | collective-permute-start | bytes 196616 | tf_op jit(solution)/shard_map/ppermute | solution.py:428
  119.8 15.6 %collective-permute-start.35 = (bf16[4,16,512]{2,1,0:T(8,128)(2,1)}, bf16[4,16,512]{2,1,0:T(8,128)(2,1)S(1)}, u32[]{:S(2)}, u32[]{:S(2)}) collective-permute-start(bf16[4,16,512]{2,1,0:T(8,128)(2,1)} %get-tuple-element.70), channel_id=1, source_target_pairs={{0,10},{1,11},{2,8},{3,9},{4,14},{5,15},{6,12},{7,13},{8,2},{9,3},... | collective-permute-start | bytes 196616 | tf_op jit(solution)/shard_map/ppermute | solution.py:428
  130.0 8.3 %collective-permute-start.36 = (bf16[4,16,512]{2,1,0:T(8,128)(2,1)}, bf16[4,16,512]{2,1,0:T(8,128)(2,1)S(1)}, u32[]{:S(2)}, u32[]{:S(2)}) collective-permute-start(bf16[4,16,512]{2,1,0:T(8,128)(2,1)} %get-tuple-element.71), channel_id=1, source_target_pairs={{0,12},{1,13},{2,14},{3,15},{4,8},{5,9},{6,10},{7,11},{8,4},{9,5},... | collective-permute-start | bytes 196616 | tf_op jit(solution)/shard_map/ppermute | solution.py:428
  134.7 8.6 %collective-permute-start.17 = (bf16[4,16,512]{2,1,0:T(8,128)(2,1)}, bf16[4,16,512]{2,1,0:T(8,128)(2,1)S(1)}, u32[]{:S(2)}, u32[]{:S(2)}) collective-permute-start(bf16[4,16,512]{2,1,0:T(8,128)(2,1)} %get-tuple-element.50), channel_id=1, source_target_pairs={{0,2},{1,3},{2,0},{3,1},{4,6},{5,7},{6,4},{7,5},{8,10},{9,11},{10,... | collective-permute-start | bytes 196616 | tf_op jit(solution)/shard_map/ppermute | solution.py:428
  135.3 9.0 %collective-permute-start.18 = (bf16[4,16,512]{2,1,0:T(8,128)(2,1)}, bf16[4,16,512]{2,1,0:T(8,128)(2,1)S(1)}, u32[]{:S(2)}, u32[]{:S(2)}) collective-permute-start(bf16[4,16,512]{2,1,0:T(8,128)(2,1)} %get-tuple-element.51), channel_id=1, source_target_pairs={{0,4},{1,5},{2,6},{3,7},{4,0},{5,1},{6,2},{7,3},{8,12},{9,13},{10,... | collective-permute-start | bytes 196616 | tf_op jit(solution)/shard_map/ppermute | solution.py:428
  135.4 15.1 %collective-permute-start.19 = (bf16[4,16,512]{2,1,0:T(8,128)(2,1)}, bf16[4,16,512]{2,1,0:T(8,128)(2,1)S(1)}, u32[]{:S(2)}, u32[]{:S(2)}) collective-permute-start(bf16[4,16,512]{2,1,0:T(8,128)(2,1)} %get-tuple-element.52), channel_id=1, source_target_pairs={{0,6},{1,7},{2,4},{3,5},{4,2},{5,3},{6,0},{7,1},{8,14},{9,15},{10,... | collective-permute-start | bytes 196616 | tf_op jit(solution)/shard_map/ppermute | solution.py:428
  138.3 12.2 %collective-permute-start.20 = (bf16[4,16,512]{2,1,0:T(8,128)(2,1)}, bf16[4,16,512]{2,1,0:T(8,128)(2,1)S(1)}, u32[]{:S(2)}, u32[]{:S(2)}) collective-permute-start(bf16[4,16,512]{2,1,0:T(8,128)(2,1)} %get-tuple-element.53), channel_id=1, source_target_pairs={{0,8},{1,9},{2,10},{3,11},{4,12},{5,13},{6,14},{7,15},{8,0},{9,1},... | collective-permute-start | bytes 196616 | tf_op jit(solution)/shard_map/ppermute | solution.py:428
  140.6 9.9 %collective-permute-start.21 = (bf16[4,16,512]{2,1,0:T(8,128)(2,1)}, bf16[4,16,512]{2,1,0:T(8,128)(2,1)S(1)}, u32[]{:S(2)}, u32[]{:S(2)}) collective-permute-start(bf16[4,16,512]{2,1,0:T(8,128)(2,1)} %get-tuple-element.54), channel_id=1, source_target_pairs={{0,10},{1,11},{2,8},{3,9},{4,14},{5,15},{6,12},{7,13},{8,2},{9,3},... | collective-permute-start | bytes 196616 | tf_op jit(solution)/shard_map/ppermute | solution.py:428
  (47 other events, 526.8 us)

commit v2 on v1

v2 whole, which is shorter than its diff:
```python
import functools
import math

import jax
import jax.numpy as jnp
from jax import lax
from jax.experimental import pallas as pl
from jax.experimental.pallas import tpu as pltpu
from jax.sharding import PartitionSpec as P

HD = 32
GRID = 8
CHUNKS = 2
ROOT = math.sqrt(2.0 / math.pi)
LIN = 2.0 * ROOT
CUBE = 8.0 * ROOT * 0.044715
F32 = jnp.float32
BF16 = jnp.bfloat16
VMEM_LIMIT = 18 * 1024 * 1024


def half_gelu(half):
    return half + half * jnp.tanh(half * (LIN + CUBE * (half * half)))


def one_hot_order(cols, inverse=False):
    stride = cols // GRID
    row = lax.broadcasted_iota(jnp.int32, (cols, cols), 0)
    col = lax.broadcasted_iota(jnp.int32, (cols, cols), 1)
    if inverse:
        row, col = col, row
    return jnp.where(col == (row % GRID) * stride + row // GRID, 1.0, 0.0).astype(BF16)


def dot(a, b):
    return jnp.dot(a, b, preferred_element_type=F32)


def vmem():
    return pl.BlockSpec(memory_space=pltpu.VMEM)


def smem():
    return pl.BlockSpec(memory_space=pltpu.SMEM)


def params():
    return pltpu.CompilerParams(vmem_limit_bytes=VMEM_LIMIT)


CORE, DP, SPACE, LAST, GROUPS = range(5)


def grid_of(info):
    return info[SPACE] // info[GROUPS]


def cost(flops, moved):
    return pl.CostEstimate(flops=flops, bytes_accessed=moved, transcendentals=flops // 1024)


def share_kernel(info, expand, project, qkv, out, expand_part, project_part, rest_part):
    expand_part[...] = expand[...]
    project_part[...] = project[...]
    width = qkv.shape[1]
    rest_part[:, :width] = qkv[...]
    rest_part[:, width:] = out[...]


def share_weights(info, w_expand, w_project, w_qkv, w_out):
    by_rows = lambda w: pl.BlockSpec((w.shape[0] // 2, w.shape[1]), lambda t, i: (i[CORE], 0))
    by_cols = pl.BlockSpec((w_expand.shape[0], w_expand.shape[1] // 2), lambda t, i: (0, i[CORE]))
    whole = lambda shape: pl.BlockSpec(shape, lambda t, i: (0, 0))
    shapes = [
        (w_expand.shape[0], w_expand.shape[1] // 2),
        (w_project.shape[0] // 2, w_project.shape[1]),
        (w_qkv.shape[0] // 2, w_qkv.shape[1] + w_out.shape[1]),
    ]
    return pl.pallas_call(
        share_kernel,
        grid_spec=pltpu.PrefetchScalarGridSpec(
            num_scalar_prefetch=1,
            grid=(1,),
            in_specs=[by_cols, by_rows(w_project), by_rows(w_qkv), by_rows(w_out)],
            out_specs=[whole(shape) for shape in shapes],
        ),
        out_shape=[jax.ShapeDtypeStruct(shape, BF16) for shape in shapes],
        compiler_params=params(),
        name="share_weights",
    )(info, w_expand, w_project, w_qkv, w_out)


def order_kernel(image, above, below, scale, shift, ordered, normed):
    rows, cols, _ = image.shape
    pick = one_hot_order(cols)
    for row in range(rows + 2):
        if row == 0:
            placed = dot(pick, above[0])
        elif row == rows + 1:
            placed = dot(pick, below[0])
        else:
            placed = dot(pick, image[row - 1])
            ordered[row - 1] = placed.astype(BF16)
        normed[row * cols : (row + 1) * cols, :] = (
            placed * (0.5 * scale[...]) + 0.5 * shift[...]
        ).astype(BF16)


def expand_kernel(first, info, *refs):
    refs = list(refs)
    take = lambda n: [refs.pop(0) for _ in range(n)]
    if first:
        sources = take(5)
    else:
        (normed,) = take(1)
    weight, bias, taps, tap_bias = take(4)
    if first:
        out, ordered, normed = take(3)
    else:
        _, out = take(2)
    raw, wide = refs
    cols = wide.shape[1] - 2 * GRID
    rows = wide.shape[0] - 2
    width = bias.shape[-1]

    if first:

        @pl.when(pl.program_id(0) == 0)
        def _():
            order_kernel(*sources, ordered, normed)

    half_bias = 0.5 * bias[...]
    half_taps = 0.5 * taps[...]
    half_tap_bias = 0.5 * tap_bias[...]
    lane = lax.broadcasted_iota(jnp.int32, (GRID, width), 0)
    batch = (rows + 2) // 2 * cols
    for start in range(0, (rows + 2) * cols, batch):
        raw[start : start + batch, :] = dot(normed[start : start + batch, :], weight[...])
    for row in range(rows + 2):
        value = half_gelu(raw[row * cols : (row + 1) * cols, :] + half_bias)
        if row == 0:
            value = value * jnp.where(info[SPACE] > 0, 1.0, 0.0)
        elif row == rows + 1:
            value = value * jnp.where(info[SPACE] < info[LAST], 1.0, 0.0)
        wide[row, GRID : GRID + cols, :] = value
        head = value[:GRID]
        tail = value[cols - GRID :]
        wide[row, :GRID, :] = jnp.where(lane == 0, 0.0, pltpu.roll(tail, 1, 0))
        wide[row, GRID + cols :, :] = jnp.where(
            lane == GRID - 1, 0.0, pltpu.roll(head, GRID - 1, 0)
        )
        if row >= 2:
            total = half_tap_bias
            for row_off in range(3):
                for col_off in range(3):
                    total = (
                        total
                        + wide[row - 2 + row_off, GRID * col_off : GRID * col_off + cols, :]
                        * half_taps[row_off, col_off][None]
                    )
            out[(row - 2) * cols : (row - 1) * cols, :] = half_gelu(total).astype(BF16)


def expand_some(info, sources, weight, bias, taps, tap_bias, tile_of, spatial):
    first = spatial is None
    chans, here = weight.shape
    inner = bias.shape[-1]
    width = min(256, here)
    if first:
        rows, cols, _ = sources[0].shape
    else:
        rows, cols = spatial[1:]
    whole = lambda shape: pl.BlockSpec(shape, lambda t, info: (0,) * len(shape))
    in_specs = [whole(s.shape) for s in sources]
    in_specs += [
        pl.BlockSpec((chans, width), lambda t, info: (0, t)),
        pl.BlockSpec((1, width), lambda t, info: (0, tile_of(info, t))),
        pl.BlockSpec((3, 3, width), lambda t, info: (0, 0, tile_of(info, t))),
        pl.BlockSpec((1, width), lambda t, info: (0, tile_of(info, t))),
    ]
    operands = [info, *sources, weight, bias, taps, tap_bias]
    out_specs = [pl.BlockSpec((rows * cols, width), lambda t, info: (0, tile_of(info, t)))]
    out_shape = [jax.ShapeDtypeStruct((rows * cols, inner), BF16)]
    aliases = {}
    if first:
        shapes = [(rows, cols, chans), ((rows + 2) * cols, chans)]
        out_specs += [whole(shape) for shape in shapes]
        out_shape += [jax.ShapeDtypeStruct(shape, BF16) for shape in shapes]
    else:
        in_specs.append(pl.BlockSpec(memory_space=pl.ANY))
        aliases = {len(operands): 0}
        operands.append(spatial[0])
    return pl.pallas_call(
        functools.partial(expand_kernel, first),
        grid_spec=pltpu.PrefetchScalarGridSpec(
            num_scalar_prefetch=1,
            grid=(here // width,),
            in_specs=in_specs,
            out_specs=out_specs,
            scratch_shapes=[
                pltpu.VMEM(((rows + 2) * cols, width), F32),
                pltpu.VMEM((rows + 2, cols + 2 * GRID, width), F32),
            ],
        ),
        out_shape=out_shape,
        input_output_aliases=aliases,
        compiler_params=params(),
        cost_estimate=cost(2 * rows * cols * chans * here, 1 << 22),
        name="expand_conv",
    )(*operands)


def pieced_dot(lhs, pieces, info, put):
    own = pieces[0]
    width = own.shape[1]
    if len(pieces) == 1:
        put(0, width, dot(lhs[...], own[...]))
        return
    mine = info[DP]
    put(pl.multiple_of(mine * width, width), width, dot(lhs[...], own[...]))
    total = None
    for n, piece in enumerate(pieces[1:]):
        depth = piece.shape[0]
        at = info[CORE] if n == 0 else 1 - info[CORE]
        span = pl.ds(pl.multiple_of(at * depth, depth), depth)
        part = dot(lhs[:, span], piece[...])
        total = part if total is None else total + part
    put(pl.multiple_of((1 - mine) * width, width), width, total)


def project_kernel(pieces, info, spatial, ordered, *refs):
    weights = refs[:pieces]
    outs = refs[pieces : pieces + GRID]
    (conv,) = refs[pieces + GRID :]
    count, cols, chans = ordered.shape
    size = outs[0].shape[1]

    def put(start, width, product):
        span = pl.ds(start, width)
        for row in range(count):
            at = slice(row * cols, (row + 1) * cols)
            conv[at, span] = (ordered[row, :, span].astype(F32) + product[at]).astype(BF16)

    pieced_dot(spatial, weights, info, put)
    mine = grid_of(info)
    for k in range(GRID):
        start = pl.multiple_of((mine ^ k) * size, size)
        for row in range(count):
            outs[k][row] = conv[pl.ds(row * cols + start, size), :]


def project_rows(info, spatial, ordered, weights, chunk, count):
    rows, cols, chans = ordered.shape
    inner = spatial.shape[1]
    size = cols // GRID
    out = jax.ShapeDtypeStruct((count, size, chans), BF16)
    whole = lambda shape: pl.BlockSpec(shape, lambda t, info: (0,) * len(shape))
    return pl.pallas_call(
        functools.partial(project_kernel, len(weights)),
        grid_spec=pltpu.PrefetchScalarGridSpec(
            num_scalar_prefetch=1,
            grid=(1,),
            in_specs=[
                pl.BlockSpec((count * cols, inner), lambda t, info: (chunk, 0)),
                pl.BlockSpec((count, cols, chans), lambda t, info: (chunk, 0, 0)),
            ]
            + [whole(w.shape) for w in weights],
            out_specs=[whole(out.shape)] * GRID,
            scratch_shapes=[pltpu.VMEM((count * cols, chans), BF16)],
        ),
        out_shape=[out] * GRID,
        compiler_params=params(),
        cost_estimate=cost(2 * count * cols * inner * chans, 1 << 22),
        name="project_rows",
    )(info, spatial, ordered, *weights)


def attend_kernel(pieces, info, gain, bias, *refs):
    refs = list(refs)
    take = lambda n: [refs.pop(0) for _ in range(n)]
    qkv_pieces, out_pieces, rest = take(1), take(1), take(pieces - 1)
    split = qkv_pieces[0].shape[1]
    for both in rest:
        qkv_pieces.append(both.at[:, :split])
        out_pieces.append(both.at[:, split:])
    tokens, outs = take(GRID), take(GRID)
    lned, triple, mixed, resid = refs
    count, size, chans = tokens[0].shape
    wins = size // GRID
    length = GRID * GRID
    group = min(256, chans)
    heads = group // HD
    keys = heads * length

    for a in range(count):
        rows = [tokens[k][a].astype(F32) for k in range(GRID)]
        for w in range(wins):
            x = jnp.concatenate([r[w * GRID : (w + 1) * GRID] for r in rows], axis=0)
            start = (a * wins + w) * length
            resid[start : start + length, :] = x
            center = jnp.mean(x, axis=-1, keepdims=True)
            off = x - center
            spread = jnp.mean(off * off, axis=-1, keepdims=True)
            lned[start : start + length, :] = (
                off * lax.rsqrt(spread + 1e-05) * gain[...] + bias[...]
            ).astype(BF16)

    def put_triple(start, width, product):
        triple[:, pl.ds(start, width)] = product.astype(BF16)

    pieced_dot(lned, qkv_pieces, info, put_triple)

    def same(shape, row_block, col_block):
        row = lax.broadcasted_iota(jnp.int32, shape, 0) // row_block
        col = lax.broadcasted_iota(jnp.int32, shape, 1) // col_block
        return jnp.where(row == col, 1.0, 0.0).astype(BF16)

    spread_mask = same((keys, group), length, HD)
    sum_mask = same((256, 256), length, length)
    factor = math.log2(math.e) / math.sqrt(HD)
    for win in range(count * wins):
        at = slice(win * length, (win + 1) * length)
        for g in range(chans // group):
            cols = slice(g * group, (g + 1) * group)
            query = triple[at, cols]
            key = triple[at, chans + g * group : chans + (g + 1) * group]
            value = triple[at, 2 * chans + g * group : 2 * chans + (g + 1) * group]
            key_wide = jnp.concatenate([key] * heads, axis=0) * spread_mask
            value_wide = jnp.concatenate([value] * heads, axis=0) * spread_mask
            scores = lax.dot_general(
                query, key_wide, (((1,), (1,)), ((), ())), preferred_element_type=F32
            )
            exponent = jnp.minimum(jnp.exp2(scores * factor), 3.3895e38)
            rounded = exponent.astype(BF16)
            sums = jnp.concatenate(
                [dot(rounded[:, n : n + 256], sum_mask) for n in range(0, keys, 256)], axis=1
            )
            soft = (exponent / sums).astype(BF16)
            mixed[at, cols] = dot(soft, value_wide).astype(BF16)

    def put_out(start, width, product):
        span = pl.ds(start, width)
        resid[:, span] = resid[:, span] + product

    pieced_dot(mixed, out_pieces, info, put_out)
    for a in range(count):
        for k in range(GRID):
            parts = []
            for w in range(wins):
                start = (a * wins + w) * length + k * GRID
                parts.append(resid[start : start + GRID, :])
            outs[k][a] = jnp.concatenate(parts, axis=0).astype(BF16)


def attend(info, tokens, gain, bias, w_qkv, w_out, rest):
    count, size, chans = tokens[0].shape
    total = count * size * GRID
    out = jax.ShapeDtypeStruct(tokens[0].shape, BF16)
    return pl.pallas_call(
        functools.partial(attend_kernel, 1 + len(rest)),
        out_shape=[out] * GRID,
        in_specs=[smem()] + [vmem()] * (4 + len(rest) + GRID),
        out_specs=[vmem()] * GRID,
        scratch_shapes=[
            pltpu.VMEM((total, chans), BF16),
            pltpu.VMEM((total, 3 * chans), BF16),
            pltpu.VMEM((total, chans), BF16),
            pltpu.VMEM((total, chans), F32),
        ],
        compiler_params=params(),
        cost_estimate=cost(16 * total * chans * chans, 1 << 22),
        name="attend",
    )(info, gain, bias, w_qkv, w_out, *rest, *tokens)


def restore_kernel(info, *refs):
    parts = refs[:GRID]
    out, buf = refs[-2:]
    count, cols, _ = out.shape
    size = parts[0].shape[1]
    back = one_hot_order(cols, inverse=True)
    mine = grid_of(info)
    for row in range(count):
        for k in range(GRID):
            at = pl.ds(row * cols + pl.multiple_of((mine ^ k) * size, size), size)
            buf[at, :] = parts[k][row]
        out[row] = dot(back, buf[row * cols : (row + 1) * cols, :]).astype(BF16)


def restore_rows(info, parts, rows, chunk, out):
    count, size, chans = parts[0].shape
    cols = size * GRID
    in_specs = [pl.BlockSpec((count, size, chans), lambda t, info: (0, 0, 0))] * GRID
    operands = [info, *parts]
    aliases = {}
    if out is not None:
        in_specs.append(pl.BlockSpec(memory_space=pl.ANY))
        aliases = {len(operands): 0}
        operands.append(out)
    return pl.pallas_call(
        restore_kernel,
        grid_spec=pltpu.PrefetchScalarGridSpec(
            num_scalar_prefetch=1,
            grid=(1,),
            in_specs=in_specs,
            out_specs=pl.BlockSpec((count, cols, chans), lambda t, info: (chunk, 0, 0)),
            scratch_shapes=[pltpu.VMEM((count * cols, chans), BF16)],
        ),
        out_shape=jax.ShapeDtypeStruct((rows, cols, chans), BF16),
        input_output_aliases=aliases,
        compiler_params=params(),
        cost_estimate=cost(2 * count * cols * cols * chans, 1 << 21),
        name="restore_rows",
    )(*operands)


def after(value, *others):
    return lax.optimization_barrier((value, *others))[0]


def local(
    fields,
    bn_scale,
    bn_shift,
    w_expand,
    expand_bias,
    dw_kernel,
    dw_bias,
    w_project,
    ln_gain,
    ln_bias,
    w_qkv,
    w_out,
):
    _, rows, cols, chans = fields.shape
    dp, space = lax.axis_size("dp"), lax.axis_size("space")
    dp_at, space_at = lax.axis_index("dp"), lax.axis_index("space")
    groups = space // GRID
    pairs = dp == 2 and space % 2 == 0
    info = jnp.stack(
        [
            jnp.asarray(v, jnp.int32)
            for v in (space_at % 2, dp_at, space_at, space - 1, groups)
        ]
    )
    as_row = lambda v: v.reshape(1, -1)
    image = fields.reshape(rows, cols, chans)
    small = (as_row(expand_bias), dw_kernel, as_row(dw_bias))
    gain, bias = as_row(ln_gain), as_row(ln_bias)

    over_dp = lambda w: lax.ppermute(w, "dp", [(0, 1), (1, 0)])
    over_core = lambda w: lax.ppermute(w, "space", [(i, i ^ 1) for i in range(space)])
    if pairs:
        mine = share_weights(info, w_expand, w_project, w_qkv, w_out)
        expand_got = over_dp(mine[0])
    above = lax.ppermute(image[rows - 1 :], "space", [(i, i + 1) for i in range(space - 1)])
    below = lax.ppermute(image[:1], "space", [(i + 1, i) for i in range(space - 1)])
    sources = (image, above, below, as_row(bn_scale), as_row(bn_shift))
    if pairs:
        project_got = over_dp(mine[1])
        rest_got = over_dp(mine[2])
        tiles = max(1, w_expand.shape[1] // 256)
        spatial, ordered, normed = expand_some(
            info, sources, w_expand, *small, lambda i, t: i[DP] * tiles + t, None
        )
        half = tiles // 2
        expand_got = after(expand_got, spatial)
        expand_other = over_core(expand_got)
        (spatial,) = expand_some(
            info,
            (normed,),
            expand_got,
            *small,
            lambda i, t: (1 - i[DP]) * tiles + i[CORE] * half + t,
            (spatial, rows, cols),
        )
        (spatial,) = expand_some(
            info,
            (normed,),
            expand_other,
            *small,
            lambda i, t: (1 - i[DP]) * tiles + (1 - i[CORE]) * half + t,
            (spatial, rows, cols),
        )
        project_got = after(project_got, expand_other)
        project_all = [w_project, project_got, over_core(project_got)]
    else:
        gathered = lambda w: lax.all_gather(w, "dp", axis=1, tiled=True)
        spatial, ordered, normed = expand_some(
            info, sources, gathered(w_expand), *small, lambda i, t: t, None
        )
        project_all = [gathered(w_project)]
        w_qkv, w_out, rest = gathered(w_qkv), gathered(w_out), []

    count = rows // CHUNKS
    swaps = [
        [(s, (((s // groups) ^ k) * groups) + s % groups) for s in range(space)]
        for k in range(GRID)
    ]
    order = (4, 6, 5, 7, 2, 3, 1)

    def exchange(parts):
        parts = list(parts)
        for k in order:
            parts[k] = lax.ppermute(parts[k], "space", swaps[k])
        return parts

    sent = []
    for chunk in range(CHUNKS):
        sent.append(
            exchange(project_rows(info, spatial, ordered, project_all, chunk, count))
        )
    if pairs:
        rest_got = after(rest_got, spatial)
        rest = [rest_got, over_core(rest_got)]
    back = [exchange(attend(info, parts, gain, bias, w_qkv, w_out, rest)) for parts in sent]
    result = None
    for chunk in range(CHUNKS):
        result = restore_rows(info, back[chunk], rows, chunk, result)
    return result.reshape(fields.shape)


def solution(mesh):
    in_specs = (
        P("dp", "space", None, None),
        P(),
        P(),
        P(None, "dp"),
        P(),
        P(),
        P(),
        P(None, "dp"),
        P(),
        P(),
        P(None, "dp"),
        P(None, "dp"),
    )
    out_specs = P("dp", "space", None, None)
    return jax.shard_map(local, mesh=mesh, in_specs=in_specs, out_specs=out_specs, check_vma=False)
```

time: 157 us -> 120 us (0.76)
  Pallas kernels: 59.6 us -> 39.4 us
  waiting for transfers between devices: 29.4 us -> 14.4 us
    ppermute x10 -> x8, waiting for transfers between devices: 23.9 us -> 6.18 us  [the longest x3 5.3 us: local(): over_dp = lambda w: lax.ppermute(w, 'dp', [(0, 1), (1, 0)])]
    pallas_call x7 -> x8, Pallas kernels: 47.7 us -> 35.6 us  [the longest x3 15.9 us: expand_some(): pl.pallas_call(functools.partial(expand_kernel, first), grid_spec=pltpu.P...]
    pallas_call x2, Pallas kernels: 11.9 us -> 3.74 us  [project_rows(): pl.pallas_call(functools.partial(project_kernel, len(weights)), grid_spec...]
    unnamed x82 -> x30, local copies, waits for them, and re-layouts: 3 us -> 9.43 us
    dynamic_slice x4 -> x0, local copies, waits for them, and re-layouts: 4.2 us -> none  [fetch(): mine = lax.dynamic_slice_in_dim(weight, core * part, part, axis=0)]
    ppermute x28, waiting for transfers between devices: 5.52 us -> 8.24 us  [exchange(): parts[k] = lax.ppermute(parts[k], 'space', swaps[k])]
    another operation x4 -> x1, local copies, waits for them, and re-layouts: 1.9 us -> 0.08 us  [local(): jnp.stack([jnp.asarray(v, jnp.int32) for v in (space_at % 2, dp_at, space...]
    ppermute x10 -> x8, starting transfers between devices: 11.7 us -> 10.2 us  [the longest x3 3.61 us: local(): over_dp = lambda w: lax.ppermute(w, 'dp', [(0, 1), (1, 0)])]
  transfers between devices with their start and end apart: 38 -> 36, of which waited for: 6 -> 7; matrix products, arithmetic and copies ran while one was open for 4% -> 1% of each run, Pallas kernels for 36% -> 31%
where the time goes in v2:
time: 120 us; the launch traced here: 119 us
  starting transfers between devices  54.5 us (45%)
  Pallas kernels  39.4 us (33%)
  waiting for transfers between devices  14.4 us (12%)
  local copies, waits for them, and re-layouts  10.5 us (9%)
    ppermute x28, starting transfers between devices, exchange(): parts[k] = lax.ppermute(parts[k], 'space', swaps[k])  44.4 us
    pallas_call x3, Pallas kernels, expand_some(): pl.pallas_call(functools.partial(expand_kernel, first), grid_spec=pltpu.P...  15.9 us
    pallas_call x2, Pallas kernels, attend(): pl.pallas_call(functools.partial(attend_kernel, 1 + len(rest)), out_shape...  15.8 us
    unnamed x30, local copies, waits for them, and re-layouts  9.43 us
    ppermute x28, waiting for transfers between devices, exchange(): parts[k] = lax.ppermute(parts[k], 'space', swaps[k])  8.24 us
    ppermute x3, waiting for transfers between devices, local(): over_dp = lambda w: lax.ppermute(w, 'dp', [(0, 1), (1, 0)])  5.3 us
    pallas_call x2, Pallas kernels, project_rows(): pl.pallas_call(functools.partial(project_kernel, len(weights)), grid_spec...  3.74 us
    ppermute x3, starting transfers between devices, local(): over_dp = lambda w: lax.ppermute(w, 'dp', [(0, 1), (1, 0)])  3.61 us
  transfers between devices with their start and end apart: 36, of which 7 were waited for; matrix products, arithmetic and copies ran while one was open for 1% of the time, Pallas kernels for 31%

profile of v2, /device:TPU:0, one launch (start us, length us, event | category | flops | bytes accessed | tf_op | source)
XLA Modules:
  0.0 119.1 jit_solution(17060167238582629228)
XLA Ops:
  5.3 3.0 %collective-permute-start.3 = (bf16[512,512]{1,0:T(8,128)(2,1)S(1)}, bf16[512,512]{1,0:T(8,128)(2,1)S(1)}, u32[]{:S(2)}, u32[]{:S(2)}) collective-permute-start(bf16[512,512]{1,0:T(8,128)(2,1)S(1)} %get-tuple-element.48), channel_id=1, source_target_pairs={{0,16},{16,0},{1,17},{17,1},{2,18},{18,2},{3,19},{19,3},{4,20},{20... | collective-permute-start | bytes 1572872 | tf_op jit(solution)/shard_map/ppermute | solution.py:451
  10.6 3.0 %collective-permute-start.1 = (bf16[1,128,512]{2,1,0:T(8,128)(2,1)S(1)}, bf16[1,128,512]{2,1,0:T(8,128)(2,1)S(1)}, u32[]{:S(2)}, u32[]{:S(2)}) collective-permute-start(bf16[1,128,512]{2,1,0:T(8,128)(2,1)S(1)} %get-tuple-element.88), channel_id=1, source_target_pairs={{0,1},{1,2},{2,3},{3,4},{4,5},{5,6},{6,7},{7,8},{8,9},{9,10},{10,1... | collective-permute-start | bytes 393224 | tf_op jit(solution)/shard_map/ppermute | solution.py:456
  19.5 7.9 %expand_conv.3 = (bf16[1024,2048]{1,0:T(8,128)(2,1)S(1)}, bf16[8,128,512]{2,1,0:T(8,128)(2,1)S(1)}, bf16[1280,512]{1,0:T(8,128)(2,1)S(1)}) custom-call(s32[5]{0:T(128)S(1)} %stack.15.info, bf16[8,128,512]{2,1,0:T(8,128)(2,1)S(1)} %bitcast.15, bf16[1,128,512]{2,1,0:T(8,128)(2,1)S(1)} %collective-permute-done.1.refs_1_, ...), custom_call_target="tpu_custom_call" | custom-call | flops 1073741824 | bytes 4194304 | tf_op jit(solution)/shard_map/expand_conv/pallas_call | solution.py:193
  27.4 2.2 %collective-permute-start.4 = (bf16[512,512]{1,0:T(8,128)(2,1)S(1)}, bf16[512,512]{1,0:T(8,128)(2,1)S(1)}, u32[]{:S(2)}, u32[]{:S(2)}) collective-permute-start(bf16[512,512]{1,0:T(8,128)(2,1)S(1)} %collective-permute-done.3.refs_1_), channel_id=1, source_target_pairs={{0,1},{1,0},{2,3},{3,2},{4,5},{5,4},{6,7},{7,6},{8,9},{9,8},{10,11... | collective-permute-start | bytes 1572872 | tf_op jit(solution)/shard_map/ppermute | solution.py:452
  31.5 3.9 %expand_conv.4.refs_5_ = bf16[1024,2048]{1,0:T(8,128)(2,1)S(1)} custom-call(s32[5]{0:T(128)S(1)} %stack.15.info, bf16[1280,512]{1,0:T(8,128)(2,1)S(1)} %get-tuple-element.47.refs_0_, bf16[512,512]{1,0:T(8,128)(2,1)S(1)} %collective-permute-done.3.refs_1_, f32[1,2048]{1,0:T(1,128)S(1)} %bitcast.17, ...), custom_call_target="tpu_custom_call", output_to_operand_aliasing={{}: (6, {})} | custom-call | flops 536870912 | bytes 4194304 | tf_op jit(solution)/shard_map/expand_conv/pallas_call | solution.py:193
  35.4 4.1 %expand_conv.5.spatial = bf16[1024,2048]{1,0:T(8,128)(2,1)S(1)} custom-call(s32[5]{0:T(128)S(1)} %stack.15.info, bf16[1280,512]{1,0:T(8,128)(2,1)S(1)} %get-tuple-element.47.refs_0_, bf16[512,512]{1,0:T(8,128)(2,1)S(1)} %collective-permute-done.4.refs_1_, f32[1,2048]{1,0:T(1,128)S(1)} %bitcast.18, ...), custom_call_target="tpu_custom_call", output_to_operand_aliasing={{}: (6, {})} | custom-call | flops 536870912 | bytes 4194304 | tf_op jit(solution)/shard_map/expand_conv/pallas_call | solution.py:193
  39.6 3.9 %collective-permute-done.refs_2_ = bf16[256,1024]{1,0:T(8,128)(2,1)S(1)} collective-permute-done((bf16[256,1024]{1,0:T(8,128)(2,1)S(1)}, bf16[256,1024]{1,0:T(8,128)(2,1)S(1)}, u32[]{:S(2)}, u32[]{:S(2)}) %collective-permute-start) | collective-permute-done | bytes 524320 | tf_op jit(solution)/shard_map/ppermute | solution.py:451
  43.5 1.9 %project_rows.3 = (bf16[4,16,512]{2,1,0:T(8,128)(2,1)S(1)}, bf16[4,16,512]{2,1,0:T(8,128)(2,1)S(1)}, bf16[4,16,512]{2,1,0:T(8,128)(2,1)S(1)}, bf16[4,16,512]{2,1...) custom-call(s32[5]{0:T(128)S(1)} %stack.15.info, ...), custom_call_target="tpu_custom_call" | custom-call | flops 1073741824 | bytes 4194304 | tf_op jit(solution)/shard_map/project_rows/pallas_call | solution.py:258
  45.4 2.9 %collective-permute-start.22 = (bf16[4,16,512]{2,1,0:T(8,128)(2,1)S(1)}, bf16[4,16,512]{2,1,0:T(8,128)(2,1)S(1)}, u32[]{:S(2)}, u32[]{:S(2)}) collective-permute-start(bf16[4,16,512]{2,1,0:T(8,128)(2,1)S(1)} %get-tuple-element.72), channel_id=1, source_target_pairs={{0,2},{1,3},{2,0},{3,1},{4,6},{5,7},{6,4},{7,5},{8,10},{9,11},{10,... | collective-permute-start | bytes 196616 | tf_op jit(solution)/shard_map/ppermute | solution.py:505
  48.3 1.6 %collective-permute-start.23 = (bf16[4,16,512]{2,1,0:T(8,128)(2,1)S(1)}, bf16[4,16,512]{2,1,0:T(8,128)(2,1)S(1)}, u32[]{:S(2)}, u32[]{:S(2)}) collective-permute-start(bf16[4,16,512]{2,1,0:T(8,128)(2,1)S(1)} %get-tuple-element.73), channel_id=1, source_target_pairs={{0,4},{1,5},{2,6},{3,7},{4,0},{5,1},{6,2},{7,3},{8,12},{9,13},{10,... | collective-permute-start | bytes 196616 | tf_op jit(solution)/shard_map/ppermute | solution.py:505
  51.2 3.0 %collective-permute-start.25 = (bf16[4,16,512]{2,1,0:T(8,128)(2,1)S(1)}, bf16[4,16,512]{2,1,0:T(8,128)(2,1)S(1)}, u32[]{:S(2)}, u32[]{:S(2)}) collective-permute-start(bf16[4,16,512]{2,1,0:T(8,128)(2,1)S(1)} %get-tuple-element.75), channel_id=1, source_target_pairs={{0,8},{1,9},{2,10},{3,11},{4,12},{5,13},{6,14},{7,15},{8,0},{9,1},... | collective-permute-start | bytes 196616 | tf_op jit(solution)/shard_map/ppermute | solution.py:505
  54.2 1.9 %project_rows.2 = (bf16[4,16,512]{2,1,0:T(8,128)(2,1)S(1)}, bf16[4,16,512]{2,1,0:T(8,128)(2,1)S(1)}, bf16[4,16,512]{2,1,0:T(8,128)(2,1)S(1)}, bf16[4,16,512]{2,1...) custom-call(s32[5]{0:T(128)S(1)} %stack.15.info, ...), custom_call_target="tpu_custom_call" | custom-call | flops 1073741824 | bytes 4194304 | tf_op jit(solution)/shard_map/project_rows/pallas_call | solution.py:258
  56.2 3.4 %collective-permute-start.27 = (bf16[4,16,512]{2,1,0:T(8,128)(2,1)S(1)}, bf16[4,16,512]{2,1,0:T(8,128)(2,1)S(1)}, u32[]{:S(2)}, u32[]{:S(2)}) collective-permute-start(bf16[4,16,512]{2,1,0:T(8,128)(2,1)S(1)} %get-tuple-element.77), channel_id=1, source_target_pairs={{0,12},{1,13},{2,14},{3,15},{4,8},{5,9},{6,10},{7,11},{8,4},{9,5},... | collective-permute-start | bytes 196616 | tf_op jit(solution)/shard_map/ppermute | solution.py:505
  61.6 4.6 %collective-permute-done.26.refs_9_ = bf16[4,16,512]{2,1,0:T(8,128)(2,1)S(1)} collective-permute-done((bf16[4,16,512]{2,1,0:T(8,128)(2,1)S(1)}, bf16[4,16,512]{2,1,0:T(8,128)(2,1)S(1)}, u32[]{:S(2)}, u32[]{:S(2)}) %collective-permute-start.26) | collective-permute-done | bytes 65568 | tf_op jit(solution)/shard_map/ppermute | solution.py:505
  66.2 2.1 %collective-permute-start.11 = (bf16[4,16,512]{2,1,0:T(8,128)(2,1)S(1)}, bf16[4,16,512]{2,1,0:T(8,128)(2,1)S(1)}, u32[]{:S(2)}, u32[]{:S(2)}) collective-permute-start(bf16[4,16,512]{2,1,0:T(8,128)(2,1)S(1)} %get-tuple-element.59), channel_id=1, source_target_pairs={{0,8},{1,9},{2,10},{3,11},{4,12},{5,13},{6,14},{7,15},{8,0},{9,1},... | collective-permute-start | bytes 196616 | tf_op jit(solution)/shard_map/ppermute | solution.py:505
  68.3 1.6 %collective-permute-start.12 = (bf16[4,16,512]{2,1,0:T(8,128)(2,1)S(1)}, bf16[4,16,512]{2,1,0:T(8,128)(2,1)S(1)}, u32[]{:S(2)}, u32[]{:S(2)}) collective-permute-start(bf16[4,16,512]{2,1,0:T(8,128)(2,1)S(1)} %get-tuple-element.60), channel_id=1, source_target_pairs={{0,10},{1,11},{2,8},{3,9},{4,14},{5,15},{6,12},{7,13},{8,2},{9,3},... | collective-permute-start | bytes 196616 | tf_op jit(solution)/shard_map/ppermute | solution.py:505
  69.9 1.7 %collective-permute-start.13 = (bf16[4,16,512]{2,1,0:T(8,128)(2,1)S(1)}, bf16[4,16,512]{2,1,0:T(8,128)(2,1)S(1)}, u32[]{:S(2)}, u32[]{:S(2)}) collective-permute-start(bf16[4,16,512]{2,1,0:T(8,128)(2,1)S(1)} %get-tuple-element.61), channel_id=1, source_target_pairs={{0,12},{1,13},{2,14},{3,15},{4,8},{5,9},{6,10},{7,11},{8,4},{9,5},... | collective-permute-start | bytes 196616 | tf_op jit(solution)/shard_map/ppermute | solution.py:505
  71.6 2.6 %collective-permute-start.14 = (bf16[4,16,512]{2,1,0:T(8,128)(2,1)S(1)}, bf16[4,16,512]{2,1,0:T(8,128)(2,1)S(1)}, u32[]{:S(2)}, u32[]{:S(2)}) collective-permute-start(bf16[4,16,512]{2,1,0:T(8,128)(2,1)S(1)} %get-tuple-element.62), channel_id=1, source_target_pairs={{0,14},{1,15},{2,12},{3,13},{4,10},{5,11},{6,8},{7,9},{8,6},{9,7},... | collective-permute-start | bytes 196616 | tf_op jit(solution)/shard_map/ppermute | solution.py:505
  74.2 7.9 %attend.3 = (bf16[4,16,512]{2,1,0:T(8,128)(2,1)S(1)}, bf16[4,16,512]{2,1,0:T(8,128)(2,1)S(1)}, bf16[4,16,512]{2,1,0:T(8,128)(2,1)S(1)}, bf16[4,16,512]{2,1,0:T(8...) custom-call(s32[5]{0:T(128)S(1)} %stack.15.info, ...), custom_call_target="tpu_custom_call" | custom-call | flops 2147483648 | bytes 4194304 | tf_op jit(solution)/shard_map/attend/pallas_call | solution.py:359
  83.6 2.1 %collective-permute-start.31 = (bf16[4,16,512]{2,1,0:T(8,128)(2,1)S(1)}, bf16[4,16,512]{2,1,0:T(8,128)(2,1)S(1)}, u32[]{:S(2)}, u32[]{:S(2)}) collective-permute-start(bf16[4,16,512]{2,1,0:T(8,128)(2,1)S(1)} %get-tuple-element.82), channel_id=1, source_target_pairs={{0,6},{1,7},{2,4},{3,5},{4,2},{5,3},{6,0},{7,1},{8,14},{9,15},{10,... | collective-permute-start | bytes 196616 | tf_op jit(solution)/shard_map/ppermute | solution.py:505
  85.7 1.8 %collective-permute-start.32 = (bf16[4,16,512]{2,1,0:T(8,128)(2,1)S(1)}, bf16[4,16,512]{2,1,0:T(8,128)(2,1)S(1)}, u32[]{:S(2)}, u32[]{:S(2)}) collective-permute-start(bf16[4,16,512]{2,1,0:T(8,128)(2,1)S(1)} %get-tuple-element.83), channel_id=1, source_target_pairs={{0,8},{1,9},{2,10},{3,11},{4,12},{5,13},{6,14},{7,15},{8,0},{9,1},... | collective-permute-start | bytes 196616 | tf_op jit(solution)/shard_map/ppermute | solution.py:505
  87.5 1.5 %collective-permute-start.33 = (bf16[4,16,512]{2,1,0:T(8,128)(2,1)S(1)}, bf16[4,16,512]{2,1,0:T(8,128)(2,1)S(1)}, u32[]{:S(2)}, u32[]{:S(2)}) collective-permute-start(bf16[4,16,512]{2,1,0:T(8,128)(2,1)S(1)} %get-tuple-element.84), channel_id=1, source_target_pairs={{0,10},{1,11},{2,8},{3,9},{4,14},{5,15},{6,12},{7,13},{8,2},{9,3},... | collective-permute-start | bytes 196616 | tf_op jit(solution)/shard_map/ppermute | solution.py:505
  89.0 7.9 %attend.2 = (bf16[4,16,512]{2,1,0:T(8,128)(2,1)S(1)}, bf16[4,16,512]{2,1,0:T(8,128)(2,1)S(1)}, bf16[4,16,512]{2,1,0:T(8,128)(2,1)S(1)}, bf16[4,16,512]{2,1,0:T(8...) custom-call(s32[5]{0:T(128)S(1)} %stack.15.info, ...), custom_call_target="tpu_custom_call" | custom-call | flops 2147483648 | bytes 4194304 | tf_op jit(solution)/shard_map/attend/pallas_call | solution.py:359
  96.9 2.4 %collective-permute-start.34 = (bf16[4,16,512]{2,1,0:T(8,128)(2,1)S(1)}, bf16[4,16,512]{2,1,0:T(8,128)(2,1)S(1)}, u32[]{:S(2)}, u32[]{:S(2)}) collective-permute-start(bf16[4,16,512]{2,1,0:T(8,128)(2,1)S(1)} %get-tuple-element.85), channel_id=1, source_target_pairs={{0,12},{1,13},{2,14},{3,15},{4,8},{5,9},{6,10},{7,11},{8,4},{9,5},... | collective-permute-start | bytes 196616 | tf_op jit(solution)/shard_map/ppermute | solution.py:505
  99.3 2.0 %collective-permute-start.35 = (bf16[4,16,512]{2,1,0:T(8,128)(2,1)S(1)}, bf16[4,16,512]{2,1,0:T(8,128)(2,1)S(1)}, u32[]{:S(2)}, u32[]{:S(2)}) collective-permute-start(bf16[4,16,512]{2,1,0:T(8,128)(2,1)S(1)} %get-tuple-element.86), channel_id=1, source_target_pairs={{0,14},{1,15},{2,12},{3,13},{4,10},{5,11},{6,8},{7,9},{8,6},{9,7},... | collective-permute-start | bytes 196616 | tf_op jit(solution)/shard_map/ppermute | solution.py:505
  102.3 2.5 %collective-permute-start.17 = (bf16[4,16,512]{2,1,0:T(8,128)(2,1)S(1)}, bf16[4,16,512]{2,1,0:T(8,128)(2,1)S(1)}, u32[]{:S(2)}, u32[]{:S(2)}) collective-permute-start(bf16[4,16,512]{2,1,0:T(8,128)(2,1)S(1)} %get-tuple-element.66), channel_id=1, source_target_pairs={{0,6},{1,7},{2,4},{3,5},{4,2},{5,3},{6,0},{7,1},{8,14},{9,15},{10,... | collective-permute-start | bytes 196616 | tf_op jit(solution)/shard_map/ppermute | solution.py:505
  104.8 1.8 %collective-permute-start.18 = (bf16[4,16,512]{2,1,0:T(8,128)(2,1)S(1)}, bf16[4,16,512]{2,1,0:T(8,128)(2,1)S(1)}, u32[]{:S(2)}, u32[]{:S(2)}) collective-permute-start(bf16[4,16,512]{2,1,0:T(8,128)(2,1)S(1)} %get-tuple-element.67), channel_id=1, source_target_pairs={{0,8},{1,9},{2,10},{3,11},{4,12},{5,13},{6,14},{7,15},{8,0},{9,1},... | collective-permute-start | bytes 196616 | tf_op jit(solution)/shard_map/ppermute | solution.py:505
  108.1 2.3 %collective-permute-start.20 = (bf16[4,16,512]{2,1,0:T(8,128)(2,1)S(1)}, bf16[4,16,512]{2,1,0:T(8,128)(2,1)S(1)}, u32[]{:S(2)}, u32[]{:S(2)}) collective-permute-start(bf16[4,16,512]{2,1,0:T(8,128)(2,1)S(1)} %get-tuple-element.69), channel_id=1, source_target_pairs={{0,12},{1,13},{2,14},{3,15},{4,8},{5,9},{6,10},{7,11},{8,4},{9,5},... | collective-permute-start | bytes 196616 | tf_op jit(solution)/shard_map/ppermute | solution.py:505
  110.4 2.0 %collective-permute-start.21 = (bf16[4,16,512]{2,1,0:T(8,128)(2,1)S(1)}, bf16[4,16,512]{2,1,0:T(8,128)(2,1)S(1)}, u32[]{:S(2)}, u32[]{:S(2)}) collective-permute-start(bf16[4,16,512]{2,1,0:T(8,128)(2,1)S(1)} %get-tuple-element.70), channel_id=1, source_target_pairs={{0,14},{1,15},{2,12},{3,13},{4,10},{5,11},{6,8},{7,9},{8,6},{9,7},... | collective-permute-start | bytes 196616 | tf_op jit(solution)/shard_map/ppermute | solution.py:505
  112.5 1.6 %restore_rows.2.refs_8_ = bf16[8,128,512]{2,1,0:T(8,128)(2,1)} custom-call(s32[5]{0:T(128)S(1)} %stack.15.info, bf16[4,16,512]{2,1,0:T(8,128)(2,1)S(1)} %get-tuple-element.79.refs_0_, bf16[4,16,512]{2,1,0:T(8,128)(2,1)S(1)} %collective-permute-done.29.refs_1_, bf16[4,16,512]{2,1,0:T(8,128)(2,1)S(1)} %collective-permute-done.30.refs_2_, ...), custom_call_target="tpu_custom_call" | custom-call | flops 67108864 | bytes 2097152 | tf_op jit(solution)/shard_map/restore_rows/pallas_call | solution.py:400
  114.3 3.1 %collective-permute-done.21.refs_7_ = bf16[4,16,512]{2,1,0:T(8,128)(2,1)S(1)} collective-permute-done((bf16[4,16,512]{2,1,0:T(8,128)(2,1)S(1)}, bf16[4,16,512]{2,1,0:T(8,128)(2,1)S(1)}, u32[]{:S(2)}, u32[]{:S(2)}) %collective-permute-start.21) | collective-permute-done | bytes 65568 | tf_op jit(solution)/shard_map/ppermute | solution.py:505
  117.4 1.6 %restore_rows.3 = bf16[8,128,512]{2,1,0:T(8,128)(2,1)} custom-call(s32[5]{0:T(128)S(1)} %stack.15.info, bf16[4,16,512]{2,1,0:T(8,128)(2,1)S(1)} %get-tuple-element.63.refs_0_, bf16[4,16,512]{2,1,0:T(8,128)(2,1)S(1)} %collective-permute-done.15.refs_1_, bf16[4,16,512]{2,1,0:T(8,128)(2,1)S(1)} %collective-permute-done.16.refs_2_, ...), custom_call_target="tpu_custom_call", output_to_operand_aliasing={{}: (9, {})} | custom-call | flops 67108864 | bytes 2097152 | tf_op jit(solution)/shard_map/restore_rows/pallas_call | solution.py:400
  (82 shorter events, 22.8 us)
Async XLA Ops:
  5.3 22.1 %collective-permute-start.3 = (bf16[512,512]{1,0:T(8,128)(2,1)S(1)}, bf16[512,512]{1,0:T(8,128)(2,1)S(1)}, u32[]{:S(2)}, u32[]{:S(2)}) collective-permute-start(bf16[512,512]{1,0:T(8,128)(2,1)S(1)} %get-tuple-element.48), channel_id=1, source_target_pairs={{0,16},{16,0},{1,17},{17,1},{2,18},{18,2},{3,19},{19,3},{4,20},{20... | collective-permute-start | bytes 1572872 | tf_op jit(solution)/shard_map/ppermute | solution.py:451
  13.6 17.8 %collective-permute-start.6 = (bf16[1024,256]{1,0:T(8,128)(2,1)S(1)}, bf16[1024,256]{1,0:T(8,128)(2,1)S(1)}, u32[]{:S(2)}, u32[]{:S(2)}) collective-permute-start(bf16[1024,256]{1,0:T(8,128)(2,1)S(1)} %get-tuple-element.53), channel_id=1, source_target_pairs={{0,16},{16,0},{1,17},{17,1},{2,18},{18,2},{3,19},{19,3},{4,20},{20... | collective-permute-start | bytes 1572872 | tf_op jit(solution)/shard_map/ppermute | solution.py:451
  29.6 13.9 %collective-permute-start = (bf16[256,1024]{1,0:T(8,128)(2,1)S(1)}, bf16[256,1024]{1,0:T(8,128)(2,1)S(1)}, u32[]{:S(2)}, u32[]{:S(2)}) collective-permute-start(bf16[256,1024]{1,0:T(8,128)(2,1)S(1)} %get-tuple-element.46), channel_id=1, source_target_pairs={{0,16},{16,0},{1,17},{17,1},{2,18},{18,2},{3,19},{19,3},{4,20},{20... | collective-permute-start | bytes 1572872 | tf_op jit(solution)/shard_map/ppermute | solution.py:451
  31.5 12.0 %collective-permute-start.7 = (bf16[1024,256]{1,0:T(8,128)(2,1)S(1)}, bf16[1024,256]{1,0:T(8,128)(2,1)S(1)}, u32[]{:S(2)}, u32[]{:S(2)}) collective-permute-start(bf16[1024,256]{1,0:T(8,128)(2,1)S(1)} %collective-permute-done.6.refs_1_), channel_id=1, source_target_pairs={{0,1},{1,0},{2,3},{3,2},{4,5},{5,4},{6,7},{7,6},{8,9},{9,8},{10,11... | collective-permute-start | bytes 1572872 | tf_op jit(solution)/shard_map/ppermute | solution.py:452
  43.5 12.6 %collective-permute-start.5 = (bf16[256,1024]{1,0:T(8,128)(2,1)S(1)}, bf16[256,1024]{1,0:T(8,128)(2,1)S(1)}, u32[]{:S(2)}, u32[]{:S(2)}) collective-permute-start(bf16[256,1024]{1,0:T(8,128)(2,1)S(1)} %collective-permute-done.refs_2_), channel_id=1, source_target_pairs={{0,1},{1,0},{2,3},{3,2},{4,5},{5,4},{6,7},{7,6},{8,9},{9,8},{10,11... | collective-permute-start | bytes 1572872 | tf_op jit(solution)/shard_map/ppermute | solution.py:452
  45.4 10.7 %collective-permute-start.22 = (bf16[4,16,512]{2,1,0:T(8,128)(2,1)S(1)}, bf16[4,16,512]{2,1,0:T(8,128)(2,1)S(1)}, u32[]{:S(2)}, u32[]{:S(2)}) collective-permute-start(bf16[4,16,512]{2,1,0:T(8,128)(2,1)S(1)} %get-tuple-element.72), channel_id=1, source_target_pairs={{0,2},{1,3},{2,0},{3,1},{4,6},{5,7},{6,4},{7,5},{8,10},{9,11},{10,... | collective-permute-start | bytes 196616 | tf_op jit(solution)/shard_map/ppermute | solution.py:505
  48.3 11.3 %collective-permute-start.23 = (bf16[4,16,512]{2,1,0:T(8,128)(2,1)S(1)}, bf16[4,16,512]{2,1,0:T(8,128)(2,1)S(1)}, u32[]{:S(2)}, u32[]{:S(2)}) collective-permute-start(bf16[4,16,512]{2,1,0:T(8,128)(2,1)S(1)} %get-tuple-element.73), channel_id=1, source_target_pairs={{0,4},{1,5},{2,6},{3,7},{4,0},{5,1},{6,2},{7,3},{8,12},{9,13},{10,... | collective-permute-start | bytes 196616 | tf_op jit(solution)/shard_map/ppermute | solution.py:505
  49.9 11.2 %collective-permute-start.24 = (bf16[4,16,512]{2,1,0:T(8,128)(2,1)S(1)}, bf16[4,16,512]{2,1,0:T(8,128)(2,1)S(1)}, u32[]{:S(2)}, u32[]{:S(2)}) collective-permute-start(bf16[4,16,512]{2,1,0:T(8,128)(2,1)S(1)} %get-tuple-element.74), channel_id=1, source_target_pairs={{0,6},{1,7},{2,4},{3,5},{4,2},{5,3},{6,0},{7,1},{8,14},{9,15},{10,... | collective-permute-start | bytes 196616 | tf_op jit(solution)/shard_map/ppermute | solution.py:505
  51.2 10.5 %collective-permute-start.25 = (bf16[4,16,512]{2,1,0:T(8,128)(2,1)S(1)}, bf16[4,16,512]{2,1,0:T(8,128)(2,1)S(1)}, u32[]{:S(2)}, u32[]{:S(2)}) collective-permute-start(bf16[4,16,512]{2,1,0:T(8,128)(2,1)S(1)} %get-tuple-element.75), channel_id=1, source_target_pairs={{0,8},{1,9},{2,10},{3,11},{4,12},{5,13},{6,14},{7,15},{8,0},{9,1},... | collective-permute-start | bytes 196616 | tf_op jit(solution)/shard_map/ppermute | solution.py:505
  56.1 10.1 %collective-permute-start.26 = (bf16[4,16,512]{2,1,0:T(8,128)(2,1)S(1)}, bf16[4,16,512]{2,1,0:T(8,128)(2,1)S(1)}, u32[]{:S(2)}, u32[]{:S(2)}) collective-permute-start(bf16[4,16,512]{2,1,0:T(8,128)(2,1)S(1)} %get-tuple-element.76), channel_id=1, source_target_pairs={{0,10},{1,11},{2,8},{3,9},{4,14},{5,15},{6,12},{7,13},{8,2},{9,3},... | collective-permute-start | bytes 196616 | tf_op jit(solution)/shard_map/ppermute | solution.py:505
  56.2 10.1 %collective-permute-start.27 = (bf16[4,16,512]{2,1,0:T(8,128)(2,1)S(1)}, bf16[4,16,512]{2,1,0:T(8,128)(2,1)S(1)}, u32[]{:S(2)}, u32[]{:S(2)}) collective-permute-start(bf16[4,16,512]{2,1,0:T(8,128)(2,1)S(1)} %get-tuple-element.77), channel_id=1, source_target_pairs={{0,12},{1,13},{2,14},{3,15},{4,8},{5,9},{6,10},{7,11},{8,4},{9,5},... | collective-permute-start | bytes 196616 | tf_op jit(solution)/shard_map/ppermute | solution.py:505
  59.6 8.7 %collective-permute-start.28 = (bf16[4,16,512]{2,1,0:T(8,128)(2,1)S(1)}, bf16[4,16,512]{2,1,0:T(8,128)(2,1)S(1)}, u32[]{:S(2)}, u32[]{:S(2)}) collective-permute-start(bf16[4,16,512]{2,1,0:T(8,128)(2,1)S(1)} %get-tuple-element.78), channel_id=1, source_target_pairs={{0,14},{1,15},{2,12},{3,13},{4,10},{5,11},{6,8},{7,9},{8,6},{9,7},... | collective-permute-start | bytes 196616 | tf_op jit(solution)/shard_map/ppermute | solution.py:505
  61.1 8.8 %collective-permute-start.8 = (bf16[4,16,512]{2,1,0:T(8,128)(2,1)S(1)}, bf16[4,16,512]{2,1,0:T(8,128)(2,1)S(1)}, u32[]{:S(2)}, u32[]{:S(2)}) collective-permute-start(bf16[4,16,512]{2,1,0:T(8,128)(2,1)S(1)} %get-tuple-element.56), channel_id=1, source_target_pairs={{0,2},{1,3},{2,0},{3,1},{4,6},{5,7},{6,4},{7,5},{8,10},{9,11},{10,... | collective-permute-start | bytes 196616 | tf_op jit(solution)/shard_map/ppermute | solution.py:505
  61.6 10.0 %collective-permute-start.9 = (bf16[4,16,512]{2,1,0:T(8,128)(2,1)S(1)}, bf16[4,16,512]{2,1,0:T(8,128)(2,1)S(1)}, u32[]{:S(2)}, u32[]{:S(2)}) collective-permute-start(bf16[4,16,512]{2,1,0:T(8,128)(2,1)S(1)} %get-tuple-element.57), channel_id=1, source_target_pairs={{0,4},{1,5},{2,6},{3,7},{4,0},{5,1},{6,2},{7,3},{8,12},{9,13},{10,... | collective-permute-start | bytes 196616 | tf_op jit(solution)/shard_map/ppermute | solution.py:505
  66.2 15.9 %collective-permute-start.10 = (bf16[4,16,512]{2,1,0:T(8,128)(2,1)S(1)}, bf16[4,16,512]{2,1,0:T(8,128)(2,1)S(1)}, u32[]{:S(2)}, u32[]{:S(2)}) collective-permute-start(bf16[4,16,512]{2,1,0:T(8,128)(2,1)S(1)} %get-tuple-element.58), channel_id=1, source_target_pairs={{0,6},{1,7},{2,4},{3,5},{4,2},{5,3},{6,0},{7,1},{8,14},{9,15},{10,... | collective-permute-start | bytes 196616 | tf_op jit(solution)/shard_map/ppermute | solution.py:505
  66.2 16.9 %collective-permute-start.11 = (bf16[4,16,512]{2,1,0:T(8,128)(2,1)S(1)}, bf16[4,16,512]{2,1,0:T(8,128)(2,1)S(1)}, u32[]{:S(2)}, u32[]{:S(2)}) collective-permute-start(bf16[4,16,512]{2,1,0:T(8,128)(2,1)S(1)} %get-tuple-element.59), channel_id=1, source_target_pairs={{0,8},{1,9},{2,10},{3,11},{4,12},{5,13},{6,14},{7,15},{8,0},{9,1},... | collective-permute-start | bytes 196616 | tf_op jit(solution)/shard_map/ppermute | solution.py:505
  68.3 15.3 %collective-permute-start.12 = (bf16[4,16,512]{2,1,0:T(8,128)(2,1)S(1)}, bf16[4,16,512]{2,1,0:T(8,128)(2,1)S(1)}, u32[]{:S(2)}, u32[]{:S(2)}) collective-permute-start(bf16[4,16,512]{2,1,0:T(8,128)(2,1)S(1)} %get-tuple-element.60), channel_id=1, source_target_pairs={{0,10},{1,11},{2,8},{3,9},{4,14},{5,15},{6,12},{7,13},{8,2},{9,3},... | collective-permute-start | bytes 196616 | tf_op jit(solution)/shard_map/ppermute | solution.py:505
  69.9 15.8 %collective-permute-start.13 = (bf16[4,16,512]{2,1,0:T(8,128)(2,1)S(1)}, bf16[4,16,512]{2,1,0:T(8,128)(2,1)S(1)}, u32[]{:S(2)}, u32[]{:S(2)}) collective-permute-start(bf16[4,16,512]{2,1,0:T(8,128)(2,1)S(1)} %get-tuple-element.61), channel_id=1, source_target_pairs={{0,12},{1,13},{2,14},{3,15},{4,8},{5,9},{6,10},{7,11},{8,4},{9,5},... | collective-permute-start | bytes 196616 | tf_op jit(solution)/shard_map/ppermute | solution.py:505
  71.6 15.9 %collective-permute-start.14 = (bf16[4,16,512]{2,1,0:T(8,128)(2,1)S(1)}, bf16[4,16,512]{2,1,0:T(8,128)(2,1)S(1)}, u32[]{:S(2)}, u32[]{:S(2)}) collective-permute-start(bf16[4,16,512]{2,1,0:T(8,128)(2,1)S(1)} %get-tuple-element.62), channel_id=1, source_target_pairs={{0,14},{1,15},{2,12},{3,13},{4,10},{5,11},{6,8},{7,9},{8,6},{9,7},... | collective-permute-start | bytes 196616 | tf_op jit(solution)/shard_map/ppermute | solution.py:505
  82.1 14.8 %collective-permute-start.29 = (bf16[4,16,512]{2,1,0:T(8,128)(2,1)S(1)}, bf16[4,16,512]{2,1,0:T(8,128)(2,1)S(1)}, u32[]{:S(2)}, u32[]{:S(2)}) collective-permute-start(bf16[4,16,512]{2,1,0:T(8,128)(2,1)S(1)} %get-tuple-element.80), channel_id=1, source_target_pairs={{0,2},{1,3},{2,0},{3,1},{4,6},{5,7},{6,4},{7,5},{8,10},{9,11},{10,... | collective-permute-start | bytes 196616 | tf_op jit(solution)/shard_map/ppermute | solution.py:505
  83.1 16.1 %collective-permute-start.30 = (bf16[4,16,512]{2,1,0:T(8,128)(2,1)S(1)}, bf16[4,16,512]{2,1,0:T(8,128)(2,1)S(1)}, u32[]{:S(2)}, u32[]{:S(2)}) collective-permute-start(bf16[4,16,512]{2,1,0:T(8,128)(2,1)S(1)} %get-tuple-element.81), channel_id=1, source_target_pairs={{0,4},{1,5},{2,6},{3,7},{4,0},{5,1},{6,2},{7,3},{8,12},{9,13},{10,... | collective-permute-start | bytes 196616 | tf_op jit(solution)/shard_map/ppermute | solution.py:505
  83.6 17.7 %collective-permute-start.31 = (bf16[4,16,512]{2,1,0:T(8,128)(2,1)S(1)}, bf16[4,16,512]{2,1,0:T(8,128)(2,1)S(1)}, u32[]{:S(2)}, u32[]{:S(2)}) collective-permute-start(bf16[4,16,512]{2,1,0:T(8,128)(2,1)S(1)} %get-tuple-element.82), channel_id=1, source_target_pairs={{0,6},{1,7},{2,4},{3,5},{4,2},{5,3},{6,0},{7,1},{8,14},{9,15},{10,... | collective-permute-start | bytes 196616 | tf_op jit(solution)/shard_map/ppermute | solution.py:505
  85.7 16.6 %collective-permute-start.32 = (bf16[4,16,512]{2,1,0:T(8,128)(2,1)S(1)}, bf16[4,16,512]{2,1,0:T(8,128)(2,1)S(1)}, u32[]{:S(2)}, u32[]{:S(2)}) collective-permute-start(bf16[4,16,512]{2,1,0:T(8,128)(2,1)S(1)} %get-tuple-element.83), channel_id=1, source_target_pairs={{0,8},{1,9},{2,10},{3,11},{4,12},{5,13},{6,14},{7,15},{8,0},{9,1},... | collective-permute-start | bytes 196616 | tf_op jit(solution)/shard_map/ppermute | solution.py:505
  87.5 14.8 %collective-permute-start.33 = (bf16[4,16,512]{2,1,0:T(8,128)(2,1)S(1)}, bf16[4,16,512]{2,1,0:T(8,128)(2,1)S(1)}, u32[]{:S(2)}, u32[]{:S(2)}) collective-permute-start(bf16[4,16,512]{2,1,0:T(8,128)(2,1)S(1)} %get-tuple-element.84), channel_id=1, source_target_pairs={{0,10},{1,11},{2,8},{3,9},{4,14},{5,15},{6,12},{7,13},{8,2},{9,3},... | collective-permute-start | bytes 196616 | tf_op jit(solution)/shard_map/ppermute | solution.py:505
  96.9 7.9 %collective-permute-start.34 = (bf16[4,16,512]{2,1,0:T(8,128)(2,1)S(1)}, bf16[4,16,512]{2,1,0:T(8,128)(2,1)S(1)}, u32[]{:S(2)}, u32[]{:S(2)}) collective-permute-start(bf16[4,16,512]{2,1,0:T(8,128)(2,1)S(1)} %get-tuple-element.85), channel_id=1, source_target_pairs={{0,12},{1,13},{2,14},{3,15},{4,8},{5,9},{6,10},{7,11},{8,4},{9,5},... | collective-permute-start | bytes 196616 | tf_op jit(solution)/shard_map/ppermute | solution.py:505
  99.3 7.6 %collective-permute-start.35 = (bf16[4,16,512]{2,1,0:T(8,128)(2,1)S(1)}, bf16[4,16,512]{2,1,0:T(8,128)(2,1)S(1)}, u32[]{:S(2)}, u32[]{:S(2)}) collective-permute-start(bf16[4,16,512]{2,1,0:T(8,128)(2,1)S(1)} %get-tuple-element.86), channel_id=1, source_target_pairs={{0,14},{1,15},{2,12},{3,13},{4,10},{5,11},{6,8},{7,9},{8,6},{9,7},... | collective-permute-start | bytes 196616 | tf_op jit(solution)/shard_map/ppermute | solution.py:505
  101.3 6.8 %collective-permute-start.15 = (bf16[4,16,512]{2,1,0:T(8,128)(2,1)S(1)}, bf16[4,16,512]{2,1,0:T(8,128)(2,1)S(1)}, u32[]{:S(2)}, u32[]{:S(2)}) collective-permute-start(bf16[4,16,512]{2,1,0:T(8,128)(2,1)S(1)} %get-tuple-element.64), channel_id=1, source_target_pairs={{0,2},{1,3},{2,0},{3,1},{4,6},{5,7},{6,4},{7,5},{8,10},{9,11},{10,... | collective-permute-start | bytes 196616 | tf_op jit(solution)/shard_map/ppermute | solution.py:505
  102.3 8.2 %collective-permute-start.16 = (bf16[4,16,512]{2,1,0:T(8,128)(2,1)S(1)}, bf16[4,16,512]{2,1,0:T(8,128)(2,1)S(1)}, u32[]{:S(2)}, u32[]{:S(2)}) collective-permute-start(bf16[4,16,512]{2,1,0:T(8,128)(2,1)S(1)} %get-tuple-element.65), channel_id=1, source_target_pairs={{0,4},{1,5},{2,6},{3,7},{4,0},{5,1},{6,2},{7,3},{8,12},{9,13},{10,... | collective-permute-start | bytes 196616 | tf_op jit(solution)/shard_map/ppermute | solution.py:505
  102.3 11.8 %collective-permute-start.17 = (bf16[4,16,512]{2,1,0:T(8,128)(2,1)S(1)}, bf16[4,16,512]{2,1,0:T(8,128)(2,1)S(1)}, u32[]{:S(2)}, u32[]{:S(2)}) collective-permute-start(bf16[4,16,512]{2,1,0:T(8,128)(2,1)S(1)} %get-tuple-element.66), channel_id=1, source_target_pairs={{0,6},{1,7},{2,4},{3,5},{4,2},{5,3},{6,0},{7,1},{8,14},{9,15},{10,... | collective-permute-start | bytes 196616 | tf_op jit(solution)/shard_map/ppermute | solution.py:505
  104.8 9.3 %collective-permute-start.18 = (bf16[4,16,512]{2,1,0:T(8,128)(2,1)S(1)}, bf16[4,16,512]{2,1,0:T(8,128)(2,1)S(1)}, u32[]{:S(2)}, u32[]{:S(2)}) collective-permute-start(bf16[4,16,512]{2,1,0:T(8,128)(2,1)S(1)} %get-tuple-element.67), channel_id=1, source_target_pairs={{0,8},{1,9},{2,10},{3,11},{4,12},{5,13},{6,14},{7,15},{8,0},{9,1},... | collective-permute-start | bytes 196616 | tf_op jit(solution)/shard_map/ppermute | solution.py:505
  106.9 7.2 %collective-permute-start.19 = (bf16[4,16,512]{2,1,0:T(8,128)(2,1)S(1)}, bf16[4,16,512]{2,1,0:T(8,128)(2,1)S(1)}, u32[]{:S(2)}, u32[]{:S(2)}) collective-permute-start(bf16[4,16,512]{2,1,0:T(8,128)(2,1)S(1)} %get-tuple-element.68), channel_id=1, source_target_pairs={{0,10},{1,11},{2,8},{3,9},{4,14},{5,15},{6,12},{7,13},{8,2},{9,3},... | collective-permute-start | bytes 196616 | tf_op jit(solution)/shard_map/ppermute | solution.py:505
  110.4 7.0 %collective-permute-start.21 = (bf16[4,16,512]{2,1,0:T(8,128)(2,1)S(1)}, bf16[4,16,512]{2,1,0:T(8,128)(2,1)S(1)}, u32[]{:S(2)}, u32[]{:S(2)}) collective-permute-start(bf16[4,16,512]{2,1,0:T(8,128)(2,1)S(1)} %get-tuple-element.70), channel_id=1, source_target_pairs={{0,14},{1,15},{2,12},{3,13},{4,10},{5,11},{6,8},{7,9},{8,6},{9,7},... | collective-permute-start | bytes 196616 | tf_op jit(solution)/shard_map/ppermute | solution.py:505
  (19 other events, 151.5 us)

commit v3 on v2

v3 whole, which is shorter than its diff:
```python
import functools
import math

import jax
import jax.numpy as jnp
from jax import lax
from jax.experimental import pallas as pl
from jax.experimental.pallas import tpu as pltpu
from jax.sharding import PartitionSpec as P

HD = 32
GRID = 8
CHUNKS = 1
SPLIT = (True,)
ORDER = (4, 6, 5, 7, 2, 3, 1)
ROOT = math.sqrt(2.0 / math.pi)
LIN = 2.0 * ROOT
CUBE = 8.0 * ROOT * 0.044715
F32 = jnp.float32
BF16 = jnp.bfloat16
VMEM_LIMIT = 18 * 1024 * 1024


def half_gelu(half):
    return half + half * jnp.tanh(half * (LIN + CUBE * (half * half)))


def one_hot_order(cols, inverse=False):
    stride = cols // GRID
    row = lax.broadcasted_iota(jnp.int32, (cols, cols), 0)
    col = lax.broadcasted_iota(jnp.int32, (cols, cols), 1)
    if inverse:
        row, col = col, row
    return jnp.where(col == (row % GRID) * stride + row // GRID, 1.0, 0.0).astype(BF16)


def dot(a, b):
    return jnp.dot(a, b, preferred_element_type=F32)


def vmem():
    return pl.BlockSpec(memory_space=pltpu.VMEM)


def smem():
    return pl.BlockSpec(memory_space=pltpu.SMEM)


def hbm():
    return pl.BlockSpec(memory_space=pltpu.HBM)


def in_hbm(array):
    return pltpu.with_memory_space_constraint(array, pltpu.HBM)


def any_space():
    return pl.BlockSpec(memory_space=pl.ANY)


def params():
    return pltpu.CompilerParams(vmem_limit_bytes=VMEM_LIMIT)


CORE, DP, SPACE, LAST, GROUPS = range(5)


def grid_of(info):
    return info[SPACE] // info[GROUPS]


def cost():
    return pl.CostEstimate(flops=1, bytes_accessed=1, transcendentals=1)


def copy_all(pairs, sems):
    copies = [pltpu.make_async_copy(src, dst, sems.at[n]) for n, (src, dst) in enumerate(pairs)]
    for copy in copies:
        copy.start()
    return copies


def edges_kernel(image, top, bottom, sems):
    rows = image.shape[0]
    for copy in copy_all([(image.at[rows - 1 : rows], bottom), (image.at[0:1], top)], sems):
        copy.wait()


def edge_rows(image):
    edge = jax.ShapeDtypeStruct((1,) + image.shape[1:], BF16)
    return pl.pallas_call(
        edges_kernel,
        in_specs=[hbm()],
        out_specs=[any_space()] * 2,
        out_shape=[edge, edge],
        scratch_shapes=[pltpu.SemaphoreType.DMA((2,))],
        compiler_params=params(),
        name="edge_rows",
    )(in_hbm(image))


def shares_kernel(info, expand, project, expand_part, project_part, sems):
    def span(part, axis):
        size = part.shape[axis]
        return pl.ds(pl.multiple_of(info[CORE] * size, size), size)

    moves = [
        (expand.at[:, span(expand_part, 1)], expand_part),
        (project.at[span(project_part, 0)], project_part),
    ]
    for copy in copy_all(moves, sems):
        copy.wait()


def share_weights(info, w_expand, w_project):
    shapes = [
        (w_expand.shape[0], w_expand.shape[1] // 2),
        (w_project.shape[0] // 2, w_project.shape[1]),
    ]
    return pl.pallas_call(
        shares_kernel,
        in_specs=[smem(), hbm(), hbm()],
        out_specs=[vmem()] * 2,
        out_shape=[jax.ShapeDtypeStruct(shape, BF16) for shape in shapes],
        scratch_shapes=[pltpu.SemaphoreType.DMA((2,))],
        compiler_params=params(),
        name="share_weights",
    )(info, *map(in_hbm, (w_expand, w_project)))


def order_kernel(image, above, below, scale, shift, ordered, normed):
    rows, cols, _ = image.shape
    pick = one_hot_order(cols)
    for row in range(rows + 2):
        if row == 0:
            placed = dot(pick, above[0])
        elif row == rows + 1:
            placed = dot(pick, below[0])
        else:
            placed = dot(pick, image[row - 1])
            ordered[row - 1] = placed.astype(BF16)
        normed[row] = (
            placed * (0.5 * scale[...]) + 0.5 * shift[...]
        ).astype(BF16)


def expand_kernel(first, tile_of, info, *refs):
    refs = list(refs)
    take = lambda n: [refs.pop(0) for _ in range(n)]
    step = pl.program_id(0)
    if first:
        image, above, below, scale, shift, weight, bias, taps, tap_bias = take(9)
        out, ordered, normed = take(3)
        raw, wide, sems, *held = refs
        moved = [(image, held[0])]
        moved += list(zip((scale, shift, weight, bias, taps, tap_bias), held[1:]))
        image, scale, shift, weight, bias, taps, tap_bias = held

        @pl.when(step == 0)
        def _():
            copies = copy_all(moved, sems)
            for copy in copies:
                copy.wait()
            order_kernel(image, above, below, scale, shift, ordered, normed)

    else:
        normed, weight, bias, taps, tap_bias, out, raw, wide = refs
    width = raw.shape[1]
    cols = wide.shape[1] - 2 * GRID
    rows = wide.shape[0] - 2
    if first:
        here = pl.ds(pl.multiple_of(step * width, width), width)
        tile = pl.ds(pl.multiple_of(tile_of(info, step) * width, width), width)
    else:
        here = tile = slice(None)
    weight = weight[:, here]
    half_bias = 0.5 * bias[:, tile]
    half_taps = 0.5 * taps[:, :, tile]
    half_tap_bias = 0.5 * tap_bias[:, tile]
    lane = lax.broadcasted_iota(jnp.int32, (GRID, width), 0)
    batch = (rows + 2) // 2
    for row in range(0, rows + 2, batch):
        tokens = normed[row : row + batch].reshape(batch * cols, -1)
        raw[row * cols : (row + batch) * cols, :] = dot(tokens, weight)
    for row in range(rows + 2):
        value = half_gelu(raw[row * cols : (row + 1) * cols, :] + half_bias)
        if row == 0:
            value = value * jnp.where(info[SPACE] > 0, 1.0, 0.0)
        elif row == rows + 1:
            value = value * jnp.where(info[SPACE] < info[LAST], 1.0, 0.0)
        wide[row, GRID : GRID + cols, :] = value
        head = value[:GRID]
        tail = value[cols - GRID :]
        wide[row, :GRID, :] = jnp.where(lane == 0, 0.0, pltpu.roll(tail, 1, 0))
        wide[row, GRID + cols :, :] = jnp.where(
            lane == GRID - 1, 0.0, pltpu.roll(head, GRID - 1, 0)
        )
        if row >= 2:
            total = half_tap_bias
            for row_off in range(3):
                for col_off in range(3):
                    total = (
                        total
                        + wide[row - 2 + row_off, GRID * col_off : GRID * col_off + cols, :]
                        * half_taps[row_off, col_off][None]
                    )
            out[(row - 2) * cols : (row - 1) * cols, :] = half_gelu(total).astype(BF16)


def expand_some(info, sources, weight, bias, taps, tap_bias, tile_of, first):
    chans, here = weight.shape
    width = min(256, here)
    if first:
        rows, cols, _ = sources[0].shape
    else:
        rows, cols = sources[0].shape[0] - 2, sources[0].shape[1]
    whole = lambda shape: pl.BlockSpec(shape, lambda t, info: (0,) * len(shape))
    held = []
    if first:
        in_specs = [hbm(), whole(sources[1].shape), whole(sources[2].shape)] + [hbm()] * 6
        fetched = [sources[0], *sources[3:], weight, bias, taps, tap_bias]
        held = [pltpu.SemaphoreType.DMA((len(fetched),))]
        held += [pltpu.VMEM(f.shape, f.dtype) for f in fetched]
    else:
        in_specs = [whole(s.shape) for s in sources]
        in_specs += [
            pl.BlockSpec((chans, width), lambda t, info: (0, t)),
            pl.BlockSpec((1, width), lambda t, info: (0, tile_of(info, t))),
            pl.BlockSpec((3, 3, width), lambda t, info: (0, 0, tile_of(info, t))),
            pl.BlockSpec((1, width), lambda t, info: (0, tile_of(info, t))),
        ]
    operands = [info, *sources, weight, bias, taps, tap_bias]
    if first:
        operands = [o if n in (0, 2, 3) else in_hbm(o) for n, o in enumerate(operands)]
    out_specs = [pl.BlockSpec((rows * cols, width), lambda t, info: (0, t))]
    out_shape = [jax.ShapeDtypeStruct((rows * cols, here), BF16)]
    if first:
        shapes = [(rows, cols, chans), (rows + 2, cols, chans)]
        out_specs += [whole(shape) for shape in shapes]
        out_shape += [jax.ShapeDtypeStruct(shape, BF16) for shape in shapes]
    return pl.pallas_call(
        functools.partial(expand_kernel, first, tile_of),
        grid_spec=pltpu.PrefetchScalarGridSpec(
            num_scalar_prefetch=1,
            grid=(here // width,),
            in_specs=in_specs,
            out_specs=out_specs,
            scratch_shapes=[
                pltpu.VMEM(((rows + 2) * cols, width), F32),
                pltpu.VMEM((rows + 2, cols + 2 * GRID, width), F32),
                *held,
            ],
        ),
        out_shape=out_shape,
        compiler_params=params(),
        cost_estimate=cost(),
        name="expand_conv",
    )(*operands)


def pieced_dot(lhs, pieces, info, put):
    width = pieces[0].shape[1]
    for n, piece in enumerate(pieces):
        if len(pieces) == 1:
            start = 0
        else:
            start = pl.multiple_of((1 - info[DP] if n else info[DP]) * width, width)
        put(start, width, dot(lhs[...], piece[...]))


def project_kernel(pieces, split, info, ordered, *refs):
    refs = list(refs)
    take = lambda n: [refs.pop(0) for _ in range(n)]
    spatial, weights, outs, (conv, other) = take(pieces), take(pieces), take(GRID if split else 1), refs
    count, cols, chans = ordered.shape
    size = cols // GRID
    own = weights[0]
    width = own.shape[1]

    def put(start, product):
        span = pl.ds(start, width)
        for row in range(count):
            at = slice(row * cols, (row + 1) * cols)
            conv[at, span] = (ordered[row, :, span].astype(F32) + product[at]).astype(BF16)

    if pieces == 1:
        put(0, dot(spatial[0][...], own[...]))
    else:
        mine, core = info[DP], info[CORE]
        half = own.shape[0] // 2
        for n, at in ((1, core), (2, 1 - core)):
            other[pl.ds(pl.multiple_of(at * half, half), half), :] = weights[n][...]
        part = half // 2
        starts = (
            (mine * half, half),
            ((1 - mine) * half + core * part, part),
            ((1 - mine) * half + (1 - core) * part, part),
        )
        for weight, column in ((own, mine), (other, 1 - mine)):
            total = None
            for lhs, (start, depth) in zip(spatial, starts):
                rows = pl.ds(pl.multiple_of(start, part), depth)
                product = dot(lhs[...], weight[rows, :])
                total = product if total is None else total + product
            put(pl.multiple_of(column * width, width), total)

    for k in range(GRID):
        place = (grid_of(info) ^ k) if split else k
        for row in range(count):
            start = row * cols + pl.multiple_of(place * size, size)
            block_of(outs, k)[row] = conv[pl.ds(start, size), :]


def block_of(parts, k):
    return parts[k] if len(parts) > 1 else parts[0].at[k]


def project_rows(info, spatial, ordered, weights, chunk, count, split):
    rows, cols, chans = ordered.shape
    size = cols // GRID
    block = (count, size, chans)
    outs = [block] * GRID if split else [(GRID,) + block]
    whole = lambda shape: pl.BlockSpec(shape, lambda t, info: (0,) * len(shape))
    return pl.pallas_call(
        functools.partial(project_kernel, len(weights), split),
        grid_spec=pltpu.PrefetchScalarGridSpec(
            num_scalar_prefetch=1,
            grid=(1,),
            in_specs=[pl.BlockSpec((count, cols, chans), lambda t, info: (chunk, 0, 0))]
            + [pl.BlockSpec((count * cols, s.shape[1]), lambda t, info: (chunk, 0)) for s in spatial]
            + [whole(w.shape) for w in weights],
            out_specs=[whole(out) for out in outs],
            scratch_shapes=[pltpu.VMEM((count * cols, chans), BF16), pltpu.VMEM(weights[0].shape, BF16)],
        ),
        out_shape=[jax.ShapeDtypeStruct(out, BF16) for out in outs],
        compiler_params=params(),
        cost_estimate=cost(),
        name="project_rows",
    )(info, ordered, *spatial, *weights)


def attend_kernel(pieces, blocks, info, gain, bias, *refs):
    refs = list(refs)
    take = lambda n: [refs.pop(0) for _ in range(n)]
    qkv_pieces, out_pieces = take(pieces), take(pieces)
    tokens, outs = take(blocks), take(blocks)
    lned, triple, mixed, resid = refs
    count, size, chans = tokens[0].shape[-3:]
    wins = size // GRID
    length = GRID * GRID
    group = min(256, chans)
    heads = group // HD
    keys = heads * length

    for a in range(count):
        rows = [block_of(tokens, k)[a].astype(F32) for k in range(GRID)]
        for w in range(wins):
            x = jnp.concatenate([r[w * GRID : (w + 1) * GRID] for r in rows], axis=0)
            start = (a * wins + w) * length
            resid[start : start + length, :] = x
            center = jnp.mean(x, axis=-1, keepdims=True)
            off = x - center
            spread = jnp.mean(off * off, axis=-1, keepdims=True)
            lned[start : start + length, :] = (
                off * lax.rsqrt(spread + 1e-05) * gain[...] + bias[...]
            ).astype(BF16)

    def put_triple(start, width, product):
        triple[:, pl.ds(start, width)] = product.astype(BF16)

    pieced_dot(lned, qkv_pieces, info, put_triple)

    def same(shape, row_block, col_block):
        row = lax.broadcasted_iota(jnp.int32, shape, 0) // row_block
        col = lax.broadcasted_iota(jnp.int32, shape, 1) // col_block
        return jnp.where(row == col, 1.0, 0.0).astype(BF16)

    spread_mask = same((keys, group), length, HD)
    sum_mask = same((256, 256), length, length)
    factor = math.log2(math.e) / math.sqrt(HD)
    for win in range(count * wins):
        at = slice(win * length, (win + 1) * length)
        for g in range(chans // group):
            cols = slice(g * group, (g + 1) * group)
            query = triple[at, cols]
            key = triple[at, chans + g * group : chans + (g + 1) * group]
            value = triple[at, 2 * chans + g * group : 2 * chans + (g + 1) * group]
            key_wide = jnp.concatenate([key] * heads, axis=0) * spread_mask
            value_wide = jnp.concatenate([value] * heads, axis=0) * spread_mask
            scores = lax.dot_general(
                query, key_wide, (((1,), (1,)), ((), ())), preferred_element_type=F32
            )
            exponent = jnp.minimum(jnp.exp2(scores * factor), 3.3895e38)
            rounded = exponent.astype(BF16)
            sums = jnp.concatenate(
                [dot(rounded[:, n : n + 256], sum_mask) for n in range(0, keys, 256)], axis=1
            )
            soft = (exponent / sums).astype(BF16)
            mixed[at, cols] = dot(soft, value_wide).astype(BF16)

    def put_out(start, width, product):
        span = pl.ds(start, width)
        resid[:, span] = resid[:, span] + product

    pieced_dot(mixed, out_pieces, info, put_out)
    for a in range(count):
        for k in range(GRID):
            parts = []
            for w in range(wins):
                start = (a * wins + w) * length + k * GRID
                parts.append(resid[start : start + GRID, :])
            block_of(outs, k)[a] = jnp.concatenate(parts, axis=0).astype(BF16)


def attend(info, tokens, gain, bias, w_qkv, w_out):
    count, size, chans = tokens[0].shape[-3:]
    total = count * size * GRID
    return pl.pallas_call(
        functools.partial(attend_kernel, len(w_qkv), len(tokens)),
        out_shape=[jax.ShapeDtypeStruct(t.shape, BF16) for t in tokens],
        in_specs=[smem()] + [vmem()] * (2 + 2 * len(w_qkv) + len(tokens)),
        out_specs=[vmem()] * len(tokens),
        scratch_shapes=[
            pltpu.VMEM((total, chans), BF16),
            pltpu.VMEM((total, 3 * chans), BF16),
            pltpu.VMEM((total, chans), BF16),
            pltpu.VMEM((total, chans), F32),
        ],
        compiler_params=params(),
        cost_estimate=cost(),
        name="attend",
    )(info, gain, bias, *w_qkv, *w_out, *tokens)


def restore_kernel(blocks, info, *refs):
    parts = refs[:blocks]
    out, buf = refs[-2:]
    count, cols, chans = out.shape
    size = cols // GRID
    back = one_hot_order(cols, inverse=True)
    for row in range(count):
        if blocks == 1:
            tokens = parts[0][:, row].reshape(cols, chans)
        else:
            for k in range(GRID):
                place = pl.multiple_of((grid_of(info) ^ k) * size, size)
                buf[pl.ds(row * cols + place, size), :] = parts[k][row]
            tokens = buf[row * cols : (row + 1) * cols, :]
        out[row] = dot(back, tokens).astype(BF16)


def restore_rows(info, parts, rows, chunk, out):
    count, size, chans = parts[0].shape[-3:]
    cols = size * GRID
    in_specs = [pl.BlockSpec(p.shape, lambda t, i, n=p.ndim: (0,) * n) for p in parts]
    operands = [info, *parts]
    aliases = {}
    if out is not None:
        in_specs.append(pl.BlockSpec(memory_space=pl.ANY))
        aliases = {len(operands): 0}
        operands.append(out)
    return pl.pallas_call(
        functools.partial(restore_kernel, len(parts)),
        grid_spec=pltpu.PrefetchScalarGridSpec(
            num_scalar_prefetch=1,
            grid=(1,),
            in_specs=in_specs,
            out_specs=pl.BlockSpec((count, cols, chans), lambda t, info: (chunk, 0, 0)),
            scratch_shapes=[pltpu.VMEM((count * cols, chans), BF16)],
        ),
        out_shape=jax.ShapeDtypeStruct((rows, cols, chans), BF16),
        input_output_aliases=aliases,
        compiler_params=params(),
        cost_estimate=cost(),
        name="restore_rows",
    )(*operands)


def after(value, *others):
    return lax.optimization_barrier((value, *others))[0]


def local(
    fields,
    bn_scale,
    bn_shift,
    w_expand,
    expand_bias,
    dw_kernel,
    dw_bias,
    w_project,
    ln_gain,
    ln_bias,
    w_qkv,
    w_out,
):
    _, rows, cols, chans = fields.shape
    dp, space = lax.axis_size("dp"), lax.axis_size("space")
    dp_at, space_at = lax.axis_index("dp"), lax.axis_index("space")
    groups = space // GRID
    pairs = dp == 2 and space % 2 == 0
    info = jnp.stack(
        [
            jnp.asarray(v, jnp.int32)
            for v in (space_at % 2, dp_at, space_at, space - 1, groups)
        ]
    )
    as_row = lambda v: v.reshape(1, -1)
    image = fields.reshape(rows, cols, chans)
    small = (as_row(expand_bias), dw_kernel, as_row(dw_bias))
    gain, bias = as_row(ln_gain), as_row(ln_bias)

    over_dp = lambda w: lax.ppermute(w, "dp", [(0, 1), (1, 0)])
    over_core = lambda w: lax.ppermute(w, "space", [(i, i ^ 1) for i in range(space)])
    top, bottom = edge_rows(image)
    above = lax.ppermute(bottom, "space", [(i, i + 1) for i in range(space - 1)])
    below = lax.ppermute(top, "space", [(i + 1, i) for i in range(space - 1)])
    if pairs:
        mine = share_weights(after(info, top), w_expand, w_project)
        expand_got, project_got = map(over_dp, mine)
        above = after(above, *mine)
    sources = (image, above, below, as_row(bn_scale), as_row(bn_shift))
    if pairs:
        tiles = max(1, w_expand.shape[1] // 256)
        half = tiles // 2
        own_place = lambda i, t: i[DP] * tiles + t
        got_place = lambda i, t: (1 - i[DP]) * tiles + i[CORE] * half + t
        other_place = lambda i, t: (1 - i[DP]) * tiles + (1 - i[CORE]) * half + t
        own, ordered, normed = expand_some(info, sources, w_expand, *small, own_place, True)
        expand_got = after(expand_got, own)
        expand_other = over_core(expand_got)
        (got,) = expand_some(info, (normed,), expand_got, *small, got_place, False)
        expand_other, normed = lax.optimization_barrier((expand_other, normed, got))[:2]
        (other,) = expand_some(info, (normed,), expand_other, *small, other_place, False)
        spatial = [own, got, other]
        project_got = after(project_got, own)
        project_all = [w_project, project_got, over_core(project_got)]
    else:
        gathered = lambda w: lax.all_gather(w, "dp", axis=1, tiled=True)
        spatial, ordered, _ = expand_some(
            info, sources, gathered(w_expand), *small, lambda i, t: t, True
        )
        spatial = [spatial]
        project_all = [gathered(w_project)]
        w_qkv, w_out = [gathered(w_qkv)], [gathered(w_out)]

    count = rows // CHUNKS
    rings = [list(range(first, space, groups)) for first in range(groups)]

    def exchange(parts):
        if len(parts) == 1:
            return [
                lax.all_to_all(parts[0], "space", 0, 0, axis_index_groups=rings, tiled=True)
            ]
        parts = list(parts)
        for k in ORDER:
            pairs_k = [
                (s, (((s // groups) ^ k) * groups) + s % groups) for s in range(space)
            ]
            parts[k] = lax.ppermute(parts[k], "space", pairs_k)
        return parts

    sent = [
        exchange(project_rows(info, spatial, ordered, project_all, chunk, count, SPLIT[chunk]))
        for chunk in range(CHUNKS)
    ]
    if pairs:
        w_qkv, w_out = [w_qkv, over_dp(w_qkv)], [w_out, over_dp(w_out)]
    back = [exchange(attend(info, parts, gain, bias, w_qkv, w_out)) for parts in sent]
    result = None
    for chunk in range(CHUNKS):
        result = restore_rows(info, back[chunk], rows, chunk, result)
    return result.reshape(fields.shape)


def solution(mesh):
    in_specs = (
        P("dp", "space", None, None),
        P(),
        P(),
        P(None, "dp"),
        P(),
        P(),
        P(),
        P(None, "dp"),
        P(),
        P(),
        P(None, "dp"),
        P(None, "dp"),
    )
    out_specs = P("dp", "space", None, None)
    return jax.shard_map(local, mesh=mesh, in_specs=in_specs, out_specs=out_specs, check_vma=False)
```

time: 120 us -> 115 us (0.958); the launches traced: 119 us -> 113 us
  waiting for transfers between devices: 14.4 us -> 35.9 us
  starting transfers between devices: 54.5 us -> 36.8 us
  local copies, waits for them, and re-layouts: 10.5 us -> 0.13 us
    ppermute x30 -> x16, starting transfers between devices: 48.7 us -> 25.9 us  [the longest x14 23.1 us: exchange(): parts[k] = lax.ppermute(parts[k], 'space', pairs_k)]
    ppermute x30 -> x16, waiting for transfers between devices: 9.12 us -> 28.8 us  [the longest x14 26.8 us: exchange(): parts[k] = lax.ppermute(parts[k], 'space', pairs_k)]
    unnamed x30 -> x16, local copies, waits for them, and re-layouts: 9.43 us -> 0.04 us
    ppermute x3 -> x4, starting transfers between devices: 3.61 us -> 7.01 us  [local(): over_dp = lambda w: lax.ppermute(w, 'dp', [(0, 1), (1, 0)])]
    ppermute x3 -> x4, waiting for transfers between devices: 5.3 us -> 7.01 us  [local(): over_dp = lambda w: lax.ppermute(w, 'dp', [(0, 1), (1, 0)])]
    ppermute x3 -> x2, starting transfers between devices: 2.22 us -> 3.9 us  [local(): lax.ppermute(w, 'space', [(i, i ^ 1) for i in range(space)])]
    pallas_call x10 -> x8, Pallas kernels: 39.4 us -> 39.7 us  [the longest x3 17.3 us: expand_some(): pl.pallas_call(functools.partial(expand_kernel, first, tile_of), grid_spe...]
  transfers between devices with their start and end apart: 36 -> 22, of which waited for: 7 -> 11; matrix products, arithmetic and copies ran while one was open for 1% -> 0% of each run, Pallas kernels for 31% -> 18%
where the time goes in v3:
time: 115 us; the launch traced here: 113 us
  Pallas kernels  39.7 us (35%)
  starting transfers between devices  36.8 us (32%)
  waiting for transfers between devices  35.9 us (31%)
    ppermute x14, waiting for transfers between devices, exchange(): parts[k] = lax.ppermute(parts[k], 'space', pairs_k)  26.8 us
    ppermute x14, starting transfers between devices, exchange(): parts[k] = lax.ppermute(parts[k], 'space', pairs_k)  23.1 us
    pallas_call x3, Pallas kernels, expand_some(): pl.pallas_call(functools.partial(expand_kernel, first, tile_of), grid_spe...  17.3 us
    pallas_call x1, Pallas kernels, attend(): pl.pallas_call(functools.partial(attend_kernel, len(w_qkv), len(tokens)),...  14.6 us
    ppermute x4, starting transfers between devices, local(): over_dp = lambda w: lax.ppermute(w, 'dp', [(0, 1), (1, 0)])  7.01 us
    ppermute x4, waiting for transfers between devices, local(): over_dp = lambda w: lax.ppermute(w, 'dp', [(0, 1), (1, 0)])  7.01 us
    ppermute x2, starting transfers between devices, local(): lax.ppermute(w, 'space', [(i, i ^ 1) for i in range(space)])  3.9 us
    pallas_call x1, Pallas kernels, project_rows(): pl.pallas_call(functools.partial(project_kernel, len(weights), split), gr...  3.06 us
  transfers between devices with their start and end apart: 22, of which 11 were waited for; matrix products, arithmetic and copies ran while one was open for 0% of the time, Pallas kernels for 18%

profile of v3, /device:TPU:0, one launch (start us, length us, event | category | flops | bytes accessed | tf_op | source)
XLA Modules:
  0.0 112.7 jit_solution(10121584457031623371)
XLA Ops:
  0.0 1.1 edge_rows.1
  1.2 1.8 %share_weights.1 = (bf16[512,512]{1,0:T(8,128)(2,1)S(1)}, bf16[1024,256]{1,0:T(8,128)(2,1)S(1)}) custom-call(s32[5]{0:T(128)S(1)} %stack.15.info, bf16[512,1024]{1,0:T(8,128)(2,1)} %refs_5_.1, bf16[2048,256]{1,0:T(8,128)(2,1)} %refs_3_.5), custom_call_target="tpu_custom_call" | custom-call | tf_op jit(solution)/shard_map/share_weights/pallas_call | solution.py:120
  3.0 3.0 %collective-permute-start.4 = (bf16[512,512]{1,0:T(8,128)(2,1)S(1)}, bf16[512,512]{1,0:T(8,128)(2,1)S(1)}, u32[]{:S(2)}, u32[]{:S(2)}) collective-permute-start(bf16[512,512]{1,0:T(8,128)(2,1)S(1)} %get-tuple-element.37), channel_id=1, source_target_pairs={{0,16},{16,0},{1,17},{17,1},{2,18},{18,2},{3,19},{19,3},{4,20},{20... | collective-permute-start | bytes 1572872 | tf_op jit(solution)/shard_map/ppermute | solution.py:513
  6.1 1.5 %collective-permute-start.2 = (bf16[1,128,512]{2,1,0:T(8,128)(2,1)S(1)}, bf16[1,128,512]{2,1,0:T(8,128)(2,1)S(1)}, u32[]{:S(2)}, u32[]{:S(2)}) collective-permute-start(bf16[1,128,512]{2,1,0:T(8,128)(2,1)S(1)} %get-tuple-element.34), channel_id=1, source_target_pairs={{0,1},{1,2},{2,3},{3,4},{4,5},{5,6},{6,7},{7,8},{8,9},{9,10},{10,1... | collective-permute-start | bytes 393224 | tf_op jit(solution)/shard_map/ppermute | solution.py:516
  7.5 1.3 %collective-permute-start.3 = (bf16[1,128,512]{2,1,0:T(8,128)(2,1)S(1)}, bf16[1,128,512]{2,1,0:T(8,128)(2,1)S(1)}, u32[]{:S(2)}, u32[]{:S(2)}) collective-permute-start(bf16[1,128,512]{2,1,0:T(8,128)(2,1)S(1)} %get-tuple-element.35), channel_id=1, source_target_pairs={{1,0},{2,1},{3,2},{4,3},{5,4},{6,5},{7,6},{8,7},{9,8},{10,9},{11,1... | collective-permute-start | bytes 393224 | tf_op jit(solution)/shard_map/ppermute | solution.py:517
  8.8 1.8 %collective-permute-start = (bf16[512,768]{1,0:T(8,128)(2,1)S(1)}, bf16[512,768]{1,0:T(8,128)(2,1)S(1)}, u32[]{:S(2)}, u32[]{:S(2)}) collective-permute-start(bf16[512,768]{1,0:T(8,128)(2,1)S(1)} %copy-done.2), channel_id=1, source_target_pairs={{0,16},{16,0},{1,17},{17,1},{2,18},{18,2},{3,19},{19,3},{4,20},{20... | collective-permute-start | bytes 2359304 | tf_op jit(solution)/shard_map/ppermute | solution.py:513
  10.7 2.1 %collective-permute-done.3.refs_2_ = bf16[1,128,512]{2,1,0:T(8,128)(2,1)S(1)} collective-permute-done((bf16[1,128,512]{2,1,0:T(8,128)(2,1)S(1)}, bf16[1,128,512]{2,1,0:T(8,128)(2,1)S(1)}, u32[]{:S(2)}, u32[]{:S(2)}) %collective-permute-start.3) | collective-permute-done | bytes 131104 | tf_op jit(solution)/shard_map/ppermute | solution.py:517
  12.7 9.3 %expand_conv.3 = (bf16[1024,1024]{1,0:T(8,128)(2,1)S(1)}, bf16[8,128,512]{2,1,0:T(8,128)(2,1)S(1)}, bf16[10,128,512]{2,1,0:T(8,128)(2,1)S(1)}) custom-call(s32[5]{0:T(128)S(1)} %stack.15.info, bf16[8,128,512]{2,1,0:T(8,128)(2,1)} %bitcast.20, bf16[1,128,512]{2,1,0:T(8,128)(2,1)S(1)} %collective-permute-done.2.refs_1_, ...), custom_call_target="tpu_custom_call" | custom-call | flops 1 | bytes 1 | tf_op jit(solution)/shard_map/expand_conv/pallas_call | solution.py:241
  22.1 3.9 %collective-permute-start.5 = (bf16[512,512]{1,0:T(8,128)(2,1)S(1)}, bf16[512,512]{1,0:T(8,128)(2,1)S(1)}, u32[]{:S(2)}, u32[]{:S(2)}) collective-permute-start(bf16[512,512]{1,0:T(8,128)(2,1)S(1)} %collective-permute-done.4.refs_1_), channel_id=1, source_target_pairs={{0,1},{1,0},{2,3},{3,2},{4,5},{5,4},{6,7},{7,6},{8,9},{9,8},{10,11... | collective-permute-start | bytes 1572872 | tf_op jit(solution)/shard_map/ppermute | solution.py:514
  26.0 4.0 %collective-permute-done.6.refs_4_ = bf16[1024,256]{1,0:T(8,128)(2,1)S(1)} collective-permute-done((bf16[1024,256]{1,0:T(8,128)(2,1)S(1)}, bf16[1024,256]{1,0:T(8,128)(2,1)S(1)}, u32[]{:S(2)}, u32[]{:S(2)}) %collective-permute-start.6) | collective-permute-done | bytes 524320 | tf_op jit(solution)/shard_map/ppermute | solution.py:513
  30.0 2.1 %collective-permute-start.1 = (bf16[512,256]{1,0:T(8,128)(2,1)S(1)}, bf16[512,256]{1,0:T(8,128)(2,1)S(1)}, u32[]{:S(2)}, u32[]{:S(2)}) collective-permute-start(bf16[512,256]{1,0:T(8,128)(2,1)S(1)} %copy-done.3), channel_id=1, source_target_pairs={{0,16},{16,0},{1,17},{17,1},{2,18},{18,2},{3,19},{19,3},{4,20},{20... | collective-permute-start | bytes 786440 | tf_op jit(solution)/shard_map/ppermute | solution.py:513
  32.0 3.9 %expand_conv.4.refs_1_ = bf16[1024,512]{1,0:T(8,128)(2,1)S(1)} custom-call(s32[5]{0:T(128)S(1)} %stack.15.info, bf16[10,128,512]{2,1,0:T(8,128)(2,1)S(1)} %get-tuple-element.44.refs_0_, bf16[512,512]{1,0:T(8,128)(2,1)S(1)} %collective-permute-done.4.refs_1_, f32[1,2048]{1,0:T(1,128)S(1)} %bitcast.12, f32[3,3,2048]{2,1,0:T(4,128)S(1)} %copy-done.1, ...), custom_call_target="tpu_custom_call" | custom-call | flops 1 | bytes 1 | tf_op jit(solution)/shard_map/expand_conv/pallas_call | solution.py:241
  36.0 4.1 %expand_conv.5.refs_2_ = bf16[1024,512]{1,0:T(8,128)(2,1)S(1)} custom-call(s32[5]{0:T(128)S(1)} %stack.15.info, bf16[10,128,512]{2,1,0:T(8,128)(2,1)S(1)} %get-tuple-element.44.refs_0_, bf16[512,512]{1,0:T(8,128)(2,1)S(1)} %collective-permute-done.5.refs_1_, f32[1,2048]{1,0:T(1,128)S(1)} %bitcast.13, f32[3,3,2048]{2,1,0:T(4,128)S(1)} %copy-done.1, ...), custom_call_target="tpu_custom_call" | custom-call | flops 1 | bytes 1 | tf_op jit(solution)/shard_map/expand_conv/pallas_call | solution.py:241
  40.1 3.1 %project_rows.1 = (bf16[8,16,512]{2,1,0:T(8,128)(2,1)S(1)}, bf16[8,16,512]{2,1,0:T(8,128)(2,1)S(1)}, bf16[8,16,512]{2,1,0:T(8,128)(2,1)S(1)}, bf16[8,16,512]{2,1...) custom-call(s32[5]{0:T(128)S(1)} %stack.15.info, ...), custom_call_target="tpu_custom_call" | custom-call | flops 1 | bytes 1 | tf_op jit(solution)/shard_map/project_rows/pallas_call | solution.py:324
  43.1 2.6 %collective-permute-start.10 = (bf16[8,16,512]{2,1,0:T(8,128)(2,1)S(1)}, bf16[8,16,512]{2,1,0:T(8,128)(2,1)S(1)}, u32[]{:S(2)}, u32[]{:S(2)}) collective-permute-start(bf16[8,16,512]{2,1,0:T(8,128)(2,1)S(1)} %get-tuple-element.50), channel_id=1, source_target_pairs={{0,6},{1,7},{2,4},{3,5},{4,2},{5,3},{6,0},{7,1},{8,14},{9,15},{10,... | collective-permute-start | bytes 393224 | tf_op jit(solution)/shard_map/ppermute | solution.py:560
  45.7 2.6 %collective-permute-start.11 = (bf16[8,16,512]{2,1,0:T(8,128)(2,1)S(1)}, bf16[8,16,512]{2,1,0:T(8,128)(2,1)S(1)}, u32[]{:S(2)}, u32[]{:S(2)}) collective-permute-start(bf16[8,16,512]{2,1,0:T(8,128)(2,1)S(1)} %get-tuple-element.51), channel_id=1, source_target_pairs={{0,8},{1,9},{2,10},{3,11},{4,12},{5,13},{6,14},{7,15},{8,0},{9,1},... | collective-permute-start | bytes 393224 | tf_op jit(solution)/shard_map/ppermute | solution.py:560
  48.6 3.0 %collective-permute-done.1.refs_3_ = bf16[512,256]{1,0:T(8,128)(2,1)S(1)} collective-permute-done((bf16[512,256]{1,0:T(8,128)(2,1)S(1)}, bf16[512,256]{1,0:T(8,128)(2,1)S(1)}, u32[]{:S(2)}, u32[]{:S(2)}) %collective-permute-start.1) | collective-permute-done | bytes 262176 | tf_op jit(solution)/shard_map/ppermute | solution.py:513
  51.6 3.8 %collective-permute-start.13 = (bf16[8,16,512]{2,1,0:T(8,128)(2,1)S(1)}, bf16[8,16,512]{2,1,0:T(8,128)(2,1)S(1)}, u32[]{:S(2)}, u32[]{:S(2)}) collective-permute-start(bf16[8,16,512]{2,1,0:T(8,128)(2,1)S(1)} %get-tuple-element.53), channel_id=1, source_target_pairs={{0,12},{1,13},{2,14},{3,15},{4,8},{5,9},{6,10},{7,11},{8,4},{9,5},... | collective-permute-start | bytes 393224 | tf_op jit(solution)/shard_map/ppermute | solution.py:560
  55.4 1.1 %collective-permute-start.14 = (bf16[8,16,512]{2,1,0:T(8,128)(2,1)S(1)}, bf16[8,16,512]{2,1,0:T(8,128)(2,1)S(1)}, u32[]{:S(2)}, u32[]{:S(2)}) collective-permute-start(bf16[8,16,512]{2,1,0:T(8,128)(2,1)S(1)} %get-tuple-element.54), channel_id=1, source_target_pairs={{0,14},{1,15},{2,12},{3,13},{4,10},{5,11},{6,8},{7,9},{8,6},{9,7},... | collective-permute-start | bytes 393224 | tf_op jit(solution)/shard_map/ppermute | solution.py:560
  57.0 7.1 %collective-permute-done.11.refs_8_ = bf16[8,16,512]{2,1,0:T(8,128)(2,1)S(1)} collective-permute-done((bf16[8,16,512]{2,1,0:T(8,128)(2,1)S(1)}, bf16[8,16,512]{2,1,0:T(8,128)(2,1)S(1)}, u32[]{:S(2)}, u32[]{:S(2)}) %collective-permute-start.11) | collective-permute-done | bytes 131104 | tf_op jit(solution)/shard_map/ppermute | solution.py:560
  64.1 2.2 %collective-permute-done.12.refs_9_ = bf16[8,16,512]{2,1,0:T(8,128)(2,1)S(1)} collective-permute-done((bf16[8,16,512]{2,1,0:T(8,128)(2,1)S(1)}, bf16[8,16,512]{2,1,0:T(8,128)(2,1)S(1)}, u32[]{:S(2)}, u32[]{:S(2)}) %collective-permute-start.12) | collective-permute-done | bytes 131104 | tf_op jit(solution)/shard_map/ppermute | solution.py:560
  66.9 2.2 %collective-permute-done.9.refs_6_ = bf16[8,16,512]{2,1,0:T(8,128)(2,1)S(1)} collective-permute-done((bf16[8,16,512]{2,1,0:T(8,128)(2,1)S(1)}, bf16[8,16,512]{2,1,0:T(8,128)(2,1)S(1)}, u32[]{:S(2)}, u32[]{:S(2)}) %collective-permute-start.9) | collective-permute-done | bytes 131104 | tf_op jit(solution)/shard_map/ppermute | solution.py:560
  69.1 14.6 %attend.1 = (bf16[8,16,512]{2,1,0:T(8,128)(2,1)S(1)}, bf16[8,16,512]{2,1,0:T(8,128)(2,1)S(1)}, bf16[8,16,512]{2,1,0:T(8,128)(2,1)S(1)}, bf16[8,16,512]{2,1,0:T(8...) custom-call(s32[5]{0:T(128)S(1)} %stack.15.info, ...), custom_call_target="tpu_custom_call" | custom-call | flops 1 | bytes 1 | tf_op jit(solution)/shard_map/attend/pallas_call | solution.py:418
  84.1 4.4 %collective-permute-start.16 = (bf16[8,16,512]{2,1,0:T(8,128)(2,1)S(1)}, bf16[8,16,512]{2,1,0:T(8,128)(2,1)S(1)}, u32[]{:S(2)}, u32[]{:S(2)}) collective-permute-start(bf16[8,16,512]{2,1,0:T(8,128)(2,1)S(1)} %get-tuple-element.57), channel_id=1, source_target_pairs={{0,4},{1,5},{2,6},{3,7},{4,0},{5,1},{6,2},{7,3},{8,12},{9,13},{10,... | collective-permute-start | bytes 393224 | tf_op jit(solution)/shard_map/ppermute | solution.py:560
  88.5 2.9 %collective-permute-start.18 = (bf16[8,16,512]{2,1,0:T(8,128)(2,1)S(1)}, bf16[8,16,512]{2,1,0:T(8,128)(2,1)S(1)}, u32[]{:S(2)}, u32[]{:S(2)}) collective-permute-start(bf16[8,16,512]{2,1,0:T(8,128)(2,1)S(1)} %get-tuple-element.59), channel_id=1, source_target_pairs={{0,8},{1,9},{2,10},{3,11},{4,12},{5,13},{6,14},{7,15},{8,0},{9,1},... | collective-permute-start | bytes 393224 | tf_op jit(solution)/shard_map/ppermute | solution.py:560
  91.4 0.9 collective-permute-start.19
  92.4 2.4 %collective-permute-start.20 = (bf16[8,16,512]{2,1,0:T(8,128)(2,1)S(1)}, bf16[8,16,512]{2,1,0:T(8,128)(2,1)S(1)}, u32[]{:S(2)}, u32[]{:S(2)}) collective-permute-start(bf16[8,16,512]{2,1,0:T(8,128)(2,1)S(1)} %get-tuple-element.61), channel_id=1, source_target_pairs={{0,12},{1,13},{2,14},{3,15},{4,8},{5,9},{6,10},{7,11},{8,4},{9,5},... | collective-permute-start | bytes 393224 | tf_op jit(solution)/shard_map/ppermute | solution.py:560
  94.7 1.0 collective-permute-done.16.refs_2_
  95.7 1.2 %collective-permute-start.21 = (bf16[8,16,512]{2,1,0:T(8,128)(2,1)S(1)}, bf16[8,16,512]{2,1,0:T(8,128)(2,1)S(1)}, u32[]{:S(2)}, u32[]{:S(2)}) collective-permute-start(bf16[8,16,512]{2,1,0:T(8,128)(2,1)S(1)} %get-tuple-element.62), channel_id=1, source_target_pairs={{0,14},{1,15},{2,12},{3,13},{4,10},{5,11},{6,8},{7,9},{8,6},{9,7},... | collective-permute-start | bytes 393224 | tf_op jit(solution)/shard_map/ppermute | solution.py:560
  96.9 1.0 collective-permute-done.17.refs_3_
  98.1 12.6 %collective-permute-done.19.refs_5_ = bf16[8,16,512]{2,1,0:T(8,128)(2,1)S(1)} collective-permute-done((bf16[8,16,512]{2,1,0:T(8,128)(2,1)S(1)}, bf16[8,16,512]{2,1,0:T(8,128)(2,1)S(1)}, u32[]{:S(2)}, u32[]{:S(2)}) %collective-permute-start.19) | collective-permute-done | bytes 131104 | tf_op jit(solution)/shard_map/ppermute | solution.py:560
  110.7 2.0 %restore_rows.1 = bf16[8,128,512]{2,1,0:T(8,128)(2,1)} custom-call(s32[5]{0:T(128)S(1)} %stack.15.info, bf16[8,16,512]{2,1,0:T(8,128)(2,1)S(1)} %get-tuple-element.55.refs_0_, bf16[8,16,512]{2,1,0:T(8,128)(2,1)S(1)} %collective-permute-done.15.refs_1_, bf16[8,16,512]{2,1,0:T(8,128)(2,1)S(1)} %collective-permute-done.16.refs_2_, ...), custom_call_target="tpu_custom_call" | custom-call | flops 1 | bytes 1 | tf_op jit(solution)/shard_map/restore_rows/pallas_call | solution.py:462
  (37 shorter events, 2.1 us)
Async XLA Ops:
  0.0 8.8 %copy-start.2 = (bf16[512,768]{1,0:T(8,128)(2,1)S(1)}, bf16[512,768]{1,0:T(8,128)(2,1)}, u32[]{:S(2)}) copy-start(bf16[512,768]{1,0:T(8,128)(2,1)} %refs_0_.1) | copy-start | bytes 2359300
  1.2 28.8 %copy-start.3 = (bf16[512,256]{1,0:T(8,128)(2,1)S(1)}, bf16[512,256]{1,0:T(8,128)(2,1)}, u32[]{:S(2)}) copy-start(bf16[512,256]{1,0:T(8,128)(2,1)} %refs_2_.1) | copy-start | bytes 786436
  1.2 30.9 %copy-start.1 = (f32[3,3,2048]{2,1,0:T(4,128)S(1)}, f32[3,3,2048]{2,1,0:T(4,128)}, u32[]{:S(2)}) copy-start(f32[3,3,2048]{2,1,0:T(4,128)} %refs_3_.4) | copy-start | bytes 221188
  1.2 30.9 %copy-start.4 = (f32[2048]{0:T(1024)S(1)}, f32[2048]{0:T(1024)}, u32[]{:S(2)}) copy-start(f32[2048]{0:T(1024)} %param.16) | copy-start | bytes 24580
  1.2 30.9 %copy-start.5 = (f32[2048]{0:T(1024)S(1)}, f32[2048]{0:T(1024)}, u32[]{:S(2)}) copy-start(f32[2048]{0:T(1024)} %param.18) | copy-start | bytes 24580
  3.0 19.1 %collective-permute-start.4 = (bf16[512,512]{1,0:T(8,128)(2,1)S(1)}, bf16[512,512]{1,0:T(8,128)(2,1)S(1)}, u32[]{:S(2)}, u32[]{:S(2)}) collective-permute-start(bf16[512,512]{1,0:T(8,128)(2,1)S(1)} %get-tuple-element.37), channel_id=1, source_target_pairs={{0,16},{16,0},{1,17},{17,1},{2,18},{18,2},{3,19},{19,3},{4,20},{20... | collective-permute-start | bytes 1572872 | tf_op jit(solution)/shard_map/ppermute | solution.py:513
  6.0 24.0 %collective-permute-start.6 = (bf16[1024,256]{1,0:T(8,128)(2,1)S(1)}, bf16[1024,256]{1,0:T(8,128)(2,1)S(1)}, u32[]{:S(2)}, u32[]{:S(2)}) collective-permute-start(bf16[1024,256]{1,0:T(8,128)(2,1)S(1)} %get-tuple-element.38), channel_id=1, source_target_pairs={{0,16},{16,0},{1,17},{17,1},{2,18},{18,2},{3,19},{19,3},{4,20},{20... | collective-permute-start | bytes 1572872 | tf_op jit(solution)/shard_map/ppermute | solution.py:513
  6.1 4.6 %collective-permute-start.2 = (bf16[1,128,512]{2,1,0:T(8,128)(2,1)S(1)}, bf16[1,128,512]{2,1,0:T(8,128)(2,1)S(1)}, u32[]{:S(2)}, u32[]{:S(2)}) collective-permute-start(bf16[1,128,512]{2,1,0:T(8,128)(2,1)S(1)} %get-tuple-element.34), channel_id=1, source_target_pairs={{0,1},{1,2},{2,3},{3,4},{4,5},{5,6},{6,7},{7,8},{8,9},{9,10},{10,1... | collective-permute-start | bytes 393224 | tf_op jit(solution)/shard_map/ppermute | solution.py:516
  7.5 5.2 %collective-permute-start.3 = (bf16[1,128,512]{2,1,0:T(8,128)(2,1)S(1)}, bf16[1,128,512]{2,1,0:T(8,128)(2,1)S(1)}, u32[]{:S(2)}, u32[]{:S(2)}) collective-permute-start(bf16[1,128,512]{2,1,0:T(8,128)(2,1)S(1)} %get-tuple-element.35), channel_id=1, source_target_pairs={{1,0},{2,1},{3,2},{4,3},{5,4},{6,5},{7,6},{8,7},{9,8},{10,9},{11,1... | collective-permute-start | bytes 393224 | tf_op jit(solution)/shard_map/ppermute | solution.py:517
  8.8 46.6 %collective-permute-start = (bf16[512,768]{1,0:T(8,128)(2,1)S(1)}, bf16[512,768]{1,0:T(8,128)(2,1)S(1)}, u32[]{:S(2)}, u32[]{:S(2)}) collective-permute-start(bf16[512,768]{1,0:T(8,128)(2,1)S(1)} %copy-done.2), channel_id=1, source_target_pairs={{0,16},{16,0},{1,17},{17,1},{2,18},{18,2},{3,19},{19,3},{4,20},{20... | collective-permute-start | bytes 2359304 | tf_op jit(solution)/shard_map/ppermute | solution.py:513
  22.1 13.9 %collective-permute-start.5 = (bf16[512,512]{1,0:T(8,128)(2,1)S(1)}, bf16[512,512]{1,0:T(8,128)(2,1)S(1)}, u32[]{:S(2)}, u32[]{:S(2)}) collective-permute-start(bf16[512,512]{1,0:T(8,128)(2,1)S(1)} %collective-permute-done.4.refs_1_), channel_id=1, source_target_pairs={{0,1},{1,0},{2,3},{3,2},{4,5},{5,4},{6,7},{7,6},{8,9},{9,8},{10,11... | collective-permute-start | bytes 1572872 | tf_op jit(solution)/shard_map/ppermute | solution.py:514
  30.0 10.1 %collective-permute-start.7 = (bf16[1024,256]{1,0:T(8,128)(2,1)S(1)}, bf16[1024,256]{1,0:T(8,128)(2,1)S(1)}, u32[]{:S(2)}, u32[]{:S(2)}) collective-permute-start(bf16[1024,256]{1,0:T(8,128)(2,1)S(1)} %collective-permute-done.6.refs_4_), channel_id=1, source_target_pairs={{0,1},{1,0},{2,3},{3,2},{4,5},{5,4},{6,7},{7,6},{8,9},{9,8},{10,11... | collective-permute-start | bytes 1572872 | tf_op jit(solution)/shard_map/ppermute | solution.py:514
  30.0 21.6 %collective-permute-start.1 = (bf16[512,256]{1,0:T(8,128)(2,1)S(1)}, bf16[512,256]{1,0:T(8,128)(2,1)S(1)}, u32[]{:S(2)}, u32[]{:S(2)}) collective-permute-start(bf16[512,256]{1,0:T(8,128)(2,1)S(1)} %copy-done.3), channel_id=1, source_target_pairs={{0,16},{16,0},{1,17},{17,1},{2,18},{18,2},{3,19},{19,3},{4,20},{20... | collective-permute-start | bytes 786440 | tf_op jit(solution)/shard_map/ppermute | solution.py:513
  35.9 4.1 %copy-start = (bf16[2048,256]{1,0:T(8,128)(2,1)S(1)}, bf16[2048,256]{1,0:T(8,128)(2,1)}, u32[]{:S(2)}) copy-start(bf16[2048,256]{1,0:T(8,128)(2,1)} %refs_3_.5) | copy-start | bytes 3145732
  40.1 29.0 %copy-start.6 = (f32[512]{0:T(512)S(1)}, f32[512]{0:T(512)}, u32[]{:S(2)}) copy-start(f32[512]{0:T(512)} %param.20) | copy-start | bytes 6148
  40.1 29.0 %copy-start.7 = (f32[512]{0:T(512)S(1)}, f32[512]{0:T(512)}, u32[]{:S(2)}) copy-start(f32[512]{0:T(512)} %param.21) | copy-start | bytes 6148
  43.1 13.4 %collective-permute-start.10 = (bf16[8,16,512]{2,1,0:T(8,128)(2,1)S(1)}, bf16[8,16,512]{2,1,0:T(8,128)(2,1)S(1)}, u32[]{:S(2)}, u32[]{:S(2)}) collective-permute-start(bf16[8,16,512]{2,1,0:T(8,128)(2,1)S(1)} %get-tuple-element.50), channel_id=1, source_target_pairs={{0,6},{1,7},{2,4},{3,5},{4,2},{5,3},{6,0},{7,1},{8,14},{9,15},{10,... | collective-permute-start | bytes 393224 | tf_op jit(solution)/shard_map/ppermute | solution.py:560
  45.7 18.4 %collective-permute-start.11 = (bf16[8,16,512]{2,1,0:T(8,128)(2,1)S(1)}, bf16[8,16,512]{2,1,0:T(8,128)(2,1)S(1)}, u32[]{:S(2)}, u32[]{:S(2)}) collective-permute-start(bf16[8,16,512]{2,1,0:T(8,128)(2,1)S(1)} %get-tuple-element.51), channel_id=1, source_target_pairs={{0,8},{1,9},{2,10},{3,11},{4,12},{5,13},{6,14},{7,15},{8,0},{9,1},... | collective-permute-start | bytes 393224 | tf_op jit(solution)/shard_map/ppermute | solution.py:560
  48.3 18.0 %collective-permute-start.12 = (bf16[8,16,512]{2,1,0:T(8,128)(2,1)S(1)}, bf16[8,16,512]{2,1,0:T(8,128)(2,1)S(1)}, u32[]{:S(2)}, u32[]{:S(2)}) collective-permute-start(bf16[8,16,512]{2,1,0:T(8,128)(2,1)S(1)} %get-tuple-element.52), channel_id=1, source_target_pairs={{0,10},{1,11},{2,8},{3,9},{4,14},{5,15},{6,12},{7,13},{8,2},{9,3},... | collective-permute-start | bytes 393224 | tf_op jit(solution)/shard_map/ppermute | solution.py:560
  51.6 14.7 %collective-permute-start.13 = (bf16[8,16,512]{2,1,0:T(8,128)(2,1)S(1)}, bf16[8,16,512]{2,1,0:T(8,128)(2,1)S(1)}, u32[]{:S(2)}, u32[]{:S(2)}) collective-permute-start(bf16[8,16,512]{2,1,0:T(8,128)(2,1)S(1)} %get-tuple-element.53), channel_id=1, source_target_pairs={{0,12},{1,13},{2,14},{3,15},{4,8},{5,9},{6,10},{7,11},{8,4},{9,5},... | collective-permute-start | bytes 393224 | tf_op jit(solution)/shard_map/ppermute | solution.py:560
  55.4 10.8 %collective-permute-start.14 = (bf16[8,16,512]{2,1,0:T(8,128)(2,1)S(1)}, bf16[8,16,512]{2,1,0:T(8,128)(2,1)S(1)}, u32[]{:S(2)}, u32[]{:S(2)}) collective-permute-start(bf16[8,16,512]{2,1,0:T(8,128)(2,1)S(1)} %get-tuple-element.54), channel_id=1, source_target_pairs={{0,14},{1,15},{2,12},{3,13},{4,10},{5,11},{6,8},{7,9},{8,6},{9,7},... | collective-permute-start | bytes 393224 | tf_op jit(solution)/shard_map/ppermute | solution.py:560
  56.6 10.3 %collective-permute-start.8 = (bf16[8,16,512]{2,1,0:T(8,128)(2,1)S(1)}, bf16[8,16,512]{2,1,0:T(8,128)(2,1)S(1)}, u32[]{:S(2)}, u32[]{:S(2)}) collective-permute-start(bf16[8,16,512]{2,1,0:T(8,128)(2,1)S(1)} %get-tuple-element.48), channel_id=1, source_target_pairs={{0,2},{1,3},{2,0},{3,1},{4,6},{5,7},{6,4},{7,5},{8,10},{9,11},{10,... | collective-permute-start | bytes 393224 | tf_op jit(solution)/shard_map/ppermute | solution.py:560
  64.1 5.0 %collective-permute-start.9 = (bf16[8,16,512]{2,1,0:T(8,128)(2,1)S(1)}, bf16[8,16,512]{2,1,0:T(8,128)(2,1)S(1)}, u32[]{:S(2)}, u32[]{:S(2)}) collective-permute-start(bf16[8,16,512]{2,1,0:T(8,128)(2,1)S(1)} %get-tuple-element.49), channel_id=1, source_target_pairs={{0,4},{1,5},{2,6},{3,7},{4,0},{5,1},{6,2},{7,3},{8,12},{9,13},{10,... | collective-permute-start | bytes 393224 | tf_op jit(solution)/shard_map/ppermute | solution.py:560
  83.7 8.7 %collective-permute-start.15 = (bf16[8,16,512]{2,1,0:T(8,128)(2,1)S(1)}, bf16[8,16,512]{2,1,0:T(8,128)(2,1)S(1)}, u32[]{:S(2)}, u32[]{:S(2)}) collective-permute-start(bf16[8,16,512]{2,1,0:T(8,128)(2,1)S(1)} %get-tuple-element.56), channel_id=1, source_target_pairs={{0,2},{1,3},{2,0},{3,1},{4,6},{5,7},{6,4},{7,5},{8,10},{9,11},{10,... | collective-permute-start | bytes 393224 | tf_op jit(solution)/shard_map/ppermute | solution.py:560
  84.1 11.6 %collective-permute-start.16 = (bf16[8,16,512]{2,1,0:T(8,128)(2,1)S(1)}, bf16[8,16,512]{2,1,0:T(8,128)(2,1)S(1)}, u32[]{:S(2)}, u32[]{:S(2)}) collective-permute-start(bf16[8,16,512]{2,1,0:T(8,128)(2,1)S(1)} %get-tuple-element.57), channel_id=1, source_target_pairs={{0,4},{1,5},{2,6},{3,7},{4,0},{5,1},{6,2},{7,3},{8,12},{9,13},{10,... | collective-permute-start | bytes 393224 | tf_op jit(solution)/shard_map/ppermute | solution.py:560
  88.5 9.5 %collective-permute-start.17 = (bf16[8,16,512]{2,1,0:T(8,128)(2,1)S(1)}, bf16[8,16,512]{2,1,0:T(8,128)(2,1)S(1)}, u32[]{:S(2)}, u32[]{:S(2)}) collective-permute-start(bf16[8,16,512]{2,1,0:T(8,128)(2,1)S(1)} %get-tuple-element.58), channel_id=1, source_target_pairs={{0,6},{1,7},{2,4},{3,5},{4,2},{5,3},{6,0},{7,1},{8,14},{9,15},{10,... | collective-permute-start | bytes 393224 | tf_op jit(solution)/shard_map/ppermute | solution.py:560
  88.5 9.6 %collective-permute-start.18 = (bf16[8,16,512]{2,1,0:T(8,128)(2,1)S(1)}, bf16[8,16,512]{2,1,0:T(8,128)(2,1)S(1)}, u32[]{:S(2)}, u32[]{:S(2)}) collective-permute-start(bf16[8,16,512]{2,1,0:T(8,128)(2,1)S(1)} %get-tuple-element.59), channel_id=1, source_target_pairs={{0,8},{1,9},{2,10},{3,11},{4,12},{5,13},{6,14},{7,15},{8,0},{9,1},... | collective-permute-start | bytes 393224 | tf_op jit(solution)/shard_map/ppermute | solution.py:560
  91.4 19.2 %collective-permute-start.19 = (bf16[8,16,512]{2,1,0:T(8,128)(2,1)S(1)}, bf16[8,16,512]{2,1,0:T(8,128)(2,1)S(1)}, u32[]{:S(2)}, u32[]{:S(2)}) collective-permute-start(bf16[8,16,512]{2,1,0:T(8,128)(2,1)S(1)} %get-tuple-element.60), channel_id=1, source_target_pairs={{0,10},{1,11},{2,8},{3,9},{4,14},{5,15},{6,12},{7,13},{8,2},{9,3},... | collective-permute-start | bytes 393224 | tf_op jit(solution)/shard_map/ppermute | solution.py:560
  92.4 18.3 %collective-permute-start.20 = (bf16[8,16,512]{2,1,0:T(8,128)(2,1)S(1)}, bf16[8,16,512]{2,1,0:T(8,128)(2,1)S(1)}, u32[]{:S(2)}, u32[]{:S(2)}) collective-permute-start(bf16[8,16,512]{2,1,0:T(8,128)(2,1)S(1)} %get-tuple-element.61), channel_id=1, source_target_pairs={{0,12},{1,13},{2,14},{3,15},{4,8},{5,9},{6,10},{7,11},{8,4},{9,5},... | collective-permute-start | bytes 393224 | tf_op jit(solution)/shard_map/ppermute | solution.py:560
  95.7 15.0 %collective-permute-start.21 = (bf16[8,16,512]{2,1,0:T(8,128)(2,1)S(1)}, bf16[8,16,512]{2,1,0:T(8,128)(2,1)S(1)}, u32[]{:S(2)}, u32[]{:S(2)}) collective-permute-start(bf16[8,16,512]{2,1,0:T(8,128)(2,1)S(1)} %get-tuple-element.62), channel_id=1, source_target_pairs={{0,14},{1,15},{2,12},{3,13},{4,10},{5,11},{6,8},{7,9},{8,6},{9,7},... | collective-permute-start | bytes 393224 | tf_op jit(solution)/shard_map/ppermute | solution.py:560

commit v4 on v3

--- a/solution.py
+++ b/solution.py
@@ -11,6 +11,8 @@
 HD = 32
 GRID = 8
 CHUNKS = 1
+BATCH = 2
+STRIPS = 2
 SPLIT = (True,)
 ORDER = (4, 6, 5, 7, 2, 3, 1)
 ROOT = math.sqrt(2.0 / math.pi)
@@ -178,11 +180,14 @@
     half_taps = 0.5 * taps[:, :, tile]
     half_tap_bias = 0.5 * tap_bias[:, tile]
     lane = lax.broadcasted_iota(jnp.int32, (GRID, width), 0)
-    batch = (rows + 2) // 2
-    for row in range(0, rows + 2, batch):
-        tokens = normed[row : row + batch].reshape(batch * cols, -1)
-        raw[row * cols : (row + batch) * cols, :] = dot(tokens, weight)
-    for row in range(rows + 2):
+    strip = cols // STRIPS
+    blocks = [slice(lane, lane + 128) for lane in range(0, width, 128)]
+
+    def product(row):
+        tokens = normed[row : row + BATCH].reshape(BATCH * cols, -1)
+        raw[row * cols : (row + BATCH) * cols, :] = dot(tokens, weight)
+
+    def activate(row):
         value = half_gelu(raw[row * cols : (row + 1) * cols, :] + half_bias)
         if row == 0:
             value = value * jnp.where(info[SPACE] > 0, 1.0, 0.0)
@@ -195,16 +200,29 @@
         wide[row, GRID + cols :, :] = jnp.where(
             lane == GRID - 1, 0.0, pltpu.roll(head, GRID - 1, 0)
         )
-        if row >= 2:
-            total = half_tap_bias
-            for row_off in range(3):
+
+    def convolve(row):
+        for lanes in blocks:
+            for start in range(0, cols, strip):
+                near = [
+                    wide[row + off, start : start + strip + 2 * GRID, lanes] for off in range(3)
+                ]
+                total = half_tap_bias[:, lanes]
                 for col_off in range(3):
-                    total = (
-                        total
-                        + wide[row - 2 + row_off, GRID * col_off : GRID * col_off + cols, :]
-                        * half_taps[row_off, col_off][None]
-                    )
-            out[(row - 2) * cols : (row - 1) * cols, :] = half_gelu(total).astype(BF16)
+                    for row_off in range(3):
+                        part = near[row_off][GRID * col_off : GRID * col_off + strip]
+                        total = total + part * half_taps[row_off, col_off, lanes][None]
+                at = row * cols + start
+                out[at : at + strip, lanes] = half_gelu(total).astype(BF16)
+
+    product(0)
+    for first_row in range(0, rows + 2, BATCH):
+        if first_row + BATCH < rows + 2:
+            product(first_row + BATCH)
+        for row in range(first_row, first_row + BATCH):
+            activate(row)
+            if row >= 2:
+                convolve(row - 2)
 
 
 def expand_some(info, sources, weight, bias, taps, tap_bias, tile_of, first):
@@ -344,11 +362,11 @@
     take = lambda n: [refs.pop(0) for _ in range(n)]
     qkv_pieces, out_pieces = take(pieces), take(pieces)
     tokens, outs = take(blocks), take(blocks)
-    lned, triple, mixed, resid = refs
+    lned, triple, mixed, resid, soft = refs
     count, size, chans = tokens[0].shape[-3:]
     wins = size // GRID
     length = GRID * GRID
-    group = min(256, chans)
+    group = min(128, chans)
     heads = group // HD
     keys = heads * length
 
@@ -378,25 +396,30 @@
     spread_mask = same((keys, group), length, HD)
     sum_mask = same((256, 256), length, length)
     factor = math.log2(math.e) / math.sqrt(HD)
-    for win in range(count * wins):
-        at = slice(win * length, (win + 1) * length)
-        for g in range(chans // group):
-            cols = slice(g * group, (g + 1) * group)
-            query = triple[at, cols]
-            key = triple[at, chans + g * group : chans + (g + 1) * group]
-            value = triple[at, 2 * chans + g * group : 2 * chans + (g + 1) * group]
-            key_wide = jnp.concatenate([key] * heads, axis=0) * spread_mask
-            value_wide = jnp.concatenate([value] * heads, axis=0) * spread_mask
-            scores = lax.dot_general(
-                query, key_wide, (((1,), (1,)), ((), ())), preferred_element_type=F32
-            )
-            exponent = jnp.minimum(jnp.exp2(scores * factor), 3.3895e38)
-            rounded = exponent.astype(BF16)
-            sums = jnp.concatenate(
-                [dot(rounded[:, n : n + 256], sum_mask) for n in range(0, keys, 256)], axis=1
-            )
-            soft = (exponent / sums).astype(BF16)
-            mixed[at, cols] = dot(soft, value_wide).astype(BF16)
+    each = [(win, g) for win in range(count * wins) for g in range(chans // group)]
+    spot = lambda win, g: (
+        slice(win * length, (win + 1) * length),
+        slice(g * keys, (g + 1) * keys),
+    )
+    for win, g in each:
+        at, lanes = spot(win, g)
+        query = triple[at, g * group : (g + 1) * group]
+        key = triple[at, chans + g * group : chans + (g + 1) * group]
+        key_wide = jnp.concatenate([key] * heads, axis=0) * spread_mask
+        scores = lax.dot_general(
+            query, key_wide, (((1,), (1,)), ((), ())), preferred_element_type=F32
+        )
+        soft[at, lanes] = jnp.minimum(jnp.exp2(scores * factor), 3.3895e38).astype(BF16)
+    for start in range(0, count * wins * length, 256):
+        for lane in range(0, soft.shape[1], 256):
+            at, lanes = slice(start, start + 256), slice(lane, lane + 256)
+            exponent = soft[at, lanes]
+            soft[at, lanes] = (exponent.astype(F32) / dot(exponent, sum_mask)).astype(BF16)
+    for win, g in each:
+        at, lanes = spot(win, g)
+        value = triple[at, 2 * chans + g * group : 2 * chans + (g + 1) * group]
+        value_wide = jnp.concatenate([value] * heads, axis=0) * spread_mask
+        mixed[at, g * group : (g + 1) * group] = dot(soft[at, lanes], value_wide).astype(BF16)
 
     def put_out(start, width, product):
         span = pl.ds(start, width)
@@ -425,6 +448,7 @@
             pltpu.VMEM((total, 3 * chans), BF16),
             pltpu.VMEM((total, chans), BF16),
             pltpu.VMEM((total, chans), F32),
+            pltpu.VMEM((total, chans // HD * GRID * GRID), BF16),
         ],
         compiler_params=params(),
         cost_estimate=cost(),

time: 115 us -> 107 us (0.930)
  Pallas kernels: 39.7 us -> 31.4 us
    pallas_call x1, Pallas kernels: 14.6 us -> 6.93 us  [attend(): pl.pallas_call(functools.partial(attend_kernel, len(w_qkv), len(tokens)),...]
    ppermute x14, waiting for transfers between devices: 26.8 us -> 25.5 us  [exchange(): parts[k] = lax.ppermute(parts[k], 'space', pairs_k)]
  transfers between devices with their start and end apart: 22 -> 22, of which waited for: 11 -> 10; matrix products, arithmetic and copies ran while one was open for 0% -> 0% of each run, Pallas kernels for 18% -> 19%
where the time goes in v4:
time: 107 us; the launch traced here: 105 us
  starting transfers between devices  37.7 us (35%)
  waiting for transfers between devices  35.2 us (33%)
  Pallas kernels  31.4 us (29%)
    ppermute x14, waiting for transfers between devices, exchange(): parts[k] = lax.ppermute(parts[k], 'space', pairs_k)  25.5 us
    ppermute x14, starting transfers between devices, exchange(): parts[k] = lax.ppermute(parts[k], 'space', pairs_k)  24.1 us
    pallas_call x3, Pallas kernels, expand_some(): pl.pallas_call(functools.partial(expand_kernel, first, tile_of), grid_spe...  16.6 us
    ppermute x4, waiting for transfers between devices, local(): over_dp = lambda w: lax.ppermute(w, 'dp', [(0, 1), (1, 0)])  7.67 us
    ppermute x4, starting transfers between devices, local(): over_dp = lambda w: lax.ppermute(w, 'dp', [(0, 1), (1, 0)])  7.01 us
    pallas_call x1, Pallas kernels, attend(): pl.pallas_call(functools.partial(attend_kernel, len(w_qkv), len(tokens)),...  6.93 us
    ppermute x2, starting transfers between devices, local(): lax.ppermute(w, 'space', [(i, i ^ 1) for i in range(space)])  3.88 us
    pallas_call x1, Pallas kernels, project_rows(): pl.pallas_call(functools.partial(project_kernel, len(weights), split), gr...  3.06 us
  transfers between devices with their start and end apart: 22, of which 10 were waited for; matrix products, arithmetic and copies ran while one was open for 0% of the time, Pallas kernels for 19%

profile of v4, /device:TPU:0, one launch (start us, length us, event | category | flops | bytes accessed | tf_op | source)
XLA Modules:
  0.0 104.7 jit_solution(3610646708809944936)
XLA Ops:
  0.0 1.1 %edge_rows.1 = (bf16[1,128,512]{2,1,0:T(8,128)(2,1)S(1)}, bf16[1,128,512]{2,1,0:T(8,128)(2,1)S(1)}) custom-call(bf16[8,128,512]{2,1,0:T(8,128)(2,1)} %bitcast.19), custom_call_target="tpu_custom_call" | custom-call | tf_op jit(solution)/shard_map/edge_rows/pallas_call | solution.py:93
  1.2 1.8 %share_weights.1 = (bf16[512,512]{1,0:T(8,128)(2,1)S(1)}, bf16[1024,256]{1,0:T(8,128)(2,1)S(1)}) custom-call(s32[5]{0:T(128)S(1)} %stack.15.info, bf16[512,1024]{1,0:T(8,128)(2,1)} %refs_5_.1, bf16[2048,256]{1,0:T(8,128)(2,1)} %refs_3_.5), custom_call_target="tpu_custom_call" | custom-call | tf_op jit(solution)/shard_map/share_weights/pallas_call | solution.py:122
  3.0 3.0 %collective-permute-start.4 = (bf16[512,512]{1,0:T(8,128)(2,1)S(1)}, bf16[512,512]{1,0:T(8,128)(2,1)S(1)}, u32[]{:S(2)}, u32[]{:S(2)}) collective-permute-start(bf16[512,512]{1,0:T(8,128)(2,1)S(1)} %get-tuple-element.37), channel_id=1, source_target_pairs={{0,16},{16,0},{1,17},{17,1},{2,18},{18,2},{3,19},{19,3},{4,20},{20... | collective-permute-start | bytes 1572872 | tf_op jit(solution)/shard_map/ppermute | solution.py:537
  6.1 1.5 %collective-permute-start.2 = (bf16[1,128,512]{2,1,0:T(8,128)(2,1)S(1)}, bf16[1,128,512]{2,1,0:T(8,128)(2,1)S(1)}, u32[]{:S(2)}, u32[]{:S(2)}) collective-permute-start(bf16[1,128,512]{2,1,0:T(8,128)(2,1)S(1)} %get-tuple-element.34), channel_id=1, source_target_pairs={{0,1},{1,2},{2,3},{3,4},{4,5},{5,6},{6,7},{7,8},{8,9},{9,10},{10,1... | collective-permute-start | bytes 393224 | tf_op jit(solution)/shard_map/ppermute | solution.py:540
  7.5 1.3 %collective-permute-start.3 = (bf16[1,128,512]{2,1,0:T(8,128)(2,1)S(1)}, bf16[1,128,512]{2,1,0:T(8,128)(2,1)S(1)}, u32[]{:S(2)}, u32[]{:S(2)}) collective-permute-start(bf16[1,128,512]{2,1,0:T(8,128)(2,1)S(1)} %get-tuple-element.35), channel_id=1, source_target_pairs={{1,0},{2,1},{3,2},{4,3},{5,4},{6,5},{7,6},{8,7},{9,8},{10,9},{11,1... | collective-permute-start | bytes 393224 | tf_op jit(solution)/shard_map/ppermute | solution.py:541
  8.8 1.8 %collective-permute-start = (bf16[512,768]{1,0:T(8,128)(2,1)S(1)}, bf16[512,768]{1,0:T(8,128)(2,1)S(1)}, u32[]{:S(2)}, u32[]{:S(2)}) collective-permute-start(bf16[512,768]{1,0:T(8,128)(2,1)S(1)} %copy-done.2), channel_id=1, source_target_pairs={{0,16},{16,0},{1,17},{17,1},{2,18},{18,2},{3,19},{19,3},{4,20},{20... | collective-permute-start | bytes 2359304 | tf_op jit(solution)/shard_map/ppermute | solution.py:537
  10.7 2.1 %collective-permute-done.3.refs_2_ = bf16[1,128,512]{2,1,0:T(8,128)(2,1)S(1)} collective-permute-done((bf16[1,128,512]{2,1,0:T(8,128)(2,1)S(1)}, bf16[1,128,512]{2,1,0:T(8,128)(2,1)S(1)}, u32[]{:S(2)}, u32[]{:S(2)}) %collective-permute-start.3) | collective-permute-done | bytes 131104 | tf_op jit(solution)/shard_map/ppermute | solution.py:541
  12.7 9.0 %expand_conv.3 = (bf16[1024,1024]{1,0:T(8,128)(2,1)S(1)}, bf16[8,128,512]{2,1,0:T(8,128)(2,1)S(1)}, bf16[10,128,512]{2,1,0:T(8,128)(2,1)S(1)}) custom-call(s32[5]{0:T(128)S(1)} %stack.15.info, bf16[8,128,512]{2,1,0:T(8,128)(2,1)} %bitcast.20, bf16[1,128,512]{2,1,0:T(8,128)(2,1)S(1)} %collective-permute-done.2.refs_1_, ...), custom_call_target="tpu_custom_call" | custom-call | flops 1 | bytes 1 | tf_op jit(solution)/shard_map/expand_conv/pallas_call | solution.py:259
  21.8 3.9 %collective-permute-start.5 = (bf16[512,512]{1,0:T(8,128)(2,1)S(1)}, bf16[512,512]{1,0:T(8,128)(2,1)S(1)}, u32[]{:S(2)}, u32[]{:S(2)}) collective-permute-start(bf16[512,512]{1,0:T(8,128)(2,1)S(1)} %collective-permute-done.4.refs_1_), channel_id=1, source_target_pairs={{0,1},{1,0},{2,3},{3,2},{4,5},{5,4},{6,7},{7,6},{8,9},{9,8},{10,11... | collective-permute-start | bytes 1572872 | tf_op jit(solution)/shard_map/ppermute | solution.py:538
  25.6 4.3 %collective-permute-done.6.refs_4_ = bf16[1024,256]{1,0:T(8,128)(2,1)S(1)} collective-permute-done((bf16[1024,256]{1,0:T(8,128)(2,1)S(1)}, bf16[1024,256]{1,0:T(8,128)(2,1)S(1)}, u32[]{:S(2)}, u32[]{:S(2)}) %collective-permute-start.6) | collective-permute-done | bytes 524320 | tf_op jit(solution)/shard_map/ppermute | solution.py:537
  30.0 2.1 %collective-permute-start.1 = (bf16[512,256]{1,0:T(8,128)(2,1)S(1)}, bf16[512,256]{1,0:T(8,128)(2,1)S(1)}, u32[]{:S(2)}, u32[]{:S(2)}) collective-permute-start(bf16[512,256]{1,0:T(8,128)(2,1)S(1)} %copy-done.3), channel_id=1, source_target_pairs={{0,16},{16,0},{1,17},{17,1},{2,18},{18,2},{3,19},{19,3},{4,20},{20... | collective-permute-start | bytes 786440 | tf_op jit(solution)/shard_map/ppermute | solution.py:537
  32.0 3.7 %expand_conv.4.refs_1_ = bf16[1024,512]{1,0:T(8,128)(2,1)S(1)} custom-call(s32[5]{0:T(128)S(1)} %stack.15.info, bf16[10,128,512]{2,1,0:T(8,128)(2,1)S(1)} %get-tuple-element.44.refs_0_, bf16[512,512]{1,0:T(8,128)(2,1)S(1)} %collective-permute-done.4.refs_1_, f32[1,2048]{1,0:T(1,128)S(1)} %bitcast.12, f32[3,3,2048]{2,1,0:T(4,128)S(1)} %copy-done.1, ...), custom_call_target="tpu_custom_call" | custom-call | flops 1 | bytes 1 | tf_op jit(solution)/shard_map/expand_conv/pallas_call | solution.py:259
  35.8 3.9 %expand_conv.5.refs_2_ = bf16[1024,512]{1,0:T(8,128)(2,1)S(1)} custom-call(s32[5]{0:T(128)S(1)} %stack.15.info, bf16[10,128,512]{2,1,0:T(8,128)(2,1)S(1)} %get-tuple-element.44.refs_0_, bf16[512,512]{1,0:T(8,128)(2,1)S(1)} %collective-permute-done.5.refs_1_, f32[1,2048]{1,0:T(1,128)S(1)} %bitcast.13, f32[3,3,2048]{2,1,0:T(4,128)S(1)} %copy-done.1, ...), custom_call_target="tpu_custom_call" | custom-call | flops 1 | bytes 1 | tf_op jit(solution)/shard_map/expand_conv/pallas_call | solution.py:259
  39.7 3.1 %project_rows.1 = (bf16[8,16,512]{2,1,0:T(8,128)(2,1)S(1)}, bf16[8,16,512]{2,1,0:T(8,128)(2,1)S(1)}, bf16[8,16,512]{2,1,0:T(8,128)(2,1)S(1)}, bf16[8,16,512]{2,1...) custom-call(s32[5]{0:T(128)S(1)} %stack.15.info, ...), custom_call_target="tpu_custom_call" | custom-call | flops 1 | bytes 1 | tf_op jit(solution)/shard_map/project_rows/pallas_call | solution.py:342
  42.8 2.6 %collective-permute-start.10 = (bf16[8,16,512]{2,1,0:T(8,128)(2,1)S(1)}, bf16[8,16,512]{2,1,0:T(8,128)(2,1)S(1)}, u32[]{:S(2)}, u32[]{:S(2)}) collective-permute-start(bf16[8,16,512]{2,1,0:T(8,128)(2,1)S(1)} %get-tuple-element.50), channel_id=1, source_target_pairs={{0,6},{1,7},{2,4},{3,5},{4,2},{5,3},{6,0},{7,1},{8,14},{9,15},{10,... | collective-permute-start | bytes 393224 | tf_op jit(solution)/shard_map/ppermute | solution.py:584
  45.4 2.6 %collective-permute-start.11 = (bf16[8,16,512]{2,1,0:T(8,128)(2,1)S(1)}, bf16[8,16,512]{2,1,0:T(8,128)(2,1)S(1)}, u32[]{:S(2)}, u32[]{:S(2)}) collective-permute-start(bf16[8,16,512]{2,1,0:T(8,128)(2,1)S(1)} %get-tuple-element.51), channel_id=1, source_target_pairs={{0,8},{1,9},{2,10},{3,11},{4,12},{5,13},{6,14},{7,15},{8,0},{9,1},... | collective-permute-start | bytes 393224 | tf_op jit(solution)/shard_map/ppermute | solution.py:584
  48.3 3.3 %collective-permute-done.1.refs_3_ = bf16[512,256]{1,0:T(8,128)(2,1)S(1)} collective-permute-done((bf16[512,256]{1,0:T(8,128)(2,1)S(1)}, bf16[512,256]{1,0:T(8,128)(2,1)S(1)}, u32[]{:S(2)}, u32[]{:S(2)}) %collective-permute-start.1) | collective-permute-done | bytes 262176 | tf_op jit(solution)/shard_map/ppermute | solution.py:537
  51.6 3.8 %collective-permute-start.13 = (bf16[8,16,512]{2,1,0:T(8,128)(2,1)S(1)}, bf16[8,16,512]{2,1,0:T(8,128)(2,1)S(1)}, u32[]{:S(2)}, u32[]{:S(2)}) collective-permute-start(bf16[8,16,512]{2,1,0:T(8,128)(2,1)S(1)} %get-tuple-element.53), channel_id=1, source_target_pairs={{0,12},{1,13},{2,14},{3,15},{4,8},{5,9},{6,10},{7,11},{8,4},{9,5},... | collective-permute-start | bytes 393224 | tf_op jit(solution)/shard_map/ppermute | solution.py:584
  55.4 1.1 %collective-permute-start.14 = (bf16[8,16,512]{2,1,0:T(8,128)(2,1)S(1)}, bf16[8,16,512]{2,1,0:T(8,128)(2,1)S(1)}, u32[]{:S(2)}, u32[]{:S(2)}) collective-permute-start(bf16[8,16,512]{2,1,0:T(8,128)(2,1)S(1)} %get-tuple-element.54), channel_id=1, source_target_pairs={{0,14},{1,15},{2,12},{3,13},{4,10},{5,11},{6,8},{7,9},{8,6},{9,7},... | collective-permute-start | bytes 393224 | tf_op jit(solution)/shard_map/ppermute | solution.py:584
  57.0 5.8 %collective-permute-done.11.refs_8_ = bf16[8,16,512]{2,1,0:T(8,128)(2,1)S(1)} collective-permute-done((bf16[8,16,512]{2,1,0:T(8,128)(2,1)S(1)}, bf16[8,16,512]{2,1,0:T(8,128)(2,1)S(1)}, u32[]{:S(2)}, u32[]{:S(2)}) %collective-permute-start.11) | collective-permute-done | bytes 131104 | tf_op jit(solution)/shard_map/ppermute | solution.py:584
  63.4 2.5 %collective-permute-done.12.refs_9_ = bf16[8,16,512]{2,1,0:T(8,128)(2,1)S(1)} collective-permute-done((bf16[8,16,512]{2,1,0:T(8,128)(2,1)S(1)}, bf16[8,16,512]{2,1,0:T(8,128)(2,1)S(1)}, u32[]{:S(2)}, u32[]{:S(2)}) %collective-permute-start.12) | collective-permute-done | bytes 131104 | tf_op jit(solution)/shard_map/ppermute | solution.py:584
  66.9 1.7 %collective-permute-done.9.refs_6_ = bf16[8,16,512]{2,1,0:T(8,128)(2,1)S(1)} collective-permute-done((bf16[8,16,512]{2,1,0:T(8,128)(2,1)S(1)}, bf16[8,16,512]{2,1,0:T(8,128)(2,1)S(1)}, u32[]{:S(2)}, u32[]{:S(2)}) %collective-permute-start.9) | collective-permute-done | bytes 131104 | tf_op jit(solution)/shard_map/ppermute | solution.py:584
  68.5 6.9 %attend.1 = (bf16[8,16,512]{2,1,0:T(8,128)(2,1)S(1)}, bf16[8,16,512]{2,1,0:T(8,128)(2,1)S(1)}, bf16[8,16,512]{2,1,0:T(8,128)(2,1)S(1)}, bf16[8,16,512]{2,1,0:T(8...) custom-call(s32[5]{0:T(128)S(1)} %stack.15.info, ...), custom_call_target="tpu_custom_call" | custom-call | flops 1 | bytes 1 | tf_op jit(solution)/shard_map/attend/pallas_call | solution.py:441
  76.1 4.4 %collective-permute-start.16 = (bf16[8,16,512]{2,1,0:T(8,128)(2,1)S(1)}, bf16[8,16,512]{2,1,0:T(8,128)(2,1)S(1)}, u32[]{:S(2)}, u32[]{:S(2)}) collective-permute-start(bf16[8,16,512]{2,1,0:T(8,128)(2,1)S(1)} %get-tuple-element.57), channel_id=1, source_target_pairs={{0,4},{1,5},{2,6},{3,7},{4,0},{5,1},{6,2},{7,3},{8,12},{9,13},{10,... | collective-permute-start | bytes 393224 | tf_op jit(solution)/shard_map/ppermute | solution.py:584
  80.5 3.0 %collective-permute-start.18 = (bf16[8,16,512]{2,1,0:T(8,128)(2,1)S(1)}, bf16[8,16,512]{2,1,0:T(8,128)(2,1)S(1)}, u32[]{:S(2)}, u32[]{:S(2)}) collective-permute-start(bf16[8,16,512]{2,1,0:T(8,128)(2,1)S(1)} %get-tuple-element.59), channel_id=1, source_target_pairs={{0,8},{1,9},{2,10},{3,11},{4,12},{5,13},{6,14},{7,15},{8,0},{9,1},... | collective-permute-start | bytes 393224 | tf_op jit(solution)/shard_map/ppermute | solution.py:584
  83.5 0.9 collective-permute-start.19
  84.4 2.4 %collective-permute-start.20 = (bf16[8,16,512]{2,1,0:T(8,128)(2,1)S(1)}, bf16[8,16,512]{2,1,0:T(8,128)(2,1)S(1)}, u32[]{:S(2)}, u32[]{:S(2)}) collective-permute-start(bf16[8,16,512]{2,1,0:T(8,128)(2,1)S(1)} %get-tuple-element.61), channel_id=1, source_target_pairs={{0,12},{1,13},{2,14},{3,15},{4,8},{5,9},{6,10},{7,11},{8,4},{9,5},... | collective-permute-start | bytes 393224 | tf_op jit(solution)/shard_map/ppermute | solution.py:584
  86.8 0.9 collective-permute-done.16.refs_2_
  87.7 1.4 %collective-permute-start.21 = (bf16[8,16,512]{2,1,0:T(8,128)(2,1)S(1)}, bf16[8,16,512]{2,1,0:T(8,128)(2,1)S(1)}, u32[]{:S(2)}, u32[]{:S(2)}) collective-permute-start(bf16[8,16,512]{2,1,0:T(8,128)(2,1)S(1)} %get-tuple-element.62), channel_id=1, source_target_pairs={{0,14},{1,15},{2,12},{3,13},{4,10},{5,11},{6,8},{7,9},{8,6},{9,7},... | collective-permute-start | bytes 393224 | tf_op jit(solution)/shard_map/ppermute | solution.py:584
  89.0 1.1 %collective-permute-done.17.refs_3_ = bf16[8,16,512]{2,1,0:T(8,128)(2,1)S(1)} collective-permute-done((bf16[8,16,512]{2,1,0:T(8,128)(2,1)S(1)}, bf16[8,16,512]{2,1,0:T(8,128)(2,1)S(1)}, u32[]{:S(2)}, u32[]{:S(2)}) %collective-permute-start.17) | collective-permute-done | bytes 131104 | tf_op jit(solution)/shard_map/ppermute | solution.py:584
  90.1 12.6 %collective-permute-done.19.refs_5_ = bf16[8,16,512]{2,1,0:T(8,128)(2,1)S(1)} collective-permute-done((bf16[8,16,512]{2,1,0:T(8,128)(2,1)S(1)}, bf16[8,16,512]{2,1,0:T(8,128)(2,1)S(1)}, u32[]{:S(2)}, u32[]{:S(2)}) %collective-permute-start.19) | collective-permute-done | bytes 131104 | tf_op jit(solution)/shard_map/ppermute | solution.py:584
  102.7 2.0 %restore_rows.1 = bf16[8,128,512]{2,1,0:T(8,128)(2,1)} custom-call(s32[5]{0:T(128)S(1)} %stack.15.info, bf16[8,16,512]{2,1,0:T(8,128)(2,1)S(1)} %get-tuple-element.55.refs_0_, bf16[8,16,512]{2,1,0:T(8,128)(2,1)S(1)} %collective-permute-done.15.refs_1_, bf16[8,16,512]{2,1,0:T(8,128)(2,1)S(1)} %collective-permute-done.16.refs_2_, ...), custom_call_target="tpu_custom_call" | custom-call | flops 1 | bytes 1 | tf_op jit(solution)/shard_map/restore_rows/pallas_call | solution.py:486
  (37 shorter events, 3.1 us)
Async XLA Ops:
  0.0 8.8 %copy-start.2 = (bf16[512,768]{1,0:T(8,128)(2,1)S(1)}, bf16[512,768]{1,0:T(8,128)(2,1)}, u32[]{:S(2)}) copy-start(bf16[512,768]{1,0:T(8,128)(2,1)} %refs_0_.1) | copy-start | bytes 2359300
  1.2 28.8 %copy-start.3 = (bf16[512,256]{1,0:T(8,128)(2,1)S(1)}, bf16[512,256]{1,0:T(8,128)(2,1)}, u32[]{:S(2)}) copy-start(bf16[512,256]{1,0:T(8,128)(2,1)} %refs_2_.1) | copy-start | bytes 786436
  1.2 30.9 %copy-start.1 = (f32[3,3,2048]{2,1,0:T(4,128)S(1)}, f32[3,3,2048]{2,1,0:T(4,128)}, u32[]{:S(2)}) copy-start(f32[3,3,2048]{2,1,0:T(4,128)} %refs_3_.4) | copy-start | bytes 221188
  1.2 30.9 %copy-start.4 = (f32[2048]{0:T(1024)S(1)}, f32[2048]{0:T(1024)}, u32[]{:S(2)}) copy-start(f32[2048]{0:T(1024)} %param.16) | copy-start | bytes 24580
  1.2 30.9 %copy-start.5 = (f32[2048]{0:T(1024)S(1)}, f32[2048]{0:T(1024)}, u32[]{:S(2)}) copy-start(f32[2048]{0:T(1024)} %param.18) | copy-start | bytes 24580
  3.0 18.8 %collective-permute-start.4 = (bf16[512,512]{1,0:T(8,128)(2,1)S(1)}, bf16[512,512]{1,0:T(8,128)(2,1)S(1)}, u32[]{:S(2)}, u32[]{:S(2)}) collective-permute-start(bf16[512,512]{1,0:T(8,128)(2,1)S(1)} %get-tuple-element.37), channel_id=1, source_target_pairs={{0,16},{16,0},{1,17},{17,1},{2,18},{18,2},{3,19},{19,3},{4,20},{20... | collective-permute-start | bytes 1572872 | tf_op jit(solution)/shard_map/ppermute | solution.py:537
  6.0 24.0 %collective-permute-start.6 = (bf16[1024,256]{1,0:T(8,128)(2,1)S(1)}, bf16[1024,256]{1,0:T(8,128)(2,1)S(1)}, u32[]{:S(2)}, u32[]{:S(2)}) collective-permute-start(bf16[1024,256]{1,0:T(8,128)(2,1)S(1)} %get-tuple-element.38), channel_id=1, source_target_pairs={{0,16},{16,0},{1,17},{17,1},{2,18},{18,2},{3,19},{19,3},{4,20},{20... | collective-permute-start | bytes 1572872 | tf_op jit(solution)/shard_map/ppermute | solution.py:537
  6.1 4.6 %collective-permute-start.2 = (bf16[1,128,512]{2,1,0:T(8,128)(2,1)S(1)}, bf16[1,128,512]{2,1,0:T(8,128)(2,1)S(1)}, u32[]{:S(2)}, u32[]{:S(2)}) collective-permute-start(bf16[1,128,512]{2,1,0:T(8,128)(2,1)S(1)} %get-tuple-element.34), channel_id=1, source_target_pairs={{0,1},{1,2},{2,3},{3,4},{4,5},{5,6},{6,7},{7,8},{8,9},{9,10},{10,1... | collective-permute-start | bytes 393224 | tf_op jit(solution)/shard_map/ppermute | solution.py:540
  7.5 5.2 %collective-permute-start.3 = (bf16[1,128,512]{2,1,0:T(8,128)(2,1)S(1)}, bf16[1,128,512]{2,1,0:T(8,128)(2,1)S(1)}, u32[]{:S(2)}, u32[]{:S(2)}) collective-permute-start(bf16[1,128,512]{2,1,0:T(8,128)(2,1)S(1)} %get-tuple-element.35), channel_id=1, source_target_pairs={{1,0},{2,1},{3,2},{4,3},{5,4},{6,5},{7,6},{8,7},{9,8},{10,9},{11,1... | collective-permute-start | bytes 393224 | tf_op jit(solution)/shard_map/ppermute | solution.py:541
  8.8 46.6 %collective-permute-start = (bf16[512,768]{1,0:T(8,128)(2,1)S(1)}, bf16[512,768]{1,0:T(8,128)(2,1)S(1)}, u32[]{:S(2)}, u32[]{:S(2)}) collective-permute-start(bf16[512,768]{1,0:T(8,128)(2,1)S(1)} %copy-done.2), channel_id=1, source_target_pairs={{0,16},{16,0},{1,17},{17,1},{2,18},{18,2},{3,19},{19,3},{4,20},{20... | collective-permute-start | bytes 2359304 | tf_op jit(solution)/shard_map/ppermute | solution.py:537
  21.8 14.0 %collective-permute-start.5 = (bf16[512,512]{1,0:T(8,128)(2,1)S(1)}, bf16[512,512]{1,0:T(8,128)(2,1)S(1)}, u32[]{:S(2)}, u32[]{:S(2)}) collective-permute-start(bf16[512,512]{1,0:T(8,128)(2,1)S(1)} %collective-permute-done.4.refs_1_), channel_id=1, source_target_pairs={{0,1},{1,0},{2,3},{3,2},{4,5},{5,4},{6,7},{7,6},{8,9},{9,8},{10,11... | collective-permute-start | bytes 1572872 | tf_op jit(solution)/shard_map/ppermute | solution.py:538
  30.0 9.7 %collective-permute-start.7 = (bf16[1024,256]{1,0:T(8,128)(2,1)S(1)}, bf16[1024,256]{1,0:T(8,128)(2,1)S(1)}, u32[]{:S(2)}, u32[]{:S(2)}) collective-permute-start(bf16[1024,256]{1,0:T(8,128)(2,1)S(1)} %collective-permute-done.6.refs_4_), channel_id=1, source_target_pairs={{0,1},{1,0},{2,3},{3,2},{4,5},{5,4},{6,7},{7,6},{8,9},{9,8},{10,11... | collective-permute-start | bytes 1572872 | tf_op jit(solution)/shard_map/ppermute | solution.py:538
  30.0 21.6 %collective-permute-start.1 = (bf16[512,256]{1,0:T(8,128)(2,1)S(1)}, bf16[512,256]{1,0:T(8,128)(2,1)S(1)}, u32[]{:S(2)}, u32[]{:S(2)}) collective-permute-start(bf16[512,256]{1,0:T(8,128)(2,1)S(1)} %copy-done.3), channel_id=1, source_target_pairs={{0,16},{16,0},{1,17},{17,1},{2,18},{18,2},{3,19},{19,3},{4,20},{20... | collective-permute-start | bytes 786440 | tf_op jit(solution)/shard_map/ppermute | solution.py:537
  35.8 3.9 %copy-start = (bf16[2048,256]{1,0:T(8,128)(2,1)S(1)}, bf16[2048,256]{1,0:T(8,128)(2,1)}, u32[]{:S(2)}) copy-start(bf16[2048,256]{1,0:T(8,128)(2,1)} %refs_3_.5) | copy-start | bytes 3145732
  39.7 28.8 %copy-start.6 = (f32[512]{0:T(512)S(1)}, f32[512]{0:T(512)}, u32[]{:S(2)}) copy-start(f32[512]{0:T(512)} %param.20) | copy-start | bytes 6148
  39.7 28.8 %copy-start.7 = (f32[512]{0:T(512)S(1)}, f32[512]{0:T(512)}, u32[]{:S(2)}) copy-start(f32[512]{0:T(512)} %param.21) | copy-start | bytes 6148
  42.8 13.8 %collective-permute-start.10 = (bf16[8,16,512]{2,1,0:T(8,128)(2,1)S(1)}, bf16[8,16,512]{2,1,0:T(8,128)(2,1)S(1)}, u32[]{:S(2)}, u32[]{:S(2)}) collective-permute-start(bf16[8,16,512]{2,1,0:T(8,128)(2,1)S(1)} %get-tuple-element.50), channel_id=1, source_target_pairs={{0,6},{1,7},{2,4},{3,5},{4,2},{5,3},{6,0},{7,1},{8,14},{9,15},{10,... | collective-permute-start | bytes 393224 | tf_op jit(solution)/shard_map/ppermute | solution.py:584
  45.4 17.5 %collective-permute-start.11 = (bf16[8,16,512]{2,1,0:T(8,128)(2,1)S(1)}, bf16[8,16,512]{2,1,0:T(8,128)(2,1)S(1)}, u32[]{:S(2)}, u32[]{:S(2)}) collective-permute-start(bf16[8,16,512]{2,1,0:T(8,128)(2,1)S(1)} %get-tuple-element.51), channel_id=1, source_target_pairs={{0,8},{1,9},{2,10},{3,11},{4,12},{5,13},{6,14},{7,15},{8,0},{9,1},... | collective-permute-start | bytes 393224 | tf_op jit(solution)/shard_map/ppermute | solution.py:584
  48.0 18.0 %collective-permute-start.12 = (bf16[8,16,512]{2,1,0:T(8,128)(2,1)S(1)}, bf16[8,16,512]{2,1,0:T(8,128)(2,1)S(1)}, u32[]{:S(2)}, u32[]{:S(2)}) collective-permute-start(bf16[8,16,512]{2,1,0:T(8,128)(2,1)S(1)} %get-tuple-element.52), channel_id=1, source_target_pairs={{0,10},{1,11},{2,8},{3,9},{4,14},{5,15},{6,12},{7,13},{8,2},{9,3},... | collective-permute-start | bytes 393224 | tf_op jit(solution)/shard_map/ppermute | solution.py:584
  51.6 14.4 %collective-permute-start.13 = (bf16[8,16,512]{2,1,0:T(8,128)(2,1)S(1)}, bf16[8,16,512]{2,1,0:T(8,128)(2,1)S(1)}, u32[]{:S(2)}, u32[]{:S(2)}) collective-permute-start(bf16[8,16,512]{2,1,0:T(8,128)(2,1)S(1)} %get-tuple-element.53), channel_id=1, source_target_pairs={{0,12},{1,13},{2,14},{3,15},{4,8},{5,9},{6,10},{7,11},{8,4},{9,5},... | collective-permute-start | bytes 393224 | tf_op jit(solution)/shard_map/ppermute | solution.py:584
  55.4 10.6 %collective-permute-start.14 = (bf16[8,16,512]{2,1,0:T(8,128)(2,1)S(1)}, bf16[8,16,512]{2,1,0:T(8,128)(2,1)S(1)}, u32[]{:S(2)}, u32[]{:S(2)}) collective-permute-start(bf16[8,16,512]{2,1,0:T(8,128)(2,1)S(1)} %get-tuple-element.54), channel_id=1, source_target_pairs={{0,14},{1,15},{2,12},{3,13},{4,10},{5,11},{6,8},{7,9},{8,6},{9,7},... | collective-permute-start | bytes 393224 | tf_op jit(solution)/shard_map/ppermute | solution.py:584
  56.6 10.3 %collective-permute-start.8 = (bf16[8,16,512]{2,1,0:T(8,128)(2,1)S(1)}, bf16[8,16,512]{2,1,0:T(8,128)(2,1)S(1)}, u32[]{:S(2)}, u32[]{:S(2)}) collective-permute-start(bf16[8,16,512]{2,1,0:T(8,128)(2,1)S(1)} %get-tuple-element.48), channel_id=1, source_target_pairs={{0,2},{1,3},{2,0},{3,1},{4,6},{5,7},{6,4},{7,5},{8,10},{9,11},{10,... | collective-permute-start | bytes 393224 | tf_op jit(solution)/shard_map/ppermute | solution.py:584
  62.9 5.7 %collective-permute-start.9 = (bf16[8,16,512]{2,1,0:T(8,128)(2,1)S(1)}, bf16[8,16,512]{2,1,0:T(8,128)(2,1)S(1)}, u32[]{:S(2)}, u32[]{:S(2)}) collective-permute-start(bf16[8,16,512]{2,1,0:T(8,128)(2,1)S(1)} %get-tuple-element.49), channel_id=1, source_target_pairs={{0,4},{1,5},{2,6},{3,7},{4,0},{5,1},{6,2},{7,3},{8,12},{9,13},{10,... | collective-permute-start | bytes 393224 | tf_op jit(solution)/shard_map/ppermute | solution.py:584
  75.5 8.9 %collective-permute-start.15 = (bf16[8,16,512]{2,1,0:T(8,128)(2,1)S(1)}, bf16[8,16,512]{2,1,0:T(8,128)(2,1)S(1)}, u32[]{:S(2)}, u32[]{:S(2)}) collective-permute-start(bf16[8,16,512]{2,1,0:T(8,128)(2,1)S(1)} %get-tuple-element.56), channel_id=1, source_target_pairs={{0,2},{1,3},{2,0},{3,1},{4,6},{5,7},{6,4},{7,5},{8,10},{9,11},{10,... | collective-permute-start | bytes 393224 | tf_op jit(solution)/shard_map/ppermute | solution.py:584
  76.1 11.6 %collective-permute-start.16 = (bf16[8,16,512]{2,1,0:T(8,128)(2,1)S(1)}, bf16[8,16,512]{2,1,0:T(8,128)(2,1)S(1)}, u32[]{:S(2)}, u32[]{:S(2)}) collective-permute-start(bf16[8,16,512]{2,1,0:T(8,128)(2,1)S(1)} %get-tuple-element.57), channel_id=1, source_target_pairs={{0,4},{1,5},{2,6},{3,7},{4,0},{5,1},{6,2},{7,3},{8,12},{9,13},{10,... | collective-permute-start | bytes 393224 | tf_op jit(solution)/shard_map/ppermute | solution.py:584
  80.5 9.6 %collective-permute-start.17 = (bf16[8,16,512]{2,1,0:T(8,128)(2,1)S(1)}, bf16[8,16,512]{2,1,0:T(8,128)(2,1)S(1)}, u32[]{:S(2)}, u32[]{:S(2)}) collective-permute-start(bf16[8,16,512]{2,1,0:T(8,128)(2,1)S(1)} %get-tuple-element.58), channel_id=1, source_target_pairs={{0,6},{1,7},{2,4},{3,5},{4,2},{5,3},{6,0},{7,1},{8,14},{9,15},{10,... | collective-permute-start | bytes 393224 | tf_op jit(solution)/shard_map/ppermute | solution.py:584
  80.5 9.6 %collective-permute-start.18 = (bf16[8,16,512]{2,1,0:T(8,128)(2,1)S(1)}, bf16[8,16,512]{2,1,0:T(8,128)(2,1)S(1)}, u32[]{:S(2)}, u32[]{:S(2)}) collective-permute-start(bf16[8,16,512]{2,1,0:T(8,128)(2,1)S(1)} %get-tuple-element.59), channel_id=1, source_target_pairs={{0,8},{1,9},{2,10},{3,11},{4,12},{5,13},{6,14},{7,15},{8,0},{9,1},... | collective-permute-start | bytes 393224 | tf_op jit(solution)/shard_map/ppermute | solution.py:584
  83.5 19.2 %collective-permute-start.19 = (bf16[8,16,512]{2,1,0:T(8,128)(2,1)S(1)}, bf16[8,16,512]{2,1,0:T(8,128)(2,1)S(1)}, u32[]{:S(2)}, u32[]{:S(2)}) collective-permute-start(bf16[8,16,512]{2,1,0:T(8,128)(2,1)S(1)} %get-tuple-element.60), channel_id=1, source_target_pairs={{0,10},{1,11},{2,8},{3,9},{4,14},{5,15},{6,12},{7,13},{8,2},{9,3},... | collective-permute-start | bytes 393224 | tf_op jit(solution)/shard_map/ppermute | solution.py:584
  84.4 18.3 %collective-permute-start.20 = (bf16[8,16,512]{2,1,0:T(8,128)(2,1)S(1)}, bf16[8,16,512]{2,1,0:T(8,128)(2,1)S(1)}, u32[]{:S(2)}, u32[]{:S(2)}) collective-permute-start(bf16[8,16,512]{2,1,0:T(8,128)(2,1)S(1)} %get-tuple-element.61), channel_id=1, source_target_pairs={{0,12},{1,13},{2,14},{3,15},{4,8},{5,9},{6,10},{7,11},{8,4},{9,5},... | collective-permute-start | bytes 393224 | tf_op jit(solution)/shard_map/ppermute | solution.py:584
  87.7 15.0 %collective-permute-start.21 = (bf16[8,16,512]{2,1,0:T(8,128)(2,1)S(1)}, bf16[8,16,512]{2,1,0:T(8,128)(2,1)S(1)}, u32[]{:S(2)}, u32[]{:S(2)}) collective-permute-start(bf16[8,16,512]{2,1,0:T(8,128)(2,1)S(1)} %get-tuple-element.62), channel_id=1, source_target_pairs={{0,14},{1,15},{2,12},{3,13},{4,10},{5,11},{6,8},{7,9},{8,6},{9,7},... | collective-permute-start | bytes 393224 | tf_op jit(solution)/shard_map/ppermute | solution.py:584

commit v5 on v4

--- a/solution.py
+++ b/solution.py
@@ -10,11 +10,9 @@
 
 HD = 32
 GRID = 8
-CHUNKS = 1
 BATCH = 2
 STRIPS = 2
-SPLIT = (True,)
-ORDER = (4, 6, 5, 7, 2, 3, 1)
+MOVES = (0, 1, 4, 6, 5, 2, 7, 3)
 ROOT = math.sqrt(2.0 / math.pi)
 LIN = 2.0 * ROOT
 CUBE = 8.0 * ROOT * 0.044715
@@ -82,52 +80,56 @@
     return copies
 
 
-def edges_kernel(image, top, bottom, sems):
+def edges_kernel(info, image, top, bottom, sems):
     rows = image.shape[0]
     for copy in copy_all([(image.at[rows - 1 : rows], bottom), (image.at[0:1], top)], sems):
         copy.wait()
 
 
-def edge_rows(image):
+def edge_rows(info, image):
     edge = jax.ShapeDtypeStruct((1,) + image.shape[1:], BF16)
     return pl.pallas_call(
         edges_kernel,
-        in_specs=[hbm()],
-        out_specs=[any_space()] * 2,
+        in_specs=[smem(), hbm()],
+        out_specs=[vmem()] * 2,
         out_shape=[edge, edge],
         scratch_shapes=[pltpu.SemaphoreType.DMA((2,))],
         compiler_params=params(),
         name="edge_rows",
-    )(in_hbm(image))
-
-
-def shares_kernel(info, expand, project, expand_part, project_part, sems):
+    )(info, in_hbm(image))
+
+
+def shares_kernel(info, expand, project, qkv, out, expand_part, project_part, rest_part, sems):
     def span(part, axis):
         size = part.shape[axis]
         return pl.ds(pl.multiple_of(info[CORE] * size, size), size)
 
+    width = qkv.shape[1]
     moves = [
         (expand.at[:, span(expand_part, 1)], expand_part),
         (project.at[span(project_part, 0)], project_part),
+        (qkv.at[span(rest_part, 0)], rest_part.at[:, :width]),
+        (out.at[span(rest_part, 0)], rest_part.at[:, width:]),
     ]
     for copy in copy_all(moves, sems):
         copy.wait()
 
 
-def share_weights(info, w_expand, w_project):
+def share_weights(info, w_expand, w_project, w_qkv, w_out):
     shapes = [
         (w_expand.shape[0], w_expand.shape[1] // 2),
         (w_project.shape[0] // 2, w_project.shape[1]),
+        (w_qkv.shape[0] // 2, w_qkv.shape[1] + w_out.shape[1]),
     ]
     return pl.pallas_call(
         shares_kernel,
-        in_specs=[smem(), hbm(), hbm()],
-        out_specs=[vmem()] * 2,
+        in_specs=[smem()] + [hbm()] * 4,
+        out_specs=[vmem()] * 3,
         out_shape=[jax.ShapeDtypeStruct(shape, BF16) for shape in shapes],
-        scratch_shapes=[pltpu.SemaphoreType.DMA((2,))],
+        scratch_shapes=[pltpu.SemaphoreType.DMA((4,))],
         compiler_params=params(),
         name="share_weights",
-    )(info, *map(in_hbm, (w_expand, w_project)))
+    )(info, *map(in_hbm, (w_expand, w_project, w_qkv, w_out)))
 
 
 def order_kernel(image, above, below, scale, shift, ordered, normed):
@@ -278,12 +280,17 @@
 
 def pieced_dot(lhs, pieces, info, put):
     width = pieces[0].shape[1]
-    for n, piece in enumerate(pieces):
-        if len(pieces) == 1:
-            start = 0
-        else:
-            start = pl.multiple_of((1 - info[DP] if n else info[DP]) * width, width)
-        put(start, width, dot(lhs[...], piece[...]))
+    if len(pieces) == 1:
+        put(0, width, dot(lhs[...], pieces[0][...]))
+        return
+    put(pl.multiple_of(info[DP] * width, width), width, dot(lhs[...], pieces[0][...]))
+    total = None
+    for n, piece in enumerate(pieces[1:]):
+        depth = piece.shape[0]
+        at = 1 - info[CORE] if n else info[CORE]
+        part = dot(lhs[:, pl.ds(pl.multiple_of(at * depth, depth), depth)], piece[...])
+        total = part if total is None else total + part
+    put(pl.multiple_of((1 - info[DP]) * width, width), width, total)
 
 
 def project_kernel(pieces, split, info, ordered, *refs):
@@ -323,7 +330,7 @@
             put(pl.multiple_of(column * width, width), total)
 
     for k in range(GRID):
-        place = (grid_of(info) ^ k) if split else k
+        place = (grid_of(info) ^ MOVES[k]) if split else k
         for row in range(count):
             start = row * cols + pl.multiple_of(place * size, size)
             block_of(outs, k)[row] = conv[pl.ds(start, size), :]
@@ -360,7 +367,11 @@
 def attend_kernel(pieces, blocks, info, gain, bias, *refs):
     refs = list(refs)
     take = lambda n: [refs.pop(0) for _ in range(n)]
-    qkv_pieces, out_pieces = take(pieces), take(pieces)
+    qkv_pieces, out_pieces, rest = take(1), take(1), take(pieces - 1)
+    split = qkv_pieces[0].shape[1]
+    for both in rest:
+        qkv_pieces.append(both.at[:, :split])
+        out_pieces.append(both.at[:, split:])
     tokens, outs = take(blocks), take(blocks)
     lned, triple, mixed, resid, soft = refs
     count, size, chans = tokens[0].shape[-3:]
@@ -435,13 +446,13 @@
             block_of(outs, k)[a] = jnp.concatenate(parts, axis=0).astype(BF16)
 
 
-def attend(info, tokens, gain, bias, w_qkv, w_out):
+def attend(info, tokens, gain, bias, w_qkv, w_out, rest):
     count, size, chans = tokens[0].shape[-3:]
     total = count * size * GRID
     return pl.pallas_call(
-        functools.partial(attend_kernel, len(w_qkv), len(tokens)),
+        functools.partial(attend_kernel, 1 + len(rest), len(tokens)),
         out_shape=[jax.ShapeDtypeStruct(t.shape, BF16) for t in tokens],
-        in_specs=[smem()] + [vmem()] * (2 + 2 * len(w_qkv) + len(tokens)),
+        in_specs=[smem()] + [vmem()] * (4 + len(rest) + len(tokens)),
         out_specs=[vmem()] * len(tokens),
         scratch_shapes=[
             pltpu.VMEM((total, chans), BF16),
@@ -453,7 +464,7 @@
         compiler_params=params(),
         cost_estimate=cost(),
         name="attend",
-    )(info, gain, bias, *w_qkv, *w_out, *tokens)
+    )(info, gain, bias, w_qkv, w_out, *rest, *tokens)
 
 
 def restore_kernel(blocks, info, *refs):
@@ -467,7 +478,7 @@
             tokens = parts[0][:, row].reshape(cols, chans)
         else:
             for k in range(GRID):
-                place = pl.multiple_of((grid_of(info) ^ k) * size, size)
+                place = pl.multiple_of((grid_of(info) ^ MOVES[k]) * size, size)
                 buf[pl.ds(row * cols + place, size), :] = parts[k][row]
             tokens = buf[row * cols : (row + 1) * cols, :]
         out[row] = dot(back, tokens).astype(BF16)
@@ -536,13 +547,14 @@
 
     over_dp = lambda w: lax.ppermute(w, "dp", [(0, 1), (1, 0)])
     over_core = lambda w: lax.ppermute(w, "space", [(i, i ^ 1) for i in range(space)])
-    top, bottom = edge_rows(image)
-    above = lax.ppermute(bottom, "space", [(i, i + 1) for i in range(space - 1)])
-    below = lax.ppermute(top, "space", [(i + 1, i) for i in range(space - 1)])
+    later = info
     if pairs:
-        mine = share_weights(after(info, top), w_expand, w_project)
-        expand_got, project_got = map(over_dp, mine)
-        above = after(above, *mine)
+        mine = share_weights(info, w_expand, w_project, w_qkv, w_out)
+        expand_got, project_got, rest_got = map(over_dp, mine)
+        later = after(info, *mine)
+    top, bottom = edge_rows(later, image)
+    above = lax.ppermute(bottom, "space", [(i, (i + 1) % space) for i in range(space)])
+    below = lax.ppermute(top, "space", [((i + 1) % space, i) for i in range(space)])
     sources = (image, above, below, as_row(bn_scale), as_row(bn_shift))
     if pairs:
         tiles = max(1, w_expand.shape[1] // 256)
@@ -566,34 +578,25 @@
         )
         spatial = [spatial]
         project_all = [gathered(w_project)]
-        w_qkv, w_out = [gathered(w_qkv)], [gathered(w_out)]
-
-    count = rows // CHUNKS
-    rings = [list(range(first, space, groups)) for first in range(groups)]
+        w_qkv, w_out = gathered(w_qkv), gathered(w_out)
+
 
     def exchange(parts):
-        if len(parts) == 1:
-            return [
-                lax.all_to_all(parts[0], "space", 0, 0, axis_index_groups=rings, tiled=True)
+        parts = list(parts)
+        for n in range(1, GRID):
+            swap = [
+                (s, (((s // groups) ^ MOVES[n]) * groups) + s % groups) for s in range(space)
             ]
-        parts = list(parts)
-        for k in ORDER:
-            pairs_k = [
-                (s, (((s // groups) ^ k) * groups) + s % groups) for s in range(space)
-            ]
-            parts[k] = lax.ppermute(parts[k], "space", pairs_k)
+            parts[n] = lax.ppermute(parts[n], "space", swap)
         return parts
 
-    sent = [
-        exchange(project_rows(info, spatial, ordered, project_all, chunk, count, SPLIT[chunk]))
-        for chunk in range(CHUNKS)
-    ]
+    placed = project_rows(info, spatial, ordered, project_all, 0, rows, True)
+    rest = []
     if pairs:
-        w_qkv, w_out = [w_qkv, over_dp(w_qkv)], [w_out, over_dp(w_out)]
-    back = [exchange(attend(info, parts, gain, bias, w_qkv, w_out)) for parts in sent]
-    result = None
-    for chunk in range(CHUNKS):
-        result = restore_rows(info, back[chunk], rows, chunk, result)
+        rest_got = after(rest_got, placed[0])
+        rest = [rest_got, over_core(rest_got)]
+    back = exchange(attend(info, exchange(placed), gain, bias, w_qkv, w_out, rest))
+    result = restore_rows(info, back, rows, 0, None)
     return result.reshape(fields.shape)
 
 

time: 107 us -> 106 us (level); the launches traced: 105 us -> 106 us
  waiting for transfers between devices: 35.2 us -> 38.5 us
  starting transfers between devices: 37.7 us -> 34.7 us
    ppermute x16, waiting for transfers between devices: 27.6 us -> 32.4 us  [the longest x14 29.7 us: exchange(): parts[n] = lax.ppermute(parts[n], 'space', swap)]
    ppermute x2 -> x3, starting transfers between devices: 3.88 us -> 1 us  [local(): lax.ppermute(w, 'space', [(i, i ^ 1) for i in range(space)])]
    ppermute x4 -> x3, starting transfers between devices: 7.01 us -> 4.85 us  [local(): over_dp = lambda w: lax.ppermute(w, 'dp', [(0, 1), (1, 0)])]
    ppermute x16, starting transfers between devices: 26.8 us -> 28.8 us  [the longest x14 24.4 us: exchange(): parts[n] = lax.ppermute(parts[n], 'space', swap)]
    ppermute x4 -> x3, waiting for transfers between devices: 7.67 us -> 6.11 us  [local(): over_dp = lambda w: lax.ppermute(w, 'dp', [(0, 1), (1, 0)])]
  transfers between devices with their start and end apart: 22 -> 22, of which waited for: 10 -> 9; matrix products, arithmetic and copies ran while one was open for 0% -> 0% of each run, Pallas kernels for 19% -> 20%
where the time goes in v5:
time: 106 us
  waiting for transfers between devices  38.5 us (36%)
  starting transfers between devices  34.7 us (33%)
  Pallas kernels  32.1 us (30%)
    ppermute x14, waiting for transfers between devices, exchange(): parts[n] = lax.ppermute(parts[n], 'space', swap)  29.7 us
    ppermute x14, starting transfers between devices, exchange(): parts[n] = lax.ppermute(parts[n], 'space', swap)  24.4 us
    pallas_call x3, Pallas kernels, expand_some(): pl.pallas_call(functools.partial(expand_kernel, first, tile_of), grid_spe...  16.6 us
    pallas_call x1, Pallas kernels, attend(): pl.pallas_call(functools.partial(attend_kernel, 1 + len(rest), len(tokens...  7.01 us
    ppermute x3, waiting for transfers between devices, local(): over_dp = lambda w: lax.ppermute(w, 'dp', [(0, 1), (1, 0)])  6.11 us
    ppermute x3, starting transfers between devices, local(): over_dp = lambda w: lax.ppermute(w, 'dp', [(0, 1), (1, 0)])  4.85 us
    ppermute x1, starting transfers between devices, local(): lax.ppermute(top, 'space', [((i + 1) % space, i) for i in range(space)])  4.43 us
    pallas_call x1, Pallas kernels, project_rows(): pl.pallas_call(functools.partial(project_kernel, len(weights), split), gr...  3.06 us
  transfers between devices with their start and end apart: 22, of which 9 were waited for; matrix products, arithmetic and copies ran while one was open for 0% of the time, Pallas kernels for 20%

profile of v5, /device:TPU:0, one launch (start us, length us, event | category | flops | bytes accessed | tf_op | source)
XLA Modules:
  0.0 105.7 jit_solution(3213958219356947815)
XLA Ops:
  0.1 1.9 %share_weights.1 = (bf16[512,512]{1,0:T(8,128)(2,1)S(1)}, bf16[1024,256]{1,0:T(8,128)(2,1)S(1)}, bf16[256,1024]{1,0:T(8,128)(2,1)S(1)}) custom-call(s32[5]{0:T(128)S(1)} %stack.15.info, bf16[512,1024]{1,0:T(8,128)(2,1)} %refs_5_.1, bf16[2048,256]{1,0:T(8,128)(2,1)} %refs_3_.5, bf16[512,768]{1,0:T(8,128)(2,1)} %refs_0_.1, bf16[512,256]{1,0:T(8,128)(2,1)} %refs_1_.1), custom_call_target="tpu_custom_call" | custom-call | tf_op jit(solution)/shard_map/share_weights/pallas_call | solution.py:124
  2.0 3.0 %collective-permute-start.3 = (bf16[512,512]{1,0:T(8,128)(2,1)S(1)}, bf16[512,512]{1,0:T(8,128)(2,1)S(1)}, u32[]{:S(2)}, u32[]{:S(2)}) collective-permute-start(bf16[512,512]{1,0:T(8,128)(2,1)S(1)} %get-tuple-element.36), channel_id=1, source_target_pairs={{0,16},{16,0},{1,17},{17,1},{2,18},{18,2},{3,19},{19,3},{4,20},{20... | collective-permute-start | bytes 1572872 | tf_op jit(solution)/shard_map/ppermute | solution.py:548
  5.2 1.5 %edge_rows.1 = (bf16[1,128,512]{2,1,0:T(8,128)(2,1)S(1)}, bf16[1,128,512]{2,1,0:T(8,128)(2,1)S(1)}) custom-call(s32[5]{0:T(128)S(1)} %stack.15.info, bf16[8,128,512]{2,1,0:T(8,128)(2,1)} %bitcast.19), custom_call_target="tpu_custom_call" | custom-call | tf_op jit(solution)/shard_map/edge_rows/pallas_call | solution.py:91
  6.8 4.4 %collective-permute-start.2 = (bf16[1,128,512]{2,1,0:T(8,128)(2,1)S(1)}, bf16[1,128,512]{2,1,0:T(8,128)(2,1)S(1)}, u32[]{:S(2)}, u32[]{:S(2)}) collective-permute-start(bf16[1,128,512]{2,1,0:T(8,128)(2,1)S(1)} %get-tuple-element.40), channel_id=1, source_target_pairs={{1,0},{2,1},{3,2},{4,3},{5,4},{6,5},{7,6},{8,7},{9,8},{10,9},{11,1... | collective-permute-start | bytes 393224 | tf_op jit(solution)/shard_map/ppermute | solution.py:557
  11.2 2.8 %collective-permute-done.1.refs_1_ = bf16[1,128,512]{2,1,0:T(8,128)(2,1)S(1)} collective-permute-done((bf16[1,128,512]{2,1,0:T(8,128)(2,1)S(1)}, bf16[1,128,512]{2,1,0:T(8,128)(2,1)S(1)}, u32[]{:S(2)}, u32[]{:S(2)}) %collective-permute-start.1) | collective-permute-done | bytes 131104 | tf_op jit(solution)/shard_map/ppermute | solution.py:556
  13.9 9.0 %expand_conv.3 = (bf16[1024,1024]{1,0:T(8,128)(2,1)S(1)}, bf16[8,128,512]{2,1,0:T(8,128)(2,1)S(1)}, bf16[10,128,512]{2,1,0:T(8,128)(2,1)S(1)}) custom-call(s32[5]{0:T(128)S(1)} %stack.15.info, bf16[8,128,512]{2,1,0:T(8,128)(2,1)} %bitcast.20, bf16[1,128,512]{2,1,0:T(8,128)(2,1)S(1)} %collective-permute-done.1.refs_1_, ...), custom_call_target="tpu_custom_call" | custom-call | flops 1 | bytes 1 | tf_op jit(solution)/shard_map/expand_conv/pallas_call | solution.py:261
  22.9 1.0 collective-permute-start.4
  23.9 4.3 %collective-permute-done.5.refs_4_ = bf16[1024,256]{1,0:T(8,128)(2,1)S(1)} collective-permute-done((bf16[1024,256]{1,0:T(8,128)(2,1)S(1)}, bf16[1024,256]{1,0:T(8,128)(2,1)S(1)}, u32[]{:S(2)}, u32[]{:S(2)}) %collective-permute-start.5) | collective-permute-done | bytes 524320 | tf_op jit(solution)/shard_map/ppermute | solution.py:548
  28.2 1.7 %collective-permute-start = (bf16[256,1024]{1,0:T(8,128)(2,1)S(1)}, bf16[256,1024]{1,0:T(8,128)(2,1)S(1)}, u32[]{:S(2)}, u32[]{:S(2)}) collective-permute-start(bf16[256,1024]{1,0:T(8,128)(2,1)S(1)} %get-tuple-element.35), channel_id=1, source_target_pairs={{0,16},{16,0},{1,17},{17,1},{2,18},{18,2},{3,19},{19,3},{4,20},{20... | collective-permute-start | bytes 1572872 | tf_op jit(solution)/shard_map/ppermute | solution.py:548
  30.0 3.7 %expand_conv.4.refs_1_ = bf16[1024,512]{1,0:T(8,128)(2,1)S(1)} custom-call(s32[5]{0:T(128)S(1)} %stack.15.info, bf16[10,128,512]{2,1,0:T(8,128)(2,1)S(1)} %get-tuple-element.45.refs_0_, bf16[512,512]{1,0:T(8,128)(2,1)S(1)} %collective-permute-done.3.refs_1_, f32[1,2048]{1,0:T(1,128)S(1)} %bitcast.12, f32[3,3,2048]{2,1,0:T(4,128)S(1)} %copy-done.3, ...), custom_call_target="tpu_custom_call" | custom-call | flops 1 | bytes 1 | tf_op jit(solution)/shard_map/expand_conv/pallas_call | solution.py:261
  33.7 3.9 %expand_conv.5.refs_2_ = bf16[1024,512]{1,0:T(8,128)(2,1)S(1)} custom-call(s32[5]{0:T(128)S(1)} %stack.15.info, bf16[10,128,512]{2,1,0:T(8,128)(2,1)S(1)} %get-tuple-element.45.refs_0_, bf16[512,512]{1,0:T(8,128)(2,1)S(1)} %collective-permute-done.4.refs_1_, f32[1,2048]{1,0:T(1,128)S(1)} %bitcast.13, f32[3,3,2048]{2,1,0:T(4,128)S(1)} %copy-done.3, ...), custom_call_target="tpu_custom_call" | custom-call | flops 1 | bytes 1 | tf_op jit(solution)/shard_map/expand_conv/pallas_call | solution.py:261
  37.7 3.1 %project_rows.1 = (bf16[8,16,512]{2,1,0:T(8,128)(2,1)S(1)}, bf16[8,16,512]{2,1,0:T(8,128)(2,1)S(1)}, bf16[8,16,512]{2,1,0:T(8,128)(2,1)S(1)}, bf16[8,16,512]{2,1...) custom-call(s32[5]{0:T(128)S(1)} %stack.15.info, ...), custom_call_target="tpu_custom_call" | custom-call | flops 1 | bytes 1 | tf_op jit(solution)/shard_map/project_rows/pallas_call | solution.py:349
  40.8 1.8 %collective-permute-done.refs_2_ = bf16[256,1024]{1,0:T(8,128)(2,1)S(1)} collective-permute-done((bf16[256,1024]{1,0:T(8,128)(2,1)S(1)}, bf16[256,1024]{1,0:T(8,128)(2,1)S(1)}, u32[]{:S(2)}, u32[]{:S(2)}) %collective-permute-start) | collective-permute-done | bytes 524320 | tf_op jit(solution)/shard_map/ppermute | solution.py:548
  42.6 1.7 %collective-permute-start.8 = (bf16[8,16,512]{2,1,0:T(8,128)(2,1)S(1)}, bf16[8,16,512]{2,1,0:T(8,128)(2,1)S(1)}, u32[]{:S(2)}, u32[]{:S(2)}) collective-permute-start(bf16[8,16,512]{2,1,0:T(8,128)(2,1)S(1)} %get-tuple-element.50), channel_id=1, source_target_pairs={{0,2},{1,3},{2,0},{3,1},{4,6},{5,7},{6,4},{7,5},{8,10},{9,11},{10,... | collective-permute-start | bytes 393224 | tf_op jit(solution)/shard_map/ppermute | solution.py:590
  44.3 2.6 %collective-permute-start.9 = (bf16[8,16,512]{2,1,0:T(8,128)(2,1)S(1)}, bf16[8,16,512]{2,1,0:T(8,128)(2,1)S(1)}, u32[]{:S(2)}, u32[]{:S(2)}) collective-permute-start(bf16[8,16,512]{2,1,0:T(8,128)(2,1)S(1)} %get-tuple-element.51), channel_id=1, source_target_pairs={{0,8},{1,9},{2,10},{3,11},{4,12},{5,13},{6,14},{7,15},{8,0},{9,1},... | collective-permute-start | bytes 393224 | tf_op jit(solution)/shard_map/ppermute | solution.py:590
  46.9 1.3 %collective-permute-start.10 = (bf16[8,16,512]{2,1,0:T(8,128)(2,1)S(1)}, bf16[8,16,512]{2,1,0:T(8,128)(2,1)S(1)}, u32[]{:S(2)}, u32[]{:S(2)}) collective-permute-start(bf16[8,16,512]{2,1,0:T(8,128)(2,1)S(1)} %get-tuple-element.52), channel_id=1, source_target_pairs={{0,12},{1,13},{2,14},{3,15},{4,8},{5,9},{6,10},{7,11},{8,4},{9,5},... | collective-permute-start | bytes 393224 | tf_op jit(solution)/shard_map/ppermute | solution.py:590
  48.2 1.7 %collective-permute-start.11 = (bf16[8,16,512]{2,1,0:T(8,128)(2,1)S(1)}, bf16[8,16,512]{2,1,0:T(8,128)(2,1)S(1)}, u32[]{:S(2)}, u32[]{:S(2)}) collective-permute-start(bf16[8,16,512]{2,1,0:T(8,128)(2,1)S(1)} %get-tuple-element.53), channel_id=1, source_target_pairs={{0,10},{1,11},{2,8},{3,9},{4,14},{5,15},{6,12},{7,13},{8,2},{9,3},... | collective-permute-start | bytes 393224 | tf_op jit(solution)/shard_map/ppermute | solution.py:590
  49.9 1.3 %collective-permute-start.12 = (bf16[8,16,512]{2,1,0:T(8,128)(2,1)S(1)}, bf16[8,16,512]{2,1,0:T(8,128)(2,1)S(1)}, u32[]{:S(2)}, u32[]{:S(2)}) collective-permute-start(bf16[8,16,512]{2,1,0:T(8,128)(2,1)S(1)} %get-tuple-element.54), channel_id=1, source_target_pairs={{0,4},{1,5},{2,6},{3,7},{4,0},{5,1},{6,2},{7,3},{8,12},{9,13},{10,... | collective-permute-start | bytes 393224 | tf_op jit(solution)/shard_map/ppermute | solution.py:590
  51.2 8.7 %collective-permute-done.9.refs_6_ = bf16[8,16,512]{2,1,0:T(8,128)(2,1)S(1)} collective-permute-done((bf16[8,16,512]{2,1,0:T(8,128)(2,1)S(1)}, bf16[8,16,512]{2,1,0:T(8,128)(2,1)S(1)}, u32[]{:S(2)}, u32[]{:S(2)}) %collective-permute-start.9) | collective-permute-done | bytes 131104 | tf_op jit(solution)/shard_map/ppermute | solution.py:590
  60.0 2.8 %collective-permute-start.13 = (bf16[8,16,512]{2,1,0:T(8,128)(2,1)S(1)}, bf16[8,16,512]{2,1,0:T(8,128)(2,1)S(1)}, u32[]{:S(2)}, u32[]{:S(2)}) collective-permute-start(bf16[8,16,512]{2,1,0:T(8,128)(2,1)S(1)} %get-tuple-element.55), channel_id=1, source_target_pairs={{0,14},{1,15},{2,12},{3,13},{4,10},{5,11},{6,8},{7,9},{8,6},{9,7},... | collective-permute-start | bytes 393224 | tf_op jit(solution)/shard_map/ppermute | solution.py:590
  63.0 5.1 %collective-permute-done.11.refs_8_ = bf16[8,16,512]{2,1,0:T(8,128)(2,1)S(1)} collective-permute-done((bf16[8,16,512]{2,1,0:T(8,128)(2,1)S(1)}, bf16[8,16,512]{2,1,0:T(8,128)(2,1)S(1)}, u32[]{:S(2)}, u32[]{:S(2)}) %collective-permute-start.11) | collective-permute-done | bytes 131104 | tf_op jit(solution)/shard_map/ppermute | solution.py:590
  68.1 2.4 %collective-permute-done.14.refs_11_ = bf16[8,16,512]{2,1,0:T(8,128)(2,1)S(1)} collective-permute-done((bf16[8,16,512]{2,1,0:T(8,128)(2,1)S(1)}, bf16[8,16,512]{2,1,0:T(8,128)(2,1)S(1)}, u32[]{:S(2)}, u32[]{:S(2)}) %collective-permute-start.14) | collective-permute-done | bytes 131104 | tf_op jit(solution)/shard_map/ppermute | solution.py:590
  70.6 7.0 %attend.1 = (bf16[8,16,512]{2,1,0:T(8,128)(2,1)S(1)}, bf16[8,16,512]{2,1,0:T(8,128)(2,1)S(1)}, bf16[8,16,512]{2,1,0:T(8,128)(2,1)S(1)}, bf16[8,16,512]{2,1,0:T(8...) custom-call(s32[5]{0:T(128)S(1)} %stack.15.info, ...), custom_call_target="tpu_custom_call" | custom-call | flops 1 | bytes 1 | tf_op jit(solution)/shard_map/attend/pallas_call | solution.py:452
  77.6 1.5 %collective-permute-start.15 = (bf16[8,16,512]{2,1,0:T(8,128)(2,1)S(1)}, bf16[8,16,512]{2,1,0:T(8,128)(2,1)S(1)}, u32[]{:S(2)}, u32[]{:S(2)}) collective-permute-start(bf16[8,16,512]{2,1,0:T(8,128)(2,1)S(1)} %get-tuple-element.58), channel_id=1, source_target_pairs={{0,2},{1,3},{2,0},{3,1},{4,6},{5,7},{6,4},{7,5},{8,10},{9,11},{10,... | collective-permute-start | bytes 393224 | tf_op jit(solution)/shard_map/ppermute | solution.py:590
  79.1 2.6 %collective-permute-start.16 = (bf16[8,16,512]{2,1,0:T(8,128)(2,1)S(1)}, bf16[8,16,512]{2,1,0:T(8,128)(2,1)S(1)}, u32[]{:S(2)}, u32[]{:S(2)}) collective-permute-start(bf16[8,16,512]{2,1,0:T(8,128)(2,1)S(1)} %get-tuple-element.59), channel_id=1, source_target_pairs={{0,8},{1,9},{2,10},{3,11},{4,12},{5,13},{6,14},{7,15},{8,0},{9,1},... | collective-permute-start | bytes 393224 | tf_op jit(solution)/shard_map/ppermute | solution.py:590
  81.7 2.2 %collective-permute-start.17 = (bf16[8,16,512]{2,1,0:T(8,128)(2,1)S(1)}, bf16[8,16,512]{2,1,0:T(8,128)(2,1)S(1)}, u32[]{:S(2)}, u32[]{:S(2)}) collective-permute-start(bf16[8,16,512]{2,1,0:T(8,128)(2,1)S(1)} %get-tuple-element.60), channel_id=1, source_target_pairs={{0,12},{1,13},{2,14},{3,15},{4,8},{5,9},{6,10},{7,11},{8,4},{9,5},... | collective-permute-start | bytes 393224 | tf_op jit(solution)/shard_map/ppermute | solution.py:590
  84.5 2.3 %collective-permute-start.19 = (bf16[8,16,512]{2,1,0:T(8,128)(2,1)S(1)}, bf16[8,16,512]{2,1,0:T(8,128)(2,1)S(1)}, u32[]{:S(2)}, u32[]{:S(2)}) collective-permute-start(bf16[8,16,512]{2,1,0:T(8,128)(2,1)S(1)} %get-tuple-element.62), channel_id=1, source_target_pairs={{0,4},{1,5},{2,6},{3,7},{4,0},{5,1},{6,2},{7,3},{8,12},{9,13},{10,... | collective-permute-start | bytes 393224 | tf_op jit(solution)/shard_map/ppermute | solution.py:590
  86.9 2.4 %collective-permute-start.20 = (bf16[8,16,512]{2,1,0:T(8,128)(2,1)S(1)}, bf16[8,16,512]{2,1,0:T(8,128)(2,1)S(1)}, u32[]{:S(2)}, u32[]{:S(2)}) collective-permute-start(bf16[8,16,512]{2,1,0:T(8,128)(2,1)S(1)} %get-tuple-element.63), channel_id=1, source_target_pairs={{0,14},{1,15},{2,12},{3,13},{4,10},{5,11},{6,8},{7,9},{8,6},{9,7},... | collective-permute-start | bytes 393224 | tf_op jit(solution)/shard_map/ppermute | solution.py:590
  89.3 5.7 %collective-permute-done.16.refs_2_ = bf16[8,16,512]{2,1,0:T(8,128)(2,1)S(1)} collective-permute-done((bf16[8,16,512]{2,1,0:T(8,128)(2,1)S(1)}, bf16[8,16,512]{2,1,0:T(8,128)(2,1)S(1)}, u32[]{:S(2)}, u32[]{:S(2)}) %collective-permute-start.16) | collective-permute-done | bytes 131104 | tf_op jit(solution)/shard_map/ppermute | solution.py:590
  95.0 1.0 collective-permute-start.21
  95.9 7.4 %collective-permute-done.18.refs_4_ = bf16[8,16,512]{2,1,0:T(8,128)(2,1)S(1)} collective-permute-done((bf16[8,16,512]{2,1,0:T(8,128)(2,1)S(1)}, bf16[8,16,512]{2,1,0:T(8,128)(2,1)S(1)}, u32[]{:S(2)}, u32[]{:S(2)}) %collective-permute-start.18) | collective-permute-done | bytes 131104 | tf_op jit(solution)/shard_map/ppermute | solution.py:590
  103.7 2.0 %restore_rows.1 = bf16[8,128,512]{2,1,0:T(8,128)(2,1)} custom-call(s32[5]{0:T(128)S(1)} %stack.15.info, bf16[8,16,512]{2,1,0:T(8,128)(2,1)S(1)} %get-tuple-element.57.refs_0_, bf16[8,16,512]{2,1,0:T(8,128)(2,1)S(1)} %collective-permute-done.15.refs_1_, bf16[8,16,512]{2,1,0:T(8,128)(2,1)S(1)} %collective-permute-done.16.refs_2_, ...), custom_call_target="tpu_custom_call" | custom-call | flops 1 | bytes 1 | tf_op jit(solution)/shard_map/restore_rows/pallas_call | solution.py:497
  (37 shorter events, 1.5 us)
Async XLA Ops:
  2.0 28.0 %copy-start.3 = (f32[3,3,2048]{2,1,0:T(4,128)S(1)}, f32[3,3,2048]{2,1,0:T(4,128)}, u32[]{:S(2)}) copy-start(f32[3,3,2048]{2,1,0:T(4,128)} %refs_3_.4) | copy-start | bytes 221188
  2.0 28.0 %copy-start.4 = (f32[2048]{0:T(1024)S(1)}, f32[2048]{0:T(1024)}, u32[]{:S(2)}) copy-start(f32[2048]{0:T(1024)} %param.16) | copy-start | bytes 24580
  2.0 28.0 %copy-start.5 = (f32[2048]{0:T(1024)S(1)}, f32[2048]{0:T(1024)}, u32[]{:S(2)}) copy-start(f32[2048]{0:T(1024)} %param.18) | copy-start | bytes 24580
  2.0 20.9 %collective-permute-start.3 = (bf16[512,512]{1,0:T(8,128)(2,1)S(1)}, bf16[512,512]{1,0:T(8,128)(2,1)S(1)}, u32[]{:S(2)}, u32[]{:S(2)}) collective-permute-start(bf16[512,512]{1,0:T(8,128)(2,1)S(1)} %get-tuple-element.36), channel_id=1, source_target_pairs={{0,16},{16,0},{1,17},{17,1},{2,18},{18,2},{3,19},{19,3},{4,20},{20... | collective-permute-start | bytes 1572872 | tf_op jit(solution)/shard_map/ppermute | solution.py:548
  5.1 23.2 %collective-permute-start.5 = (bf16[1024,256]{1,0:T(8,128)(2,1)S(1)}, bf16[1024,256]{1,0:T(8,128)(2,1)S(1)}, u32[]{:S(2)}, u32[]{:S(2)}) collective-permute-start(bf16[1024,256]{1,0:T(8,128)(2,1)S(1)} %get-tuple-element.37), channel_id=1, source_target_pairs={{0,16},{16,0},{1,17},{17,1},{2,18},{18,2},{3,19},{19,3},{4,20},{20... | collective-permute-start | bytes 1572872 | tf_op jit(solution)/shard_map/ppermute | solution.py:548
  6.7 7.2 %collective-permute-start.1 = (bf16[1,128,512]{2,1,0:T(8,128)(2,1)S(1)}, bf16[1,128,512]{2,1,0:T(8,128)(2,1)S(1)}, u32[]{:S(2)}, u32[]{:S(2)}) collective-permute-start(bf16[1,128,512]{2,1,0:T(8,128)(2,1)S(1)} %get-tuple-element.39), channel_id=1, source_target_pairs={{0,1},{1,2},{2,3},{3,4},{4,5},{5,6},{6,7},{7,8},{8,9},{9,10},{10,1... | collective-permute-start | bytes 393224 | tf_op jit(solution)/shard_map/ppermute | solution.py:556
  6.8 7.2 %collective-permute-start.2 = (bf16[1,128,512]{2,1,0:T(8,128)(2,1)S(1)}, bf16[1,128,512]{2,1,0:T(8,128)(2,1)S(1)}, u32[]{:S(2)}, u32[]{:S(2)}) collective-permute-start(bf16[1,128,512]{2,1,0:T(8,128)(2,1)S(1)} %get-tuple-element.40), channel_id=1, source_target_pairs={{1,0},{2,1},{3,2},{4,3},{5,4},{6,5},{7,6},{8,7},{9,8},{10,9},{11,1... | collective-permute-start | bytes 393224 | tf_op jit(solution)/shard_map/ppermute | solution.py:557
  22.9 10.8 %collective-permute-start.4 = (bf16[512,512]{1,0:T(8,128)(2,1)S(1)}, bf16[512,512]{1,0:T(8,128)(2,1)S(1)}, u32[]{:S(2)}, u32[]{:S(2)}) collective-permute-start(bf16[512,512]{1,0:T(8,128)(2,1)S(1)} %collective-permute-done.3.refs_1_), channel_id=1, source_target_pairs={{0,1},{1,0},{2,3},{3,2},{4,5},{5,4},{6,7},{7,6},{8,9},{9,8},{10,11... | collective-permute-start | bytes 1572872 | tf_op jit(solution)/shard_map/ppermute | solution.py:549
  28.2 9.4 %collective-permute-start.6 = (bf16[1024,256]{1,0:T(8,128)(2,1)S(1)}, bf16[1024,256]{1,0:T(8,128)(2,1)S(1)}, u32[]{:S(2)}, u32[]{:S(2)}) collective-permute-start(bf16[1024,256]{1,0:T(8,128)(2,1)S(1)} %collective-permute-done.5.refs_4_), channel_id=1, source_target_pairs={{0,1},{1,0},{2,3},{3,2},{4,5},{5,4},{6,7},{7,6},{8,9},{9,8},{10,11... | collective-permute-start | bytes 1572872 | tf_op jit(solution)/shard_map/ppermute | solution.py:549
  28.2 14.3 %collective-permute-start = (bf16[256,1024]{1,0:T(8,128)(2,1)S(1)}, bf16[256,1024]{1,0:T(8,128)(2,1)S(1)}, u32[]{:S(2)}, u32[]{:S(2)}) collective-permute-start(bf16[256,1024]{1,0:T(8,128)(2,1)S(1)} %get-tuple-element.35), channel_id=1, source_target_pairs={{0,16},{16,0},{1,17},{17,1},{2,18},{18,2},{3,19},{19,3},{4,20},{20... | collective-permute-start | bytes 1572872 | tf_op jit(solution)/shard_map/ppermute | solution.py:548
  33.7 3.9 %copy-start = (bf16[2048,256]{1,0:T(8,128)(2,1)S(1)}, bf16[2048,256]{1,0:T(8,128)(2,1)}, u32[]{:S(2)}) copy-start(bf16[2048,256]{1,0:T(8,128)(2,1)} %refs_3_.5) | copy-start | bytes 3145732
  37.7 32.9 %copy-start.1 = (bf16[512,768]{1,0:T(8,128)(2,1)S(1)}, bf16[512,768]{1,0:T(8,128)(2,1)}, u32[]{:S(2)}) copy-start(bf16[512,768]{1,0:T(8,128)(2,1)} %refs_0_.1) | copy-start | bytes 2359300
  37.7 32.9 %copy-start.2 = (bf16[512,256]{1,0:T(8,128)(2,1)S(1)}, bf16[512,256]{1,0:T(8,128)(2,1)}, u32[]{:S(2)}) copy-start(bf16[512,256]{1,0:T(8,128)(2,1)} %refs_1_.1) | copy-start | bytes 786436
  37.7 32.9 %copy-start.6 = (f32[512]{0:T(512)S(1)}, f32[512]{0:T(512)}, u32[]{:S(2)}) copy-start(f32[512]{0:T(512)} %param.20) | copy-start | bytes 6148
  37.7 32.9 %copy-start.7 = (f32[512]{0:T(512)S(1)}, f32[512]{0:T(512)}, u32[]{:S(2)}) copy-start(f32[512]{0:T(512)} %param.21) | copy-start | bytes 6148
  42.6 28.0 %collective-permute-start.7 = (bf16[256,1024]{1,0:T(8,128)(2,1)S(1)}, bf16[256,1024]{1,0:T(8,128)(2,1)S(1)}, u32[]{:S(2)}, u32[]{:S(2)}) collective-permute-start(bf16[256,1024]{1,0:T(8,128)(2,1)S(1)} %collective-permute-done.refs_2_), channel_id=1, source_target_pairs={{0,1},{1,0},{2,3},{3,2},{4,5},{5,4},{6,7},{7,6},{8,9},{9,8},{10,11... | collective-permute-start | bytes 1572872 | tf_op jit(solution)/shard_map/ppermute | solution.py:549
  42.6 7.3 %collective-permute-start.8 = (bf16[8,16,512]{2,1,0:T(8,128)(2,1)S(1)}, bf16[8,16,512]{2,1,0:T(8,128)(2,1)S(1)}, u32[]{:S(2)}, u32[]{:S(2)}) collective-permute-start(bf16[8,16,512]{2,1,0:T(8,128)(2,1)S(1)} %get-tuple-element.50), channel_id=1, source_target_pairs={{0,2},{1,3},{2,0},{3,1},{4,6},{5,7},{6,4},{7,5},{8,10},{9,11},{10,... | collective-permute-start | bytes 393224 | tf_op jit(solution)/shard_map/ppermute | solution.py:590
  44.3 15.7 %collective-permute-start.9 = (bf16[8,16,512]{2,1,0:T(8,128)(2,1)S(1)}, bf16[8,16,512]{2,1,0:T(8,128)(2,1)S(1)}, u32[]{:S(2)}, u32[]{:S(2)}) collective-permute-start(bf16[8,16,512]{2,1,0:T(8,128)(2,1)S(1)} %get-tuple-element.51), channel_id=1, source_target_pairs={{0,8},{1,9},{2,10},{3,11},{4,12},{5,13},{6,14},{7,15},{8,0},{9,1},... | collective-permute-start | bytes 393224 | tf_op jit(solution)/shard_map/ppermute | solution.py:590
  46.9 15.9 %collective-permute-start.10 = (bf16[8,16,512]{2,1,0:T(8,128)(2,1)S(1)}, bf16[8,16,512]{2,1,0:T(8,128)(2,1)S(1)}, u32[]{:S(2)}, u32[]{:S(2)}) collective-permute-start(bf16[8,16,512]{2,1,0:T(8,128)(2,1)S(1)} %get-tuple-element.52), channel_id=1, source_target_pairs={{0,12},{1,13},{2,14},{3,15},{4,8},{5,9},{6,10},{7,11},{8,4},{9,5},... | collective-permute-start | bytes 393224 | tf_op jit(solution)/shard_map/ppermute | solution.py:590
  48.2 19.9 %collective-permute-start.11 = (bf16[8,16,512]{2,1,0:T(8,128)(2,1)S(1)}, bf16[8,16,512]{2,1,0:T(8,128)(2,1)S(1)}, u32[]{:S(2)}, u32[]{:S(2)}) collective-permute-start(bf16[8,16,512]{2,1,0:T(8,128)(2,1)S(1)} %get-tuple-element.53), channel_id=1, source_target_pairs={{0,10},{1,11},{2,8},{3,9},{4,14},{5,15},{6,12},{7,13},{8,2},{9,3},... | collective-permute-start | bytes 393224 | tf_op jit(solution)/shard_map/ppermute | solution.py:590
  49.9 18.2 %collective-permute-start.12 = (bf16[8,16,512]{2,1,0:T(8,128)(2,1)S(1)}, bf16[8,16,512]{2,1,0:T(8,128)(2,1)S(1)}, u32[]{:S(2)}, u32[]{:S(2)}) collective-permute-start(bf16[8,16,512]{2,1,0:T(8,128)(2,1)S(1)} %get-tuple-element.54), channel_id=1, source_target_pairs={{0,4},{1,5},{2,6},{3,7},{4,0},{5,1},{6,2},{7,3},{8,12},{9,13},{10,... | collective-permute-start | bytes 393224 | tf_op jit(solution)/shard_map/ppermute | solution.py:590
  60.0 8.1 %collective-permute-start.13 = (bf16[8,16,512]{2,1,0:T(8,128)(2,1)S(1)}, bf16[8,16,512]{2,1,0:T(8,128)(2,1)S(1)}, u32[]{:S(2)}, u32[]{:S(2)}) collective-permute-start(bf16[8,16,512]{2,1,0:T(8,128)(2,1)S(1)} %get-tuple-element.55), channel_id=1, source_target_pairs={{0,14},{1,15},{2,12},{3,13},{4,10},{5,11},{6,8},{7,9},{8,6},{9,7},... | collective-permute-start | bytes 393224 | tf_op jit(solution)/shard_map/ppermute | solution.py:590
  62.8 7.8 %collective-permute-start.14 = (bf16[8,16,512]{2,1,0:T(8,128)(2,1)S(1)}, bf16[8,16,512]{2,1,0:T(8,128)(2,1)S(1)}, u32[]{:S(2)}, u32[]{:S(2)}) collective-permute-start(bf16[8,16,512]{2,1,0:T(8,128)(2,1)S(1)} %get-tuple-element.56), channel_id=1, source_target_pairs={{0,6},{1,7},{2,4},{3,5},{4,2},{5,3},{6,0},{7,1},{8,14},{9,15},{10,... | collective-permute-start | bytes 393224 | tf_op jit(solution)/shard_map/ppermute | solution.py:590
  77.6 9.3 %collective-permute-start.15 = (bf16[8,16,512]{2,1,0:T(8,128)(2,1)S(1)}, bf16[8,16,512]{2,1,0:T(8,128)(2,1)S(1)}, u32[]{:S(2)}, u32[]{:S(2)}) collective-permute-start(bf16[8,16,512]{2,1,0:T(8,128)(2,1)S(1)} %get-tuple-element.58), channel_id=1, source_target_pairs={{0,2},{1,3},{2,0},{3,1},{4,6},{5,7},{6,4},{7,5},{8,10},{9,11},{10,... | collective-permute-start | bytes 393224 | tf_op jit(solution)/shard_map/ppermute | solution.py:590
  79.1 15.9 %collective-permute-start.16 = (bf16[8,16,512]{2,1,0:T(8,128)(2,1)S(1)}, bf16[8,16,512]{2,1,0:T(8,128)(2,1)S(1)}, u32[]{:S(2)}, u32[]{:S(2)}) collective-permute-start(bf16[8,16,512]{2,1,0:T(8,128)(2,1)S(1)} %get-tuple-element.59), channel_id=1, source_target_pairs={{0,8},{1,9},{2,10},{3,11},{4,12},{5,13},{6,14},{7,15},{8,0},{9,1},... | collective-permute-start | bytes 393224 | tf_op jit(solution)/shard_map/ppermute | solution.py:590
  81.7 14.2 %collective-permute-start.17 = (bf16[8,16,512]{2,1,0:T(8,128)(2,1)S(1)}, bf16[8,16,512]{2,1,0:T(8,128)(2,1)S(1)}, u32[]{:S(2)}, u32[]{:S(2)}) collective-permute-start(bf16[8,16,512]{2,1,0:T(8,128)(2,1)S(1)} %get-tuple-element.60), channel_id=1, source_target_pairs={{0,12},{1,13},{2,14},{3,15},{4,8},{5,9},{6,10},{7,11},{8,4},{9,5},... | collective-permute-start | bytes 393224 | tf_op jit(solution)/shard_map/ppermute | solution.py:590
  84.0 19.4 %collective-permute-start.18 = (bf16[8,16,512]{2,1,0:T(8,128)(2,1)S(1)}, bf16[8,16,512]{2,1,0:T(8,128)(2,1)S(1)}, u32[]{:S(2)}, u32[]{:S(2)}) collective-permute-start(bf16[8,16,512]{2,1,0:T(8,128)(2,1)S(1)} %get-tuple-element.61), channel_id=1, source_target_pairs={{0,10},{1,11},{2,8},{3,9},{4,14},{5,15},{6,12},{7,13},{8,2},{9,3},... | collective-permute-start | bytes 393224 | tf_op jit(solution)/shard_map/ppermute | solution.py:590
  84.5 18.8 %collective-permute-start.19 = (bf16[8,16,512]{2,1,0:T(8,128)(2,1)S(1)}, bf16[8,16,512]{2,1,0:T(8,128)(2,1)S(1)}, u32[]{:S(2)}, u32[]{:S(2)}) collective-permute-start(bf16[8,16,512]{2,1,0:T(8,128)(2,1)S(1)} %get-tuple-element.62), channel_id=1, source_target_pairs={{0,4},{1,5},{2,6},{3,7},{4,0},{5,1},{6,2},{7,3},{8,12},{9,13},{10,... | collective-permute-start | bytes 393224 | tf_op jit(solution)/shard_map/ppermute | solution.py:590
  86.9 16.5 %collective-permute-start.20 = (bf16[8,16,512]{2,1,0:T(8,128)(2,1)S(1)}, bf16[8,16,512]{2,1,0:T(8,128)(2,1)S(1)}, u32[]{:S(2)}, u32[]{:S(2)}) collective-permute-start(bf16[8,16,512]{2,1,0:T(8,128)(2,1)S(1)} %get-tuple-element.63), channel_id=1, source_target_pairs={{0,14},{1,15},{2,12},{3,13},{4,10},{5,11},{6,8},{7,9},{8,6},{9,7},... | collective-permute-start | bytes 393224 | tf_op jit(solution)/shard_map/ppermute | solution.py:590
  95.0 8.7 %collective-permute-start.21 = (bf16[8,16,512]{2,1,0:T(8,128)(2,1)S(1)}, bf16[8,16,512]{2,1,0:T(8,128)(2,1)S(1)}, u32[]{:S(2)}, u32[]{:S(2)}) collective-permute-start(bf16[8,16,512]{2,1,0:T(8,128)(2,1)S(1)} %get-tuple-element.64), channel_id=1, source_target_pairs={{0,6},{1,7},{2,4},{3,5},{4,2},{5,3},{6,0},{7,1},{8,14},{9,15},{10,... | collective-permute-start | bytes 393224 | tf_op jit(solution)/shard_map/ppermute | solution.py:590

commit v6 on v5

--- a/solution.py
+++ b/solution.py
@@ -99,37 +99,37 @@
     )(info, in_hbm(image))
 
 
-def shares_kernel(info, expand, project, qkv, out, expand_part, project_part, rest_part, sems):
-    def span(part, axis):
-        size = part.shape[axis]
-        return pl.ds(pl.multiple_of(info[CORE] * size, size), size)
-
+def share_of(info, part, axis):
+    size = part.shape[axis]
+    return pl.ds(pl.multiple_of(info[CORE] * size, size), size)
+
+
+def expand_share_kernel(info, expand, part, sems):
+    for copy in copy_all([(expand.at[:, share_of(info, part, 1)], part)], sems):
+        copy.wait()
+
+
+def shares_kernel(info, project, qkv, out, project_part, rest_part, sems):
     width = qkv.shape[1]
     moves = [
-        (expand.at[:, span(expand_part, 1)], expand_part),
-        (project.at[span(project_part, 0)], project_part),
-        (qkv.at[span(rest_part, 0)], rest_part.at[:, :width]),
-        (out.at[span(rest_part, 0)], rest_part.at[:, width:]),
+        (project.at[share_of(info, project_part, 0)], project_part),
+        (qkv.at[share_of(info, rest_part, 0)], rest_part.at[:, :width]),
+        (out.at[share_of(info, rest_part, 0)], rest_part.at[:, width:]),
     ]
     for copy in copy_all(moves, sems):
         copy.wait()
 
 
-def share_weights(info, w_expand, w_project, w_qkv, w_out):
-    shapes = [
-        (w_expand.shape[0], w_expand.shape[1] // 2),
-        (w_project.shape[0] // 2, w_project.shape[1]),
-        (w_qkv.shape[0] // 2, w_qkv.shape[1] + w_out.shape[1]),
-    ]
+def share_weights(kernel, info, weights, shapes, name):
     return pl.pallas_call(
-        shares_kernel,
-        in_specs=[smem()] + [hbm()] * 4,
-        out_specs=[vmem()] * 3,
+        kernel,
+        in_specs=[smem()] + [hbm()] * len(weights),
+        out_specs=[vmem()] * len(shapes),
         out_shape=[jax.ShapeDtypeStruct(shape, BF16) for shape in shapes],
-        scratch_shapes=[pltpu.SemaphoreType.DMA((4,))],
+        scratch_shapes=[pltpu.SemaphoreType.DMA((len(weights),))],
         compiler_params=params(),
-        name="share_weights",
-    )(info, *map(in_hbm, (w_expand, w_project, w_qkv, w_out)))
+        name=name,
+    )(info, *map(in_hbm, weights))
 
 
 def order_kernel(image, above, below, scale, shift, ordered, normed):
@@ -549,8 +549,17 @@
     over_core = lambda w: lax.ppermute(w, "space", [(i, i ^ 1) for i in range(space)])
     later = info
     if pairs:
-        mine = share_weights(info, w_expand, w_project, w_qkv, w_out)
-        expand_got, project_got, rest_got = map(over_dp, mine)
+        shape = (chans, w_expand.shape[1] // 2)
+        mine = share_weights(expand_share_kernel, info, [w_expand], [shape], "expand_share")
+        expand_got = over_dp(mine[0])
+        shapes = [
+            (w_project.shape[0] // 2, w_project.shape[1]),
+            (chans // 2, w_qkv.shape[1] + w_out.shape[1]),
+        ]
+        mine = share_weights(
+            shares_kernel, after(info, *mine), [w_project, w_qkv, w_out], shapes, "other_shares"
+        )
+        project_got, rest_got = map(over_dp, mine)
         later = after(info, *mine)
     top, bottom = edge_rows(later, image)
     above = lax.ppermute(bottom, "space", [(i, (i + 1) % space) for i in range(space)])

time: 106 us -> 106 us (level)
  waiting for transfers between devices: 38.5 us -> 36.7 us
  Pallas kernels: 32.1 us -> 33.5 us
    ppermute x3, waiting for transfers between devices: 6.11 us -> 4.25 us  [local(): over_dp = lambda w: lax.ppermute(w, 'dp', [(0, 1), (1, 0)])]
    pallas_call x1 -> x2, Pallas kernels: 1.92 us -> 3.34 us  [share_weights(): pl.pallas_call(kernel, in_specs=[smem()] + [hbm()] * len(weights), out_sp...]
  transfers between devices with their start and end apart: 22 -> 22, of which waited for: 9 -> 9; matrix products, arithmetic and copies ran while one was open for 0% -> 0% of each run, Pallas kernels for 20% -> 22%
where the time goes in v6:
time: 106 us; the launch traced here: 105 us
  waiting for transfers between devices  36.7 us (35%)
  starting transfers between devices  34.8 us (33%)
  Pallas kernels  33.5 us (32%)
    ppermute x14, waiting for transfers between devices, exchange(): parts[n] = lax.ppermute(parts[n], 'space', swap)  29.6 us
    ppermute x14, starting transfers between devices, exchange(): parts[n] = lax.ppermute(parts[n], 'space', swap)  24.4 us
    pallas_call x3, Pallas kernels, expand_some(): pl.pallas_call(functools.partial(expand_kernel, first, tile_of), grid_spe...  16.6 us
    pallas_call x1, Pallas kernels, attend(): pl.pallas_call(functools.partial(attend_kernel, 1 + len(rest), len(tokens...  7 us
    ppermute x3, starting transfers between devices, local(): over_dp = lambda w: lax.ppermute(w, 'dp', [(0, 1), (1, 0)])  4.85 us
    ppermute x1, starting transfers between devices, local(): lax.ppermute(top, 'space', [((i + 1) % space, i) for i in range(space)])  4.43 us
    ppermute x3, waiting for transfers between devices, local(): over_dp = lambda w: lax.ppermute(w, 'dp', [(0, 1), (1, 0)])  4.25 us
    pallas_call x2, Pallas kernels, share_weights(): pl.pallas_call(kernel, in_specs=[smem()] + [hbm()] * len(weights), out_sp...  3.34 us
  transfers between devices with their start and end apart: 22, of which 9 were waited for; matrix products, arithmetic and copies ran while one was open for 0% of the time, Pallas kernels for 22%

profile of v6, /device:TPU:0, one launch (start us, length us, event | category | flops | bytes accessed | tf_op | source)
XLA Modules:
  0.0 105.3 jit_solution(5000741621843817252)
XLA Ops:
  0.1 1.6 %expand_share.1 = bf16[512,512]{1,0:T(8,128)(2,1)S(1)} custom-call(s32[5]{0:T(128)S(1)} %stack.15.info, bf16[512,1024]{1,0:T(8,128)(2,1)} %refs_5_.1), custom_call_target="tpu_custom_call" | custom-call | tf_op jit(solution)/shard_map/expand_share/pallas_call | solution.py:124
  1.7 3.0 %collective-permute-start.3 = (bf16[512,512]{1,0:T(8,128)(2,1)S(1)}, bf16[512,512]{1,0:T(8,128)(2,1)S(1)}, u32[]{:S(2)}, u32[]{:S(2)}) collective-permute-start(bf16[512,512]{1,0:T(8,128)(2,1)S(1)} %expand_share.1), channel_id=1, source_target_pairs={{0,16},{16,0},{1,17},{17,1},{2,18},{18,2},{3,19},{19,3},{4,20},{20... | collective-permute-start | bytes 1572872 | tf_op jit(solution)/shard_map/ppermute | solution.py:548
  4.7 1.7 %other_shares.1 = (bf16[1024,256]{1,0:T(8,128)(2,1)S(1)}, bf16[256,1024]{1,0:T(8,128)(2,1)S(1)}) custom-call(s32[5]{0:T(128)S(1)} %stack.15.info, bf16[2048,256]{1,0:T(8,128)(2,1)} %refs_3_.5, bf16[512,768]{1,0:T(8,128)(2,1)} %refs_0_.1, bf16[512,256]{1,0:T(8,128)(2,1)} %refs_1_.1), custom_call_target="tpu_custom_call" | custom-call | tf_op jit(solution)/shard_map/other_shares/pallas_call | solution.py:124
  6.6 1.5 %edge_rows.1 = (bf16[1,128,512]{2,1,0:T(8,128)(2,1)S(1)}, bf16[1,128,512]{2,1,0:T(8,128)(2,1)S(1)}) custom-call(s32[5]{0:T(128)S(1)} %stack.15.info, bf16[8,128,512]{2,1,0:T(8,128)(2,1)} %bitcast.19), custom_call_target="tpu_custom_call" | custom-call | tf_op jit(solution)/shard_map/edge_rows/pallas_call | solution.py:91
  8.2 4.4 %collective-permute-start.2 = (bf16[1,128,512]{2,1,0:T(8,128)(2,1)S(1)}, bf16[1,128,512]{2,1,0:T(8,128)(2,1)S(1)}, u32[]{:S(2)}, u32[]{:S(2)}) collective-permute-start(bf16[1,128,512]{2,1,0:T(8,128)(2,1)S(1)} %get-tuple-element.40), channel_id=1, source_target_pairs={{1,0},{2,1},{3,2},{4,3},{5,4},{6,5},{7,6},{8,7},{9,8},{10,9},{11,1... | collective-permute-start | bytes 393224 | tf_op jit(solution)/shard_map/ppermute | solution.py:566
  12.6 2.8 %collective-permute-done.1.refs_1_ = bf16[1,128,512]{2,1,0:T(8,128)(2,1)S(1)} collective-permute-done((bf16[1,128,512]{2,1,0:T(8,128)(2,1)S(1)}, bf16[1,128,512]{2,1,0:T(8,128)(2,1)S(1)}, u32[]{:S(2)}, u32[]{:S(2)}) %collective-permute-start.1) | collective-permute-done | bytes 131104 | tf_op jit(solution)/shard_map/ppermute | solution.py:565
  15.4 9.0 %expand_conv.3 = (bf16[1024,1024]{1,0:T(8,128)(2,1)S(1)}, bf16[8,128,512]{2,1,0:T(8,128)(2,1)S(1)}, bf16[10,128,512]{2,1,0:T(8,128)(2,1)S(1)}) custom-call(s32[5]{0:T(128)S(1)} %stack.15.info, bf16[8,128,512]{2,1,0:T(8,128)(2,1)} %bitcast.20, bf16[1,128,512]{2,1,0:T(8,128)(2,1)S(1)} %collective-permute-done.1.refs_1_, ...), custom_call_target="tpu_custom_call" | custom-call | flops 1 | bytes 1 | tf_op jit(solution)/shard_map/expand_conv/pallas_call | solution.py:261
  24.4 1.1 %collective-permute-start.4 = (bf16[512,512]{1,0:T(8,128)(2,1)S(1)}, bf16[512,512]{1,0:T(8,128)(2,1)S(1)}, u32[]{:S(2)}, u32[]{:S(2)}) collective-permute-start(bf16[512,512]{1,0:T(8,128)(2,1)S(1)} %collective-permute-done.3.refs_1_), channel_id=1, source_target_pairs={{0,1},{1,0},{2,3},{3,2},{4,5},{5,4},{6,7},{7,6},{8,9},{9,8},{10,11... | collective-permute-start | bytes 1572872 | tf_op jit(solution)/shard_map/ppermute | solution.py:549
  25.4 2.5 %collective-permute-done.5.refs_4_ = bf16[1024,256]{1,0:T(8,128)(2,1)S(1)} collective-permute-done((bf16[1024,256]{1,0:T(8,128)(2,1)S(1)}, bf16[1024,256]{1,0:T(8,128)(2,1)S(1)}, u32[]{:S(2)}, u32[]{:S(2)}) %collective-permute-start.5) | collective-permute-done | bytes 524320 | tf_op jit(solution)/shard_map/ppermute | solution.py:548
  27.9 1.7 %collective-permute-start = (bf16[256,1024]{1,0:T(8,128)(2,1)S(1)}, bf16[256,1024]{1,0:T(8,128)(2,1)S(1)}, u32[]{:S(2)}, u32[]{:S(2)}) collective-permute-start(bf16[256,1024]{1,0:T(8,128)(2,1)S(1)} %get-tuple-element.36), channel_id=1, source_target_pairs={{0,16},{16,0},{1,17},{17,1},{2,18},{18,2},{3,19},{19,3},{4,20},{20... | collective-permute-start | bytes 1572872 | tf_op jit(solution)/shard_map/ppermute | solution.py:548
  29.6 3.7 %expand_conv.4.refs_1_ = bf16[1024,512]{1,0:T(8,128)(2,1)S(1)} custom-call(s32[5]{0:T(128)S(1)} %stack.15.info, bf16[10,128,512]{2,1,0:T(8,128)(2,1)S(1)} %get-tuple-element.45.refs_0_, bf16[512,512]{1,0:T(8,128)(2,1)S(1)} %collective-permute-done.3.refs_1_, f32[1,2048]{1,0:T(1,128)S(1)} %bitcast.12, f32[3,3,2048]{2,1,0:T(4,128)S(1)} %copy-done.3, ...), custom_call_target="tpu_custom_call" | custom-call | flops 1 | bytes 1 | tf_op jit(solution)/shard_map/expand_conv/pallas_call | solution.py:261
  33.4 3.9 %expand_conv.5.refs_2_ = bf16[1024,512]{1,0:T(8,128)(2,1)S(1)} custom-call(s32[5]{0:T(128)S(1)} %stack.15.info, bf16[10,128,512]{2,1,0:T(8,128)(2,1)S(1)} %get-tuple-element.45.refs_0_, bf16[512,512]{1,0:T(8,128)(2,1)S(1)} %collective-permute-done.4.refs_1_, f32[1,2048]{1,0:T(1,128)S(1)} %bitcast.13, f32[3,3,2048]{2,1,0:T(4,128)S(1)} %copy-done.3, ...), custom_call_target="tpu_custom_call" | custom-call | flops 1 | bytes 1 | tf_op jit(solution)/shard_map/expand_conv/pallas_call | solution.py:261
  37.3 3.1 %project_rows.1 = (bf16[8,16,512]{2,1,0:T(8,128)(2,1)S(1)}, bf16[8,16,512]{2,1,0:T(8,128)(2,1)S(1)}, bf16[8,16,512]{2,1,0:T(8,128)(2,1)S(1)}, bf16[8,16,512]{2,1...) custom-call(s32[5]{0:T(128)S(1)} %stack.15.info, ...), custom_call_target="tpu_custom_call" | custom-call | flops 1 | bytes 1 | tf_op jit(solution)/shard_map/project_rows/pallas_call | solution.py:349
  40.4 1.8 %collective-permute-done.refs_2_ = bf16[256,1024]{1,0:T(8,128)(2,1)S(1)} collective-permute-done((bf16[256,1024]{1,0:T(8,128)(2,1)S(1)}, bf16[256,1024]{1,0:T(8,128)(2,1)S(1)}, u32[]{:S(2)}, u32[]{:S(2)}) %collective-permute-start) | collective-permute-done | bytes 524320 | tf_op jit(solution)/shard_map/ppermute | solution.py:548
  42.2 1.7 %collective-permute-start.8 = (bf16[8,16,512]{2,1,0:T(8,128)(2,1)S(1)}, bf16[8,16,512]{2,1,0:T(8,128)(2,1)S(1)}, u32[]{:S(2)}, u32[]{:S(2)}) collective-permute-start(bf16[8,16,512]{2,1,0:T(8,128)(2,1)S(1)} %get-tuple-element.50), channel_id=1, source_target_pairs={{0,2},{1,3},{2,0},{3,1},{4,6},{5,7},{6,4},{7,5},{8,10},{9,11},{10,... | collective-permute-start | bytes 393224 | tf_op jit(solution)/shard_map/ppermute | solution.py:599
  43.9 2.6 %collective-permute-start.9 = (bf16[8,16,512]{2,1,0:T(8,128)(2,1)S(1)}, bf16[8,16,512]{2,1,0:T(8,128)(2,1)S(1)}, u32[]{:S(2)}, u32[]{:S(2)}) collective-permute-start(bf16[8,16,512]{2,1,0:T(8,128)(2,1)S(1)} %get-tuple-element.51), channel_id=1, source_target_pairs={{0,8},{1,9},{2,10},{3,11},{4,12},{5,13},{6,14},{7,15},{8,0},{9,1},... | collective-permute-start | bytes 393224 | tf_op jit(solution)/shard_map/ppermute | solution.py:599
  46.5 1.3 %collective-permute-start.10 = (bf16[8,16,512]{2,1,0:T(8,128)(2,1)S(1)}, bf16[8,16,512]{2,1,0:T(8,128)(2,1)S(1)}, u32[]{:S(2)}, u32[]{:S(2)}) collective-permute-start(bf16[8,16,512]{2,1,0:T(8,128)(2,1)S(1)} %get-tuple-element.52), channel_id=1, source_target_pairs={{0,12},{1,13},{2,14},{3,15},{4,8},{5,9},{6,10},{7,11},{8,4},{9,5},... | collective-permute-start | bytes 393224 | tf_op jit(solution)/shard_map/ppermute | solution.py:599
  47.9 1.7 %collective-permute-start.11 = (bf16[8,16,512]{2,1,0:T(8,128)(2,1)S(1)}, bf16[8,16,512]{2,1,0:T(8,128)(2,1)S(1)}, u32[]{:S(2)}, u32[]{:S(2)}) collective-permute-start(bf16[8,16,512]{2,1,0:T(8,128)(2,1)S(1)} %get-tuple-element.53), channel_id=1, source_target_pairs={{0,10},{1,11},{2,8},{3,9},{4,14},{5,15},{6,12},{7,13},{8,2},{9,3},... | collective-permute-start | bytes 393224 | tf_op jit(solution)/shard_map/ppermute | solution.py:599
  49.5 1.3 %collective-permute-start.12 = (bf16[8,16,512]{2,1,0:T(8,128)(2,1)S(1)}, bf16[8,16,512]{2,1,0:T(8,128)(2,1)S(1)}, u32[]{:S(2)}, u32[]{:S(2)}) collective-permute-start(bf16[8,16,512]{2,1,0:T(8,128)(2,1)S(1)} %get-tuple-element.54), channel_id=1, source_target_pairs={{0,4},{1,5},{2,6},{3,7},{4,0},{5,1},{6,2},{7,3},{8,12},{9,13},{10,... | collective-permute-start | bytes 393224 | tf_op jit(solution)/shard_map/ppermute | solution.py:599
  50.9 8.7 %collective-permute-done.9.refs_6_ = bf16[8,16,512]{2,1,0:T(8,128)(2,1)S(1)} collective-permute-done((bf16[8,16,512]{2,1,0:T(8,128)(2,1)S(1)}, bf16[8,16,512]{2,1,0:T(8,128)(2,1)S(1)}, u32[]{:S(2)}, u32[]{:S(2)}) %collective-permute-start.9) | collective-permute-done | bytes 131104 | tf_op jit(solution)/shard_map/ppermute | solution.py:599
  59.6 2.8 %collective-permute-start.13 = (bf16[8,16,512]{2,1,0:T(8,128)(2,1)S(1)}, bf16[8,16,512]{2,1,0:T(8,128)(2,1)S(1)}, u32[]{:S(2)}, u32[]{:S(2)}) collective-permute-start(bf16[8,16,512]{2,1,0:T(8,128)(2,1)S(1)} %get-tuple-element.55), channel_id=1, source_target_pairs={{0,14},{1,15},{2,12},{3,13},{4,10},{5,11},{6,8},{7,9},{8,6},{9,7},... | collective-permute-start | bytes 393224 | tf_op jit(solution)/shard_map/ppermute | solution.py:599
  62.7 5.1 %collective-permute-done.11.refs_8_ = bf16[8,16,512]{2,1,0:T(8,128)(2,1)S(1)} collective-permute-done((bf16[8,16,512]{2,1,0:T(8,128)(2,1)S(1)}, bf16[8,16,512]{2,1,0:T(8,128)(2,1)S(1)}, u32[]{:S(2)}, u32[]{:S(2)}) %collective-permute-start.11) | collective-permute-done | bytes 131104 | tf_op jit(solution)/shard_map/ppermute | solution.py:599
  67.8 2.4 %collective-permute-done.14.refs_11_ = bf16[8,16,512]{2,1,0:T(8,128)(2,1)S(1)} collective-permute-done((bf16[8,16,512]{2,1,0:T(8,128)(2,1)S(1)}, bf16[8,16,512]{2,1,0:T(8,128)(2,1)S(1)}, u32[]{:S(2)}, u32[]{:S(2)}) %collective-permute-start.14) | collective-permute-done | bytes 131104 | tf_op jit(solution)/shard_map/ppermute | solution.py:599
  70.2 7.0 %attend.1 = (bf16[8,16,512]{2,1,0:T(8,128)(2,1)S(1)}, bf16[8,16,512]{2,1,0:T(8,128)(2,1)S(1)}, bf16[8,16,512]{2,1,0:T(8,128)(2,1)S(1)}, bf16[8,16,512]{2,1,0:T(8...) custom-call(s32[5]{0:T(128)S(1)} %stack.15.info, ...), custom_call_target="tpu_custom_call" | custom-call | flops 1 | bytes 1 | tf_op jit(solution)/shard_map/attend/pallas_call | solution.py:452
  77.2 1.5 %collective-permute-start.15 = (bf16[8,16,512]{2,1,0:T(8,128)(2,1)S(1)}, bf16[8,16,512]{2,1,0:T(8,128)(2,1)S(1)}, u32[]{:S(2)}, u32[]{:S(2)}) collective-permute-start(bf16[8,16,512]{2,1,0:T(8,128)(2,1)S(1)} %get-tuple-element.58), channel_id=1, source_target_pairs={{0,2},{1,3},{2,0},{3,1},{4,6},{5,7},{6,4},{7,5},{8,10},{9,11},{10,... | collective-permute-start | bytes 393224 | tf_op jit(solution)/shard_map/ppermute | solution.py:599
  78.7 2.6 %collective-permute-start.16 = (bf16[8,16,512]{2,1,0:T(8,128)(2,1)S(1)}, bf16[8,16,512]{2,1,0:T(8,128)(2,1)S(1)}, u32[]{:S(2)}, u32[]{:S(2)}) collective-permute-start(bf16[8,16,512]{2,1,0:T(8,128)(2,1)S(1)} %get-tuple-element.59), channel_id=1, source_target_pairs={{0,8},{1,9},{2,10},{3,11},{4,12},{5,13},{6,14},{7,15},{8,0},{9,1},... | collective-permute-start | bytes 393224 | tf_op jit(solution)/shard_map/ppermute | solution.py:599
  81.4 2.2 %collective-permute-start.17 = (bf16[8,16,512]{2,1,0:T(8,128)(2,1)S(1)}, bf16[8,16,512]{2,1,0:T(8,128)(2,1)S(1)}, u32[]{:S(2)}, u32[]{:S(2)}) collective-permute-start(bf16[8,16,512]{2,1,0:T(8,128)(2,1)S(1)} %get-tuple-element.60), channel_id=1, source_target_pairs={{0,12},{1,13},{2,14},{3,15},{4,8},{5,9},{6,10},{7,11},{8,4},{9,5},... | collective-permute-start | bytes 393224 | tf_op jit(solution)/shard_map/ppermute | solution.py:599
  84.2 2.3 %collective-permute-start.19 = (bf16[8,16,512]{2,1,0:T(8,128)(2,1)S(1)}, bf16[8,16,512]{2,1,0:T(8,128)(2,1)S(1)}, u32[]{:S(2)}, u32[]{:S(2)}) collective-permute-start(bf16[8,16,512]{2,1,0:T(8,128)(2,1)S(1)} %get-tuple-element.62), channel_id=1, source_target_pairs={{0,4},{1,5},{2,6},{3,7},{4,0},{5,1},{6,2},{7,3},{8,12},{9,13},{10,... | collective-permute-start | bytes 393224 | tf_op jit(solution)/shard_map/ppermute | solution.py:599
  86.5 2.4 %collective-permute-start.20 = (bf16[8,16,512]{2,1,0:T(8,128)(2,1)S(1)}, bf16[8,16,512]{2,1,0:T(8,128)(2,1)S(1)}, u32[]{:S(2)}, u32[]{:S(2)}) collective-permute-start(bf16[8,16,512]{2,1,0:T(8,128)(2,1)S(1)} %get-tuple-element.63), channel_id=1, source_target_pairs={{0,14},{1,15},{2,12},{3,13},{4,10},{5,11},{6,8},{7,9},{8,6},{9,7},... | collective-permute-start | bytes 393224 | tf_op jit(solution)/shard_map/ppermute | solution.py:599
  88.9 5.7 %collective-permute-done.16.refs_2_ = bf16[8,16,512]{2,1,0:T(8,128)(2,1)S(1)} collective-permute-done((bf16[8,16,512]{2,1,0:T(8,128)(2,1)S(1)}, bf16[8,16,512]{2,1,0:T(8,128)(2,1)S(1)}, u32[]{:S(2)}, u32[]{:S(2)}) %collective-permute-start.16) | collective-permute-done | bytes 131104 | tf_op jit(solution)/shard_map/ppermute | solution.py:599
  95.6 7.4 %collective-permute-done.18.refs_4_ = bf16[8,16,512]{2,1,0:T(8,128)(2,1)S(1)} collective-permute-done((bf16[8,16,512]{2,1,0:T(8,128)(2,1)S(1)}, bf16[8,16,512]{2,1,0:T(8,128)(2,1)S(1)}, u32[]{:S(2)}, u32[]{:S(2)}) %collective-permute-start.18) | collective-permute-done | bytes 131104 | tf_op jit(solution)/shard_map/ppermute | solution.py:599
  103.3 2.0 %restore_rows.1 = bf16[8,128,512]{2,1,0:T(8,128)(2,1)} custom-call(s32[5]{0:T(128)S(1)} %stack.15.info, bf16[8,16,512]{2,1,0:T(8,128)(2,1)S(1)} %get-tuple-element.57.refs_0_, bf16[8,16,512]{2,1,0:T(8,128)(2,1)S(1)} %collective-permute-done.15.refs_1_, bf16[8,16,512]{2,1,0:T(8,128)(2,1)S(1)} %collective-permute-done.16.refs_2_, ...), custom_call_target="tpu_custom_call" | custom-call | flops 1 | bytes 1 | tf_op jit(solution)/shard_map/restore_rows/pallas_call | solution.py:497
  (38 shorter events, 2.5 us)
Async XLA Ops:
  1.7 22.7 %collective-permute-start.3 = (bf16[512,512]{1,0:T(8,128)(2,1)S(1)}, bf16[512,512]{1,0:T(8,128)(2,1)S(1)}, u32[]{:S(2)}, u32[]{:S(2)}) collective-permute-start(bf16[512,512]{1,0:T(8,128)(2,1)S(1)} %expand_share.1), channel_id=1, source_target_pairs={{0,16},{16,0},{1,17},{17,1},{2,18},{18,2},{3,19},{19,3},{4,20},{20... | collective-permute-start | bytes 1572872 | tf_op jit(solution)/shard_map/ppermute | solution.py:548
  6.5 23.1 %copy-start.3 = (f32[3,3,2048]{2,1,0:T(4,128)S(1)}, f32[3,3,2048]{2,1,0:T(4,128)}, u32[]{:S(2)}) copy-start(f32[3,3,2048]{2,1,0:T(4,128)} %refs_3_.4) | copy-start | bytes 221188
  6.5 23.1 %copy-start.4 = (f32[2048]{0:T(1024)S(1)}, f32[2048]{0:T(1024)}, u32[]{:S(2)}) copy-start(f32[2048]{0:T(1024)} %param.16) | copy-start | bytes 24580
  6.5 23.1 %copy-start.5 = (f32[2048]{0:T(1024)S(1)}, f32[2048]{0:T(1024)}, u32[]{:S(2)}) copy-start(f32[2048]{0:T(1024)} %param.18) | copy-start | bytes 24580
  6.5 21.4 %collective-permute-start.5 = (bf16[1024,256]{1,0:T(8,128)(2,1)S(1)}, bf16[1024,256]{1,0:T(8,128)(2,1)S(1)}, u32[]{:S(2)}, u32[]{:S(2)}) collective-permute-start(bf16[1024,256]{1,0:T(8,128)(2,1)S(1)} %get-tuple-element.37), channel_id=1, source_target_pairs={{0,16},{16,0},{1,17},{17,1},{2,18},{18,2},{3,19},{19,3},{4,20},{20... | collective-permute-start | bytes 1572872 | tf_op jit(solution)/shard_map/ppermute | solution.py:548
  8.1 7.2 %collective-permute-start.1 = (bf16[1,128,512]{2,1,0:T(8,128)(2,1)S(1)}, bf16[1,128,512]{2,1,0:T(8,128)(2,1)S(1)}, u32[]{:S(2)}, u32[]{:S(2)}) collective-permute-start(bf16[1,128,512]{2,1,0:T(8,128)(2,1)S(1)} %get-tuple-element.39), channel_id=1, source_target_pairs={{0,1},{1,2},{2,3},{3,4},{4,5},{5,6},{6,7},{7,8},{8,9},{9,10},{10,1... | collective-permute-start | bytes 393224 | tf_op jit(solution)/shard_map/ppermute | solution.py:565
  8.2 7.2 %collective-permute-start.2 = (bf16[1,128,512]{2,1,0:T(8,128)(2,1)S(1)}, bf16[1,128,512]{2,1,0:T(8,128)(2,1)S(1)}, u32[]{:S(2)}, u32[]{:S(2)}) collective-permute-start(bf16[1,128,512]{2,1,0:T(8,128)(2,1)S(1)} %get-tuple-element.40), channel_id=1, source_target_pairs={{1,0},{2,1},{3,2},{4,3},{5,4},{6,5},{7,6},{8,7},{9,8},{10,9},{11,1... | collective-permute-start | bytes 393224 | tf_op jit(solution)/shard_map/ppermute | solution.py:566
  24.4 9.0 %collective-permute-start.4 = (bf16[512,512]{1,0:T(8,128)(2,1)S(1)}, bf16[512,512]{1,0:T(8,128)(2,1)S(1)}, u32[]{:S(2)}, u32[]{:S(2)}) collective-permute-start(bf16[512,512]{1,0:T(8,128)(2,1)S(1)} %collective-permute-done.3.refs_1_), channel_id=1, source_target_pairs={{0,1},{1,0},{2,3},{3,2},{4,5},{5,4},{6,7},{7,6},{8,9},{9,8},{10,11... | collective-permute-start | bytes 1572872 | tf_op jit(solution)/shard_map/ppermute | solution.py:549
  27.9 9.4 %collective-permute-start.6 = (bf16[1024,256]{1,0:T(8,128)(2,1)S(1)}, bf16[1024,256]{1,0:T(8,128)(2,1)S(1)}, u32[]{:S(2)}, u32[]{:S(2)}) collective-permute-start(bf16[1024,256]{1,0:T(8,128)(2,1)S(1)} %collective-permute-done.5.refs_4_), channel_id=1, source_target_pairs={{0,1},{1,0},{2,3},{3,2},{4,5},{5,4},{6,7},{7,6},{8,9},{9,8},{10,11... | collective-permute-start | bytes 1572872 | tf_op jit(solution)/shard_map/ppermute | solution.py:549
  27.9 14.3 %collective-permute-start = (bf16[256,1024]{1,0:T(8,128)(2,1)S(1)}, bf16[256,1024]{1,0:T(8,128)(2,1)S(1)}, u32[]{:S(2)}, u32[]{:S(2)}) collective-permute-start(bf16[256,1024]{1,0:T(8,128)(2,1)S(1)} %get-tuple-element.36), channel_id=1, source_target_pairs={{0,16},{16,0},{1,17},{17,1},{2,18},{18,2},{3,19},{19,3},{4,20},{20... | collective-permute-start | bytes 1572872 | tf_op jit(solution)/shard_map/ppermute | solution.py:548
  33.4 3.9 %copy-start = (bf16[2048,256]{1,0:T(8,128)(2,1)S(1)}, bf16[2048,256]{1,0:T(8,128)(2,1)}, u32[]{:S(2)}) copy-start(bf16[2048,256]{1,0:T(8,128)(2,1)} %refs_3_.5) | copy-start | bytes 3145732
  37.3 32.9 %copy-start.1 = (bf16[512,768]{1,0:T(8,128)(2,1)S(1)}, bf16[512,768]{1,0:T(8,128)(2,1)}, u32[]{:S(2)}) copy-start(bf16[512,768]{1,0:T(8,128)(2,1)} %refs_0_.1) | copy-start | bytes 2359300
  37.3 32.9 %copy-start.2 = (bf16[512,256]{1,0:T(8,128)(2,1)S(1)}, bf16[512,256]{1,0:T(8,128)(2,1)}, u32[]{:S(2)}) copy-start(bf16[512,256]{1,0:T(8,128)(2,1)} %refs_1_.1) | copy-start | bytes 786436
  37.3 32.9 %copy-start.6 = (f32[512]{0:T(512)S(1)}, f32[512]{0:T(512)}, u32[]{:S(2)}) copy-start(f32[512]{0:T(512)} %param.20) | copy-start | bytes 6148
  37.3 32.9 %copy-start.7 = (f32[512]{0:T(512)S(1)}, f32[512]{0:T(512)}, u32[]{:S(2)}) copy-start(f32[512]{0:T(512)} %param.21) | copy-start | bytes 6148
  42.2 28.0 %collective-permute-start.7 = (bf16[256,1024]{1,0:T(8,128)(2,1)S(1)}, bf16[256,1024]{1,0:T(8,128)(2,1)S(1)}, u32[]{:S(2)}, u32[]{:S(2)}) collective-permute-start(bf16[256,1024]{1,0:T(8,128)(2,1)S(1)} %collective-permute-done.refs_2_), channel_id=1, source_target_pairs={{0,1},{1,0},{2,3},{3,2},{4,5},{5,4},{6,7},{7,6},{8,9},{9,8},{10,11... | collective-permute-start | bytes 1572872 | tf_op jit(solution)/shard_map/ppermute | solution.py:549
  42.2 7.3 %collective-permute-start.8 = (bf16[8,16,512]{2,1,0:T(8,128)(2,1)S(1)}, bf16[8,16,512]{2,1,0:T(8,128)(2,1)S(1)}, u32[]{:S(2)}, u32[]{:S(2)}) collective-permute-start(bf16[8,16,512]{2,1,0:T(8,128)(2,1)S(1)} %get-tuple-element.50), channel_id=1, source_target_pairs={{0,2},{1,3},{2,0},{3,1},{4,6},{5,7},{6,4},{7,5},{8,10},{9,11},{10,... | collective-permute-start | bytes 393224 | tf_op jit(solution)/shard_map/ppermute | solution.py:599
  43.9 15.7 %collective-permute-start.9 = (bf16[8,16,512]{2,1,0:T(8,128)(2,1)S(1)}, bf16[8,16,512]{2,1,0:T(8,128)(2,1)S(1)}, u32[]{:S(2)}, u32[]{:S(2)}) collective-permute-start(bf16[8,16,512]{2,1,0:T(8,128)(2,1)S(1)} %get-tuple-element.51), channel_id=1, source_target_pairs={{0,8},{1,9},{2,10},{3,11},{4,12},{5,13},{6,14},{7,15},{8,0},{9,1},... | collective-permute-start | bytes 393224 | tf_op jit(solution)/shard_map/ppermute | solution.py:599
  46.5 15.9 %collective-permute-start.10 = (bf16[8,16,512]{2,1,0:T(8,128)(2,1)S(1)}, bf16[8,16,512]{2,1,0:T(8,128)(2,1)S(1)}, u32[]{:S(2)}, u32[]{:S(2)}) collective-permute-start(bf16[8,16,512]{2,1,0:T(8,128)(2,1)S(1)} %get-tuple-element.52), channel_id=1, source_target_pairs={{0,12},{1,13},{2,14},{3,15},{4,8},{5,9},{6,10},{7,11},{8,4},{9,5},... | collective-permute-start | bytes 393224 | tf_op jit(solution)/shard_map/ppermute | solution.py:599
  47.9 19.9 %collective-permute-start.11 = (bf16[8,16,512]{2,1,0:T(8,128)(2,1)S(1)}, bf16[8,16,512]{2,1,0:T(8,128)(2,1)S(1)}, u32[]{:S(2)}, u32[]{:S(2)}) collective-permute-start(bf16[8,16,512]{2,1,0:T(8,128)(2,1)S(1)} %get-tuple-element.53), channel_id=1, source_target_pairs={{0,10},{1,11},{2,8},{3,9},{4,14},{5,15},{6,12},{7,13},{8,2},{9,3},... | collective-permute-start | bytes 393224 | tf_op jit(solution)/shard_map/ppermute | solution.py:599
  49.5 18.2 %collective-permute-start.12 = (bf16[8,16,512]{2,1,0:T(8,128)(2,1)S(1)}, bf16[8,16,512]{2,1,0:T(8,128)(2,1)S(1)}, u32[]{:S(2)}, u32[]{:S(2)}) collective-permute-start(bf16[8,16,512]{2,1,0:T(8,128)(2,1)S(1)} %get-tuple-element.54), channel_id=1, source_target_pairs={{0,4},{1,5},{2,6},{3,7},{4,0},{5,1},{6,2},{7,3},{8,12},{9,13},{10,... | collective-permute-start | bytes 393224 | tf_op jit(solution)/shard_map/ppermute | solution.py:599
  59.6 8.1 %collective-permute-start.13 = (bf16[8,16,512]{2,1,0:T(8,128)(2,1)S(1)}, bf16[8,16,512]{2,1,0:T(8,128)(2,1)S(1)}, u32[]{:S(2)}, u32[]{:S(2)}) collective-permute-start(bf16[8,16,512]{2,1,0:T(8,128)(2,1)S(1)} %get-tuple-element.55), channel_id=1, source_target_pairs={{0,14},{1,15},{2,12},{3,13},{4,10},{5,11},{6,8},{7,9},{8,6},{9,7},... | collective-permute-start | bytes 393224 | tf_op jit(solution)/shard_map/ppermute | solution.py:599
  62.4 7.8 %collective-permute-start.14 = (bf16[8,16,512]{2,1,0:T(8,128)(2,1)S(1)}, bf16[8,16,512]{2,1,0:T(8,128)(2,1)S(1)}, u32[]{:S(2)}, u32[]{:S(2)}) collective-permute-start(bf16[8,16,512]{2,1,0:T(8,128)(2,1)S(1)} %get-tuple-element.56), channel_id=1, source_target_pairs={{0,6},{1,7},{2,4},{3,5},{4,2},{5,3},{6,0},{7,1},{8,14},{9,15},{10,... | collective-permute-start | bytes 393224 | tf_op jit(solution)/shard_map/ppermute | solution.py:599
  77.2 9.3 %collective-permute-start.15 = (bf16[8,16,512]{2,1,0:T(8,128)(2,1)S(1)}, bf16[8,16,512]{2,1,0:T(8,128)(2,1)S(1)}, u32[]{:S(2)}, u32[]{:S(2)}) collective-permute-start(bf16[8,16,512]{2,1,0:T(8,128)(2,1)S(1)} %get-tuple-element.58), channel_id=1, source_target_pairs={{0,2},{1,3},{2,0},{3,1},{4,6},{5,7},{6,4},{7,5},{8,10},{9,11},{10,... | collective-permute-start | bytes 393224 | tf_op jit(solution)/shard_map/ppermute | solution.py:599
  78.7 15.9 %collective-permute-start.16 = (bf16[8,16,512]{2,1,0:T(8,128)(2,1)S(1)}, bf16[8,16,512]{2,1,0:T(8,128)(2,1)S(1)}, u32[]{:S(2)}, u32[]{:S(2)}) collective-permute-start(bf16[8,16,512]{2,1,0:T(8,128)(2,1)S(1)} %get-tuple-element.59), channel_id=1, source_target_pairs={{0,8},{1,9},{2,10},{3,11},{4,12},{5,13},{6,14},{7,15},{8,0},{9,1},... | collective-permute-start | bytes 393224 | tf_op jit(solution)/shard_map/ppermute | solution.py:599
  81.4 14.2 %collective-permute-start.17 = (bf16[8,16,512]{2,1,0:T(8,128)(2,1)S(1)}, bf16[8,16,512]{2,1,0:T(8,128)(2,1)S(1)}, u32[]{:S(2)}, u32[]{:S(2)}) collective-permute-start(bf16[8,16,512]{2,1,0:T(8,128)(2,1)S(1)} %get-tuple-element.60), channel_id=1, source_target_pairs={{0,12},{1,13},{2,14},{3,15},{4,8},{5,9},{6,10},{7,11},{8,4},{9,5},... | collective-permute-start | bytes 393224 | tf_op jit(solution)/shard_map/ppermute | solution.py:599
  83.6 19.4 %collective-permute-start.18 = (bf16[8,16,512]{2,1,0:T(8,128)(2,1)S(1)}, bf16[8,16,512]{2,1,0:T(8,128)(2,1)S(1)}, u32[]{:S(2)}, u32[]{:S(2)}) collective-permute-start(bf16[8,16,512]{2,1,0:T(8,128)(2,1)S(1)} %get-tuple-element.61), channel_id=1, source_target_pairs={{0,10},{1,11},{2,8},{3,9},{4,14},{5,15},{6,12},{7,13},{8,2},{9,3},... | collective-permute-start | bytes 393224 | tf_op jit(solution)/shard_map/ppermute | solution.py:599
  84.2 18.8 %collective-permute-start.19 = (bf16[8,16,512]{2,1,0:T(8,128)(2,1)S(1)}, bf16[8,16,512]{2,1,0:T(8,128)(2,1)S(1)}, u32[]{:S(2)}, u32[]{:S(2)}) collective-permute-start(bf16[8,16,512]{2,1,0:T(8,128)(2,1)S(1)} %get-tuple-element.62), channel_id=1, source_target_pairs={{0,4},{1,5},{2,6},{3,7},{4,0},{5,1},{6,2},{7,3},{8,12},{9,13},{10,... | collective-permute-start | bytes 393224 | tf_op jit(solution)/shard_map/ppermute | solution.py:599
  86.5 16.5 %collective-permute-start.20 = (bf16[8,16,512]{2,1,0:T(8,128)(2,1)S(1)}, bf16[8,16,512]{2,1,0:T(8,128)(2,1)S(1)}, u32[]{:S(2)}, u32[]{:S(2)}) collective-permute-start(bf16[8,16,512]{2,1,0:T(8,128)(2,1)S(1)} %get-tuple-element.63), channel_id=1, source_target_pairs={{0,14},{1,15},{2,12},{3,13},{4,10},{5,11},{6,8},{7,9},{8,6},{9,7},... | collective-permute-start | bytes 393224 | tf_op jit(solution)/shard_map/ppermute | solution.py:599
  94.6 8.7 %collective-permute-start.21 = (bf16[8,16,512]{2,1,0:T(8,128)(2,1)S(1)}, bf16[8,16,512]{2,1,0:T(8,128)(2,1)S(1)}, u32[]{:S(2)}, u32[]{:S(2)}) collective-permute-start(bf16[8,16,512]{2,1,0:T(8,128)(2,1)S(1)} %get-tuple-element.64), channel_id=1, source_target_pairs={{0,6},{1,7},{2,4},{3,5},{4,2},{5,3},{6,0},{7,1},{8,14},{9,15},{10,... | collective-permute-start | bytes 393224 | tf_op jit(solution)/shard_map/ppermute | solution.py:599

commit v7 on v5

--- a/solution.py
+++ b/solution.py
@@ -12,7 +12,7 @@
 GRID = 8
 BATCH = 2
 STRIPS = 2
-MOVES = (0, 1, 4, 6, 5, 2, 7, 3)
+MOVES = (0, 1, 4, 2, 6, 5, 7, 3)
 ROOT = math.sqrt(2.0 / math.pi)
 LIN = 2.0 * ROOT
 CUBE = 8.0 * ROOT * 0.044715

time: 106 us -> 104 us (0.981)
    ppermute x14, waiting for transfers between devices: 29.7 us -> 28.6 us  [exchange(): parts[n] = lax.ppermute(parts[n], 'space', swap)]
  transfers between devices with their start and end apart: 22 -> 22, of which waited for: 9 -> 11; matrix products, arithmetic and copies ran while one was open for 0% -> 0% of each run, Pallas kernels for 20% -> 20%
where the time goes in v7:
time: 104 us
  waiting for transfers between devices  37.5 us (36%)
  starting transfers between devices  34.3 us (33%)
  Pallas kernels  32.1 us (31%)
    ppermute x14, waiting for transfers between devices, exchange(): parts[n] = lax.ppermute(parts[n], 'space', swap)  28.6 us
    ppermute x14, starting transfers between devices, exchange(): parts[n] = lax.ppermute(parts[n], 'space', swap)  24 us
    pallas_call x3, Pallas kernels, expand_some(): pl.pallas_call(functools.partial(expand_kernel, first, tile_of), grid_spe...  16.6 us
    pallas_call x1, Pallas kernels, attend(): pl.pallas_call(functools.partial(attend_kernel, 1 + len(rest), len(tokens...  7.02 us
    ppermute x3, waiting for transfers between devices, local(): over_dp = lambda w: lax.ppermute(w, 'dp', [(0, 1), (1, 0)])  6.11 us
    ppermute x3, starting transfers between devices, local(): over_dp = lambda w: lax.ppermute(w, 'dp', [(0, 1), (1, 0)])  4.85 us
    ppermute x1, starting transfers between devices, local(): lax.ppermute(top, 'space', [((i + 1) % space, i) for i in range(space)])  4.43 us
    pallas_call x1, Pallas kernels, project_rows(): pl.pallas_call(functools.partial(project_kernel, len(weights), split), gr...  3.06 us
  transfers between devices with their start and end apart: 22, of which 11 were waited for; matrix products, arithmetic and copies ran while one was open for 0% of the time, Pallas kernels for 20%

profile of v7, /device:TPU:0, one launch (start us, length us, event | category | flops | bytes accessed | tf_op | source)
XLA Modules:
  0.0 104.2 jit_solution(17739330810365979680)
XLA Ops:
  0.1 1.9 %share_weights.1 = (bf16[512,512]{1,0:T(8,128)(2,1)S(1)}, bf16[1024,256]{1,0:T(8,128)(2,1)S(1)}, bf16[256,1024]{1,0:T(8,128)(2,1)S(1)}) custom-call(s32[5]{0:T(128)S(1)} %stack.15.info, bf16[512,1024]{1,0:T(8,128)(2,1)} %refs_5_.1, bf16[2048,256]{1,0:T(8,128)(2,1)} %refs_3_.5, bf16[512,768]{1,0:T(8,128)(2,1)} %refs_0_.1, bf16[512,256]{1,0:T(8,128)(2,1)} %refs_1_.1), custom_call_target="tpu_custom_call" | custom-call | tf_op jit(solution)/shard_map/share_weights/pallas_call | solution.py:124
  2.0 3.0 %collective-permute-start.3 = (bf16[512,512]{1,0:T(8,128)(2,1)S(1)}, bf16[512,512]{1,0:T(8,128)(2,1)S(1)}, u32[]{:S(2)}, u32[]{:S(2)}) collective-permute-start(bf16[512,512]{1,0:T(8,128)(2,1)S(1)} %get-tuple-element.36), channel_id=1, source_target_pairs={{0,16},{16,0},{1,17},{17,1},{2,18},{18,2},{3,19},{19,3},{4,20},{20... | collective-permute-start | bytes 1572872 | tf_op jit(solution)/shard_map/ppermute | solution.py:548
  5.2 1.5 %edge_rows.1 = (bf16[1,128,512]{2,1,0:T(8,128)(2,1)S(1)}, bf16[1,128,512]{2,1,0:T(8,128)(2,1)S(1)}) custom-call(s32[5]{0:T(128)S(1)} %stack.15.info, bf16[8,128,512]{2,1,0:T(8,128)(2,1)} %bitcast.19), custom_call_target="tpu_custom_call" | custom-call | tf_op jit(solution)/shard_map/edge_rows/pallas_call | solution.py:91
  6.8 4.4 %collective-permute-start.2 = (bf16[1,128,512]{2,1,0:T(8,128)(2,1)S(1)}, bf16[1,128,512]{2,1,0:T(8,128)(2,1)S(1)}, u32[]{:S(2)}, u32[]{:S(2)}) collective-permute-start(bf16[1,128,512]{2,1,0:T(8,128)(2,1)S(1)} %get-tuple-element.40), channel_id=1, source_target_pairs={{1,0},{2,1},{3,2},{4,3},{5,4},{6,5},{7,6},{8,7},{9,8},{10,9},{11,1... | collective-permute-start | bytes 393224 | tf_op jit(solution)/shard_map/ppermute | solution.py:557
  11.2 2.8 %collective-permute-done.1.refs_1_ = bf16[1,128,512]{2,1,0:T(8,128)(2,1)S(1)} collective-permute-done((bf16[1,128,512]{2,1,0:T(8,128)(2,1)S(1)}, bf16[1,128,512]{2,1,0:T(8,128)(2,1)S(1)}, u32[]{:S(2)}, u32[]{:S(2)}) %collective-permute-start.1) | collective-permute-done | bytes 131104 | tf_op jit(solution)/shard_map/ppermute | solution.py:556
  13.9 9.0 %expand_conv.3 = (bf16[1024,1024]{1,0:T(8,128)(2,1)S(1)}, bf16[8,128,512]{2,1,0:T(8,128)(2,1)S(1)}, bf16[10,128,512]{2,1,0:T(8,128)(2,1)S(1)}) custom-call(s32[5]{0:T(128)S(1)} %stack.15.info, bf16[8,128,512]{2,1,0:T(8,128)(2,1)} %bitcast.20, bf16[1,128,512]{2,1,0:T(8,128)(2,1)S(1)} %collective-permute-done.1.refs_1_, ...), custom_call_target="tpu_custom_call" | custom-call | flops 1 | bytes 1 | tf_op jit(solution)/shard_map/expand_conv/pallas_call | solution.py:261
  22.9 1.0 collective-permute-start.4
  23.9 4.3 %collective-permute-done.5.refs_4_ = bf16[1024,256]{1,0:T(8,128)(2,1)S(1)} collective-permute-done((bf16[1024,256]{1,0:T(8,128)(2,1)S(1)}, bf16[1024,256]{1,0:T(8,128)(2,1)S(1)}, u32[]{:S(2)}, u32[]{:S(2)}) %collective-permute-start.5) | collective-permute-done | bytes 524320 | tf_op jit(solution)/shard_map/ppermute | solution.py:548
  28.2 1.7 %collective-permute-start = (bf16[256,1024]{1,0:T(8,128)(2,1)S(1)}, bf16[256,1024]{1,0:T(8,128)(2,1)S(1)}, u32[]{:S(2)}, u32[]{:S(2)}) collective-permute-start(bf16[256,1024]{1,0:T(8,128)(2,1)S(1)} %get-tuple-element.35), channel_id=1, source_target_pairs={{0,16},{16,0},{1,17},{17,1},{2,18},{18,2},{3,19},{19,3},{4,20},{20... | collective-permute-start | bytes 1572872 | tf_op jit(solution)/shard_map/ppermute | solution.py:548
  30.0 3.7 %expand_conv.4.refs_1_ = bf16[1024,512]{1,0:T(8,128)(2,1)S(1)} custom-call(s32[5]{0:T(128)S(1)} %stack.15.info, bf16[10,128,512]{2,1,0:T(8,128)(2,1)S(1)} %get-tuple-element.45.refs_0_, bf16[512,512]{1,0:T(8,128)(2,1)S(1)} %collective-permute-done.3.refs_1_, f32[1,2048]{1,0:T(1,128)S(1)} %bitcast.12, f32[3,3,2048]{2,1,0:T(4,128)S(1)} %copy-done.3, ...), custom_call_target="tpu_custom_call" | custom-call | flops 1 | bytes 1 | tf_op jit(solution)/shard_map/expand_conv/pallas_call | solution.py:261
  33.7 3.9 %expand_conv.5.refs_2_ = bf16[1024,512]{1,0:T(8,128)(2,1)S(1)} custom-call(s32[5]{0:T(128)S(1)} %stack.15.info, bf16[10,128,512]{2,1,0:T(8,128)(2,1)S(1)} %get-tuple-element.45.refs_0_, bf16[512,512]{1,0:T(8,128)(2,1)S(1)} %collective-permute-done.4.refs_1_, f32[1,2048]{1,0:T(1,128)S(1)} %bitcast.13, f32[3,3,2048]{2,1,0:T(4,128)S(1)} %copy-done.3, ...), custom_call_target="tpu_custom_call" | custom-call | flops 1 | bytes 1 | tf_op jit(solution)/shard_map/expand_conv/pallas_call | solution.py:261
  37.7 3.1 %project_rows.1 = (bf16[8,16,512]{2,1,0:T(8,128)(2,1)S(1)}, bf16[8,16,512]{2,1,0:T(8,128)(2,1)S(1)}, bf16[8,16,512]{2,1,0:T(8,128)(2,1)S(1)}, bf16[8,16,512]{2,1...) custom-call(s32[5]{0:T(128)S(1)} %stack.15.info, ...), custom_call_target="tpu_custom_call" | custom-call | flops 1 | bytes 1 | tf_op jit(solution)/shard_map/project_rows/pallas_call | solution.py:349
  40.8 1.8 %collective-permute-done.refs_2_ = bf16[256,1024]{1,0:T(8,128)(2,1)S(1)} collective-permute-done((bf16[256,1024]{1,0:T(8,128)(2,1)S(1)}, bf16[256,1024]{1,0:T(8,128)(2,1)S(1)}, u32[]{:S(2)}, u32[]{:S(2)}) %collective-permute-start) | collective-permute-done | bytes 524320 | tf_op jit(solution)/shard_map/ppermute | solution.py:548
  42.6 1.7 %collective-permute-start.8 = (bf16[8,16,512]{2,1,0:T(8,128)(2,1)S(1)}, bf16[8,16,512]{2,1,0:T(8,128)(2,1)S(1)}, u32[]{:S(2)}, u32[]{:S(2)}) collective-permute-start(bf16[8,16,512]{2,1,0:T(8,128)(2,1)S(1)} %get-tuple-element.50), channel_id=1, source_target_pairs={{0,2},{1,3},{2,0},{3,1},{4,6},{5,7},{6,4},{7,5},{8,10},{9,11},{10,... | collective-permute-start | bytes 393224 | tf_op jit(solution)/shard_map/ppermute | solution.py:590
  44.3 2.6 %collective-permute-start.9 = (bf16[8,16,512]{2,1,0:T(8,128)(2,1)S(1)}, bf16[8,16,512]{2,1,0:T(8,128)(2,1)S(1)}, u32[]{:S(2)}, u32[]{:S(2)}) collective-permute-start(bf16[8,16,512]{2,1,0:T(8,128)(2,1)S(1)} %get-tuple-element.51), channel_id=1, source_target_pairs={{0,8},{1,9},{2,10},{3,11},{4,12},{5,13},{6,14},{7,15},{8,0},{9,1},... | collective-permute-start | bytes 393224 | tf_op jit(solution)/shard_map/ppermute | solution.py:590
  46.9 1.6 %collective-permute-start.10 = (bf16[8,16,512]{2,1,0:T(8,128)(2,1)S(1)}, bf16[8,16,512]{2,1,0:T(8,128)(2,1)S(1)}, u32[]{:S(2)}, u32[]{:S(2)}) collective-permute-start(bf16[8,16,512]{2,1,0:T(8,128)(2,1)S(1)} %get-tuple-element.52), channel_id=1, source_target_pairs={{0,4},{1,5},{2,6},{3,7},{4,0},{5,1},{6,2},{7,3},{8,12},{9,13},{10,... | collective-permute-start | bytes 393224 | tf_op jit(solution)/shard_map/ppermute | solution.py:590
  48.7 3.5 %collective-permute-start.12 = (bf16[8,16,512]{2,1,0:T(8,128)(2,1)S(1)}, bf16[8,16,512]{2,1,0:T(8,128)(2,1)S(1)}, u32[]{:S(2)}, u32[]{:S(2)}) collective-permute-start(bf16[8,16,512]{2,1,0:T(8,128)(2,1)S(1)} %get-tuple-element.54), channel_id=1, source_target_pairs={{0,10},{1,11},{2,8},{3,9},{4,14},{5,15},{6,12},{7,13},{8,2},{9,3},... | collective-permute-start | bytes 393224 | tf_op jit(solution)/shard_map/ppermute | solution.py:590
  52.2 2.5 %collective-permute-done.9.refs_6_ = bf16[8,16,512]{2,1,0:T(8,128)(2,1)S(1)} collective-permute-done((bf16[8,16,512]{2,1,0:T(8,128)(2,1)S(1)}, bf16[8,16,512]{2,1,0:T(8,128)(2,1)S(1)}, u32[]{:S(2)}, u32[]{:S(2)}) %collective-permute-start.9) | collective-permute-done | bytes 131104 | tf_op jit(solution)/shard_map/ppermute | solution.py:590
  54.7 3.2 %collective-permute-start.13 = (bf16[8,16,512]{2,1,0:T(8,128)(2,1)S(1)}, bf16[8,16,512]{2,1,0:T(8,128)(2,1)S(1)}, u32[]{:S(2)}, u32[]{:S(2)}) collective-permute-start(bf16[8,16,512]{2,1,0:T(8,128)(2,1)S(1)} %get-tuple-element.55), channel_id=1, source_target_pairs={{0,14},{1,15},{2,12},{3,13},{4,10},{5,11},{6,8},{7,9},{8,6},{9,7},... | collective-permute-start | bytes 393224 | tf_op jit(solution)/shard_map/ppermute | solution.py:590
  58.3 9.8 %collective-permute-done.12.refs_9_ = bf16[8,16,512]{2,1,0:T(8,128)(2,1)S(1)} collective-permute-done((bf16[8,16,512]{2,1,0:T(8,128)(2,1)S(1)}, bf16[8,16,512]{2,1,0:T(8,128)(2,1)S(1)}, u32[]{:S(2)}, u32[]{:S(2)}) %collective-permute-start.12) | collective-permute-done | bytes 131104 | tf_op jit(solution)/shard_map/ppermute | solution.py:590
  68.1 0.6 collective-permute-done.14.refs_11_
  68.8 7.0 %attend.1 = (bf16[8,16,512]{2,1,0:T(8,128)(2,1)S(1)}, bf16[8,16,512]{2,1,0:T(8,128)(2,1)S(1)}, bf16[8,16,512]{2,1,0:T(8,128)(2,1)S(1)}, bf16[8,16,512]{2,1,0:T(8...) custom-call(s32[5]{0:T(128)S(1)} %stack.15.info, ...), custom_call_target="tpu_custom_call" | custom-call | flops 1 | bytes 1 | tf_op jit(solution)/shard_map/attend/pallas_call | solution.py:452
  75.8 1.6 %collective-permute-start.15 = (bf16[8,16,512]{2,1,0:T(8,128)(2,1)S(1)}, bf16[8,16,512]{2,1,0:T(8,128)(2,1)S(1)}, u32[]{:S(2)}, u32[]{:S(2)}) collective-permute-start(bf16[8,16,512]{2,1,0:T(8,128)(2,1)S(1)} %get-tuple-element.58), channel_id=1, source_target_pairs={{0,2},{1,3},{2,0},{3,1},{4,6},{5,7},{6,4},{7,5},{8,10},{9,11},{10,... | collective-permute-start | bytes 393224 | tf_op jit(solution)/shard_map/ppermute | solution.py:590
  77.3 4.3 %collective-permute-start.16 = (bf16[8,16,512]{2,1,0:T(8,128)(2,1)S(1)}, bf16[8,16,512]{2,1,0:T(8,128)(2,1)S(1)}, u32[]{:S(2)}, u32[]{:S(2)}) collective-permute-start(bf16[8,16,512]{2,1,0:T(8,128)(2,1)S(1)} %get-tuple-element.59), channel_id=1, source_target_pairs={{0,8},{1,9},{2,10},{3,11},{4,12},{5,13},{6,14},{7,15},{8,0},{9,1},... | collective-permute-start | bytes 393224 | tf_op jit(solution)/shard_map/ppermute | solution.py:590
  81.7 1.5 %collective-permute-start.18 = (bf16[8,16,512]{2,1,0:T(8,128)(2,1)S(1)}, bf16[8,16,512]{2,1,0:T(8,128)(2,1)S(1)}, u32[]{:S(2)}, u32[]{:S(2)}) collective-permute-start(bf16[8,16,512]{2,1,0:T(8,128)(2,1)S(1)} %get-tuple-element.61), channel_id=1, source_target_pairs={{0,12},{1,13},{2,14},{3,15},{4,8},{5,9},{6,10},{7,11},{8,4},{9,5},... | collective-permute-start | bytes 393224 | tf_op jit(solution)/shard_map/ppermute | solution.py:590
  83.1 2.0 %collective-permute-start.19 = (bf16[8,16,512]{2,1,0:T(8,128)(2,1)S(1)}, bf16[8,16,512]{2,1,0:T(8,128)(2,1)S(1)}, u32[]{:S(2)}, u32[]{:S(2)}) collective-permute-start(bf16[8,16,512]{2,1,0:T(8,128)(2,1)S(1)} %get-tuple-element.62), channel_id=1, source_target_pairs={{0,10},{1,11},{2,8},{3,9},{4,14},{5,15},{6,12},{7,13},{8,2},{9,3},... | collective-permute-start | bytes 393224 | tf_op jit(solution)/shard_map/ppermute | solution.py:590
  85.1 1.8 %collective-permute-start.20 = (bf16[8,16,512]{2,1,0:T(8,128)(2,1)S(1)}, bf16[8,16,512]{2,1,0:T(8,128)(2,1)S(1)}, u32[]{:S(2)}, u32[]{:S(2)}) collective-permute-start(bf16[8,16,512]{2,1,0:T(8,128)(2,1)S(1)} %get-tuple-element.63), channel_id=1, source_target_pairs={{0,14},{1,15},{2,12},{3,13},{4,10},{5,11},{6,8},{7,9},{8,6},{9,7},... | collective-permute-start | bytes 393224 | tf_op jit(solution)/shard_map/ppermute | solution.py:590
  87.0 1.7 %collective-permute-done.16.refs_2_ = bf16[8,16,512]{2,1,0:T(8,128)(2,1)S(1)} collective-permute-done((bf16[8,16,512]{2,1,0:T(8,128)(2,1)S(1)}, bf16[8,16,512]{2,1,0:T(8,128)(2,1)S(1)}, u32[]{:S(2)}, u32[]{:S(2)}) %collective-permute-start.16) | collective-permute-done | bytes 131104 | tf_op jit(solution)/shard_map/ppermute | solution.py:590
  88.7 2.7 %collective-permute-done.17.refs_3_ = bf16[8,16,512]{2,1,0:T(8,128)(2,1)S(1)} collective-permute-done((bf16[8,16,512]{2,1,0:T(8,128)(2,1)S(1)}, bf16[8,16,512]{2,1,0:T(8,128)(2,1)S(1)}, u32[]{:S(2)}, u32[]{:S(2)}) %collective-permute-start.17) | collective-permute-done | bytes 131104 | tf_op jit(solution)/shard_map/ppermute | solution.py:590
  91.4 0.6 collective-permute-done.18.refs_4_
  92.0 10.2 %collective-permute-done.19.refs_5_ = bf16[8,16,512]{2,1,0:T(8,128)(2,1)S(1)} collective-permute-done((bf16[8,16,512]{2,1,0:T(8,128)(2,1)S(1)}, bf16[8,16,512]{2,1,0:T(8,128)(2,1)S(1)}, u32[]{:S(2)}, u32[]{:S(2)}) %collective-permute-start.19) | collective-permute-done | bytes 131104 | tf_op jit(solution)/shard_map/ppermute | solution.py:590
  102.3 2.0 %restore_rows.1 = bf16[8,128,512]{2,1,0:T(8,128)(2,1)} custom-call(s32[5]{0:T(128)S(1)} %stack.15.info, bf16[8,16,512]{2,1,0:T(8,128)(2,1)S(1)} %get-tuple-element.57.refs_0_, bf16[8,16,512]{2,1,0:T(8,128)(2,1)S(1)} %collective-permute-done.15.refs_1_, bf16[8,16,512]{2,1,0:T(8,128)(2,1)S(1)} %collective-permute-done.16.refs_2_, ...), custom_call_target="tpu_custom_call" | custom-call | flops 1 | bytes 1 | tf_op jit(solution)/shard_map/restore_rows/pallas_call | solution.py:497
  (37 shorter events, 1.0 us)
Async XLA Ops:
  2.0 28.0 %copy-start.3 = (f32[3,3,2048]{2,1,0:T(4,128)S(1)}, f32[3,3,2048]{2,1,0:T(4,128)}, u32[]{:S(2)}) copy-start(f32[3,3,2048]{2,1,0:T(4,128)} %refs_3_.4) | copy-start | bytes 221188
  2.0 28.0 %copy-start.4 = (f32[2048]{0:T(1024)S(1)}, f32[2048]{0:T(1024)}, u32[]{:S(2)}) copy-start(f32[2048]{0:T(1024)} %param.16) | copy-start | bytes 24580
  2.0 28.0 %copy-start.5 = (f32[2048]{0:T(1024)S(1)}, f32[2048]{0:T(1024)}, u32[]{:S(2)}) copy-start(f32[2048]{0:T(1024)} %param.18) | copy-start | bytes 24580
  2.0 20.9 %collective-permute-start.3 = (bf16[512,512]{1,0:T(8,128)(2,1)S(1)}, bf16[512,512]{1,0:T(8,128)(2,1)S(1)}, u32[]{:S(2)}, u32[]{:S(2)}) collective-permute-start(bf16[512,512]{1,0:T(8,128)(2,1)S(1)} %get-tuple-element.36), channel_id=1, source_target_pairs={{0,16},{16,0},{1,17},{17,1},{2,18},{18,2},{3,19},{19,3},{4,20},{20... | collective-permute-start | bytes 1572872 | tf_op jit(solution)/shard_map/ppermute | solution.py:548
  5.1 23.2 %collective-permute-start.5 = (bf16[1024,256]{1,0:T(8,128)(2,1)S(1)}, bf16[1024,256]{1,0:T(8,128)(2,1)S(1)}, u32[]{:S(2)}, u32[]{:S(2)}) collective-permute-start(bf16[1024,256]{1,0:T(8,128)(2,1)S(1)} %get-tuple-element.37), channel_id=1, source_target_pairs={{0,16},{16,0},{1,17},{17,1},{2,18},{18,2},{3,19},{19,3},{4,20},{20... | collective-permute-start | bytes 1572872 | tf_op jit(solution)/shard_map/ppermute | solution.py:548
  6.7 7.2 %collective-permute-start.1 = (bf16[1,128,512]{2,1,0:T(8,128)(2,1)S(1)}, bf16[1,128,512]{2,1,0:T(8,128)(2,1)S(1)}, u32[]{:S(2)}, u32[]{:S(2)}) collective-permute-start(bf16[1,128,512]{2,1,0:T(8,128)(2,1)S(1)} %get-tuple-element.39), channel_id=1, source_target_pairs={{0,1},{1,2},{2,3},{3,4},{4,5},{5,6},{6,7},{7,8},{8,9},{9,10},{10,1... | collective-permute-start | bytes 393224 | tf_op jit(solution)/shard_map/ppermute | solution.py:556
  6.8 7.2 %collective-permute-start.2 = (bf16[1,128,512]{2,1,0:T(8,128)(2,1)S(1)}, bf16[1,128,512]{2,1,0:T(8,128)(2,1)S(1)}, u32[]{:S(2)}, u32[]{:S(2)}) collective-permute-start(bf16[1,128,512]{2,1,0:T(8,128)(2,1)S(1)} %get-tuple-element.40), channel_id=1, source_target_pairs={{1,0},{2,1},{3,2},{4,3},{5,4},{6,5},{7,6},{8,7},{9,8},{10,9},{11,1... | collective-permute-start | bytes 393224 | tf_op jit(solution)/shard_map/ppermute | solution.py:557
  22.9 10.8 %collective-permute-start.4 = (bf16[512,512]{1,0:T(8,128)(2,1)S(1)}, bf16[512,512]{1,0:T(8,128)(2,1)S(1)}, u32[]{:S(2)}, u32[]{:S(2)}) collective-permute-start(bf16[512,512]{1,0:T(8,128)(2,1)S(1)} %collective-permute-done.3.refs_1_), channel_id=1, source_target_pairs={{0,1},{1,0},{2,3},{3,2},{4,5},{5,4},{6,7},{7,6},{8,9},{9,8},{10,11... | collective-permute-start | bytes 1572872 | tf_op jit(solution)/shard_map/ppermute | solution.py:549
  28.2 9.4 %collective-permute-start.6 = (bf16[1024,256]{1,0:T(8,128)(2,1)S(1)}, bf16[1024,256]{1,0:T(8,128)(2,1)S(1)}, u32[]{:S(2)}, u32[]{:S(2)}) collective-permute-start(bf16[1024,256]{1,0:T(8,128)(2,1)S(1)} %collective-permute-done.5.refs_4_), channel_id=1, source_target_pairs={{0,1},{1,0},{2,3},{3,2},{4,5},{5,4},{6,7},{7,6},{8,9},{9,8},{10,11... | collective-permute-start | bytes 1572872 | tf_op jit(solution)/shard_map/ppermute | solution.py:549
  28.2 14.3 %collective-permute-start = (bf16[256,1024]{1,0:T(8,128)(2,1)S(1)}, bf16[256,1024]{1,0:T(8,128)(2,1)S(1)}, u32[]{:S(2)}, u32[]{:S(2)}) collective-permute-start(bf16[256,1024]{1,0:T(8,128)(2,1)S(1)} %get-tuple-element.35), channel_id=1, source_target_pairs={{0,16},{16,0},{1,17},{17,1},{2,18},{18,2},{3,19},{19,3},{4,20},{20... | collective-permute-start | bytes 1572872 | tf_op jit(solution)/shard_map/ppermute | solution.py:548
  33.7 3.9 %copy-start = (bf16[2048,256]{1,0:T(8,128)(2,1)S(1)}, bf16[2048,256]{1,0:T(8,128)(2,1)}, u32[]{:S(2)}) copy-start(bf16[2048,256]{1,0:T(8,128)(2,1)} %refs_3_.5) | copy-start | bytes 3145732
  37.7 31.1 %copy-start.1 = (bf16[512,768]{1,0:T(8,128)(2,1)S(1)}, bf16[512,768]{1,0:T(8,128)(2,1)}, u32[]{:S(2)}) copy-start(bf16[512,768]{1,0:T(8,128)(2,1)} %refs_0_.1) | copy-start | bytes 2359300
  37.7 31.1 %copy-start.2 = (bf16[512,256]{1,0:T(8,128)(2,1)S(1)}, bf16[512,256]{1,0:T(8,128)(2,1)}, u32[]{:S(2)}) copy-start(bf16[512,256]{1,0:T(8,128)(2,1)} %refs_1_.1) | copy-start | bytes 786436
  37.7 31.1 %copy-start.6 = (f32[512]{0:T(512)S(1)}, f32[512]{0:T(512)}, u32[]{:S(2)}) copy-start(f32[512]{0:T(512)} %param.20) | copy-start | bytes 6148
  37.7 31.1 %copy-start.7 = (f32[512]{0:T(512)S(1)}, f32[512]{0:T(512)}, u32[]{:S(2)}) copy-start(f32[512]{0:T(512)} %param.21) | copy-start | bytes 6148
  42.6 26.2 %collective-permute-start.7 = (bf16[256,1024]{1,0:T(8,128)(2,1)S(1)}, bf16[256,1024]{1,0:T(8,128)(2,1)S(1)}, u32[]{:S(2)}, u32[]{:S(2)}) collective-permute-start(bf16[256,1024]{1,0:T(8,128)(2,1)S(1)} %collective-permute-done.refs_2_), channel_id=1, source_target_pairs={{0,1},{1,0},{2,3},{3,2},{4,5},{5,4},{6,7},{7,6},{8,9},{9,8},{10,11... | collective-permute-start | bytes 1572872 | tf_op jit(solution)/shard_map/ppermute | solution.py:549
  42.6 6.1 %collective-permute-start.8 = (bf16[8,16,512]{2,1,0:T(8,128)(2,1)S(1)}, bf16[8,16,512]{2,1,0:T(8,128)(2,1)S(1)}, u32[]{:S(2)}, u32[]{:S(2)}) collective-permute-start(bf16[8,16,512]{2,1,0:T(8,128)(2,1)S(1)} %get-tuple-element.50), channel_id=1, source_target_pairs={{0,2},{1,3},{2,0},{3,1},{4,6},{5,7},{6,4},{7,5},{8,10},{9,11},{10,... | collective-permute-start | bytes 393224 | tf_op jit(solution)/shard_map/ppermute | solution.py:590
  44.3 10.4 %collective-permute-start.9 = (bf16[8,16,512]{2,1,0:T(8,128)(2,1)S(1)}, bf16[8,16,512]{2,1,0:T(8,128)(2,1)S(1)}, u32[]{:S(2)}, u32[]{:S(2)}) collective-permute-start(bf16[8,16,512]{2,1,0:T(8,128)(2,1)S(1)} %get-tuple-element.51), channel_id=1, source_target_pairs={{0,8},{1,9},{2,10},{3,11},{4,12},{5,13},{6,14},{7,15},{8,0},{9,1},... | collective-permute-start | bytes 393224 | tf_op jit(solution)/shard_map/ppermute | solution.py:590
  46.9 11.0 %collective-permute-start.10 = (bf16[8,16,512]{2,1,0:T(8,128)(2,1)S(1)}, bf16[8,16,512]{2,1,0:T(8,128)(2,1)S(1)}, u32[]{:S(2)}, u32[]{:S(2)}) collective-permute-start(bf16[8,16,512]{2,1,0:T(8,128)(2,1)S(1)} %get-tuple-element.52), channel_id=1, source_target_pairs={{0,4},{1,5},{2,6},{3,7},{4,0},{5,1},{6,2},{7,3},{8,12},{9,13},{10,... | collective-permute-start | bytes 393224 | tf_op jit(solution)/shard_map/ppermute | solution.py:590
  48.5 9.8 %collective-permute-start.11 = (bf16[8,16,512]{2,1,0:T(8,128)(2,1)S(1)}, bf16[8,16,512]{2,1,0:T(8,128)(2,1)S(1)}, u32[]{:S(2)}, u32[]{:S(2)}) collective-permute-start(bf16[8,16,512]{2,1,0:T(8,128)(2,1)S(1)} %get-tuple-element.53), channel_id=1, source_target_pairs={{0,12},{1,13},{2,14},{3,15},{4,8},{5,9},{6,10},{7,11},{8,4},{9,5},... | collective-permute-start | bytes 393224 | tf_op jit(solution)/shard_map/ppermute | solution.py:590
  48.7 19.4 %collective-permute-start.12 = (bf16[8,16,512]{2,1,0:T(8,128)(2,1)S(1)}, bf16[8,16,512]{2,1,0:T(8,128)(2,1)S(1)}, u32[]{:S(2)}, u32[]{:S(2)}) collective-permute-start(bf16[8,16,512]{2,1,0:T(8,128)(2,1)S(1)} %get-tuple-element.54), channel_id=1, source_target_pairs={{0,10},{1,11},{2,8},{3,9},{4,14},{5,15},{6,12},{7,13},{8,2},{9,3},... | collective-permute-start | bytes 393224 | tf_op jit(solution)/shard_map/ppermute | solution.py:590
  54.7 13.4 %collective-permute-start.13 = (bf16[8,16,512]{2,1,0:T(8,128)(2,1)S(1)}, bf16[8,16,512]{2,1,0:T(8,128)(2,1)S(1)}, u32[]{:S(2)}, u32[]{:S(2)}) collective-permute-start(bf16[8,16,512]{2,1,0:T(8,128)(2,1)S(1)} %get-tuple-element.55), channel_id=1, source_target_pairs={{0,14},{1,15},{2,12},{3,13},{4,10},{5,11},{6,8},{7,9},{8,6},{9,7},... | collective-permute-start | bytes 393224 | tf_op jit(solution)/shard_map/ppermute | solution.py:590
  57.9 10.9 %collective-permute-start.14 = (bf16[8,16,512]{2,1,0:T(8,128)(2,1)S(1)}, bf16[8,16,512]{2,1,0:T(8,128)(2,1)S(1)}, u32[]{:S(2)}, u32[]{:S(2)}) collective-permute-start(bf16[8,16,512]{2,1,0:T(8,128)(2,1)S(1)} %get-tuple-element.56), channel_id=1, source_target_pairs={{0,6},{1,7},{2,4},{3,5},{4,2},{5,3},{6,0},{7,1},{8,14},{9,15},{10,... | collective-permute-start | bytes 393224 | tf_op jit(solution)/shard_map/ppermute | solution.py:590
  75.8 9.3 %collective-permute-start.15 = (bf16[8,16,512]{2,1,0:T(8,128)(2,1)S(1)}, bf16[8,16,512]{2,1,0:T(8,128)(2,1)S(1)}, u32[]{:S(2)}, u32[]{:S(2)}) collective-permute-start(bf16[8,16,512]{2,1,0:T(8,128)(2,1)S(1)} %get-tuple-element.58), channel_id=1, source_target_pairs={{0,2},{1,3},{2,0},{3,1},{4,6},{5,7},{6,4},{7,5},{8,10},{9,11},{10,... | collective-permute-start | bytes 393224 | tf_op jit(solution)/shard_map/ppermute | solution.py:590
  77.3 11.4 %collective-permute-start.16 = (bf16[8,16,512]{2,1,0:T(8,128)(2,1)S(1)}, bf16[8,16,512]{2,1,0:T(8,128)(2,1)S(1)}, u32[]{:S(2)}, u32[]{:S(2)}) collective-permute-start(bf16[8,16,512]{2,1,0:T(8,128)(2,1)S(1)} %get-tuple-element.59), channel_id=1, source_target_pairs={{0,8},{1,9},{2,10},{3,11},{4,12},{5,13},{6,14},{7,15},{8,0},{9,1},... | collective-permute-start | bytes 393224 | tf_op jit(solution)/shard_map/ppermute | solution.py:590
  81.7 9.7 %collective-permute-start.17 = (bf16[8,16,512]{2,1,0:T(8,128)(2,1)S(1)}, bf16[8,16,512]{2,1,0:T(8,128)(2,1)S(1)}, u32[]{:S(2)}, u32[]{:S(2)}) collective-permute-start(bf16[8,16,512]{2,1,0:T(8,128)(2,1)S(1)} %get-tuple-element.60), channel_id=1, source_target_pairs={{0,4},{1,5},{2,6},{3,7},{4,0},{5,1},{6,2},{7,3},{8,12},{9,13},{10,... | collective-permute-start | bytes 393224 | tf_op jit(solution)/shard_map/ppermute | solution.py:590
  81.7 10.3 %collective-permute-start.18 = (bf16[8,16,512]{2,1,0:T(8,128)(2,1)S(1)}, bf16[8,16,512]{2,1,0:T(8,128)(2,1)S(1)}, u32[]{:S(2)}, u32[]{:S(2)}) collective-permute-start(bf16[8,16,512]{2,1,0:T(8,128)(2,1)S(1)} %get-tuple-element.61), channel_id=1, source_target_pairs={{0,12},{1,13},{2,14},{3,15},{4,8},{5,9},{6,10},{7,11},{8,4},{9,5},... | collective-permute-start | bytes 393224 | tf_op jit(solution)/shard_map/ppermute | solution.py:590
  83.1 19.1 %collective-permute-start.19 = (bf16[8,16,512]{2,1,0:T(8,128)(2,1)S(1)}, bf16[8,16,512]{2,1,0:T(8,128)(2,1)S(1)}, u32[]{:S(2)}, u32[]{:S(2)}) collective-permute-start(bf16[8,16,512]{2,1,0:T(8,128)(2,1)S(1)} %get-tuple-element.62), channel_id=1, source_target_pairs={{0,10},{1,11},{2,8},{3,9},{4,14},{5,15},{6,12},{7,13},{8,2},{9,3},... | collective-permute-start | bytes 393224 | tf_op jit(solution)/shard_map/ppermute | solution.py:590
  85.1 17.1 %collective-permute-start.20 = (bf16[8,16,512]{2,1,0:T(8,128)(2,1)S(1)}, bf16[8,16,512]{2,1,0:T(8,128)(2,1)S(1)}, u32[]{:S(2)}, u32[]{:S(2)}) collective-permute-start(bf16[8,16,512]{2,1,0:T(8,128)(2,1)S(1)} %get-tuple-element.63), channel_id=1, source_target_pairs={{0,14},{1,15},{2,12},{3,13},{4,10},{5,11},{6,8},{7,9},{8,6},{9,7},... | collective-permute-start | bytes 393224 | tf_op jit(solution)/shard_map/ppermute | solution.py:590
  88.7 13.6 %collective-permute-start.21 = (bf16[8,16,512]{2,1,0:T(8,128)(2,1)S(1)}, bf16[8,16,512]{2,1,0:T(8,128)(2,1)S(1)}, u32[]{:S(2)}, u32[]{:S(2)}) collective-permute-start(bf16[8,16,512]{2,1,0:T(8,128)(2,1)S(1)} %get-tuple-element.64), channel_id=1, source_target_pairs={{0,6},{1,7},{2,4},{3,5},{4,2},{5,3},{6,0},{7,1},{8,14},{9,15},{10,... | collective-permute-start | bytes 393224 | tf_op jit(solution)/shard_map/ppermute | solution.py:590
